TPU v7x, 512 devices: a whole 4x4x16 slice. The times are simulated.
512 devices in a mesh: dp: 8 (over x_hi, y), ctx: 64 (over x_lo, z, core).
Axes of the slice: x: 4 (x_hi: 2, x_lo: 2; x = x_hi * 2 + x_lo), y: 4, z: 16, core: 2. Of those that a mesh axis runs over, the one named last changes fastest.
Arguments:
- queries: bfloat16 [8, 8192, 2048], P('dp', 'ctx'), may hold values from -6 to 6
- key_vectors: bfloat16 [8, 8192, 256], P('dp', 'ctx'), may hold values from -6 to 6
- value_vectors: bfloat16 [8, 8192, 256], P('dp', 'ctx'), may hold values from -6 to 6
- out_grad: bfloat16 [8, 8192, 2048], P('dp', 'ctx'), may hold values from -6 to 6
- sink_logits: float32 [32], replicated, may hold values from 2 to 7
- lengths: int32 [8, 16], replicated, may hold values from 1 to 512, 5120 in all within a row
- route_plan: int32 [16], replicated, may hold values from 0 to 7
Outputs:
- attn_out: bfloat16 [8, 8192, 2048], P('dp', 'ctx')
- query_grad: bfloat16 [8, 8192, 2048], P('dp', 'ctx')
- key_grad: bfloat16 [8, 8192, 256], P('dp', 'ctx')
- value_grad: bfloat16 [8, 8192, 256], P('dp', 'ctx')
- sink_grad: float32 [32], replicated
Inputs may be any that keep to these rules, and one draw needn't show every extreme that they name: The 16 lengths of each generating group sum to 5120, and the largest is 512.
All inputs are finite; a program needn't handle non-finite values.
Results may differ from a plain program's by a relative error of at most 0.035.
Values may be sent and summed in bfloat16 or wider, within the bound.
No kernel may reach another device: no remote copies, remote signals or barrier semaphores. Data moves between devices by JAX's collectives and lax.ppermute only.
A program may use at most 64 MiB of HBM per device.

v0:
```python
import jax
import jax.numpy as jnp
from jax import lax
from jax.sharding import PartitionSpec as P

D_HEAD = 64
KV_HEADS = 4
HEAD_GROUP = 8
SPAN = 4


masked_score = -1e30


def for_sending(shard):
    return jax.tree.map(lambda a: a.astype(jnp.bfloat16) if a.dtype == jnp.float32 else a, shard)


def partner_2(value, axis, bit):
    mask = 2**bit
    pairs = [(source, source ^ mask) for source in range(lax.axis_size(axis))]
    return lax.ppermute(value, axis, pairs)


def from_behind(shard, axis, by):
    length = lax.axis_size(axis)
    pairs = [(i, i + by) for i in range(length) if 0 <= i + by < length]
    return lax.ppermute(shard, axis, pairs)


def pick_entry(lookup, wanted):
    places = jnp.arange(lookup.shape[0], dtype=jnp.int32)
    return jnp.sum(jnp.where(places == wanted, lookup, 0))


def group_pass(kv_head, queries, out_grad, key_window, value_window, sink_logits, allowed):
    score_scale = D_HEAD ** (-0.5)
    head_width = HEAD_GROUP * D_HEAD
    tok_rows = queries.shape[0]
    query_rows = queries[:, kv_head * head_width : (kv_head + 1) * head_width].reshape(
        tok_rows, HEAD_GROUP, D_HEAD
    )
    grad_rows = out_grad[:, kv_head * head_width : (kv_head + 1) * head_width].reshape(
        tok_rows, HEAD_GROUP, D_HEAD
    )
    key_rows = key_window[:, kv_head * D_HEAD : (kv_head + 1) * D_HEAD]
    value_rows = value_window[:, kv_head * D_HEAD : (kv_head + 1) * D_HEAD]
    scores = (
        jnp.einsum("tnd,ud->ntu", query_rows, key_rows, preferred_element_type=jnp.float32)
        * score_scale
    )
    scores = jnp.where(allowed, scores, masked_score)
    sink_rows = sink_logits[kv_head * HEAD_GROUP : (kv_head + 1) * HEAD_GROUP][:, None]
    row_max = jnp.maximum(jnp.max(scores, axis=-1), sink_rows)
    weights = jnp.where(allowed, jnp.exp(scores - row_max[..., None]), 0.0)
    totals = jnp.sum(weights, axis=-1) + jnp.exp(sink_rows - row_max)
    attn_probs = weights / totals[..., None]
    sink_probs = jnp.exp(sink_rows - row_max) / totals
    probs_low = attn_probs.astype(jnp.bfloat16)
    attn_out = jnp.einsum(
        "ntu,ud->tnd", probs_low, value_rows, preferred_element_type=jnp.float32
    ).astype(jnp.bfloat16)
    out_dot = jnp.sum(grad_rows.astype(jnp.float32) * attn_out.astype(jnp.float32), axis=-1).T
    dprobs = jnp.einsum("tnd,ud->ntu", grad_rows, value_rows, preferred_element_type=jnp.float32)
    dscores = (attn_probs * (dprobs - out_dot[..., None])).astype(jnp.bfloat16)
    query_grad = (
        jnp.einsum("ntu,ud->tnd", dscores, key_rows, preferred_element_type=jnp.float32)
        * score_scale
    ).astype(jnp.bfloat16)
    key_grad = (
        jnp.einsum("ntu,tnd->ud", dscores, query_rows, preferred_element_type=jnp.float32)
        * score_scale
    )
    value_grad = jnp.einsum("ntu,tnd->ud", probs_low, grad_rows, preferred_element_type=jnp.float32)
    sink_terms = -jnp.sum(sink_probs * out_dot, axis=-1)
    return (
        attn_out.reshape(tok_rows, head_width),
        query_grad.reshape(tok_rows, head_width),
        key_grad,
        value_grad,
        sink_terms,
    )


def per_device(queries, key_vectors, value_vectors, out_grad, sink_logits, lengths, route_plan):
    tok_rows = queries.shape[1]
    ctx_index = lax.axis_index("ctx")
    group_index = lax.axis_index("dp")
    slot_index = ctx_index // SPAN
    within = ctx_index % SPAN
    route_key = pick_entry(route_plan, slot_index)
    source = jnp.bitwise_xor(group_index, route_key)
    row_pick = (jnp.arange(lengths.shape[0], dtype=jnp.int32) == source)[:, None]
    col_pick = (jnp.arange(lengths.shape[1], dtype=jnp.int32) == slot_index)[None, :]
    length = jnp.sum(jnp.where(row_pick & col_pick, lengths, 0))
    moved_rows = (queries[0], key_vectors[0], value_vectors[0])
    for bit_index in range(lax.axis_size("dp").bit_length() - 1):
        partner = jax.tree.map(
            lambda part, own: part.astype(own.dtype),
            partner_2(for_sending(moved_rows), "dp", bit_index),
            moved_rows,
        )
        is_taken = jnp.bitwise_and(jnp.right_shift(route_key, bit_index), 1) == 1
        moved_rows = tuple(
            (
                jnp.where(is_taken, fresh_block, old_block)
                for fresh_block, old_block in zip(partner, moved_rows)
            )
        )
    my_queries, my_keys, my_values = moved_rows
    earlier = [from_behind((my_keys, my_values), "ctx", distance) for distance in range(1, SPAN)]
    ordered = ([(my_keys, my_values)] + earlier)[::-1]
    key_window = jnp.concatenate([kv_pair[0] for kv_pair in ordered], axis=0)
    value_window = jnp.concatenate([kv_pair[1] for kv_pair in ordered], axis=0)
    token_ids = jnp.arange(tok_rows, dtype=jnp.int32)
    query_pos = within * tok_rows + token_ids
    block_ids = jnp.arange(SPAN, dtype=jnp.int32)
    key_pos = ((within - (SPAN - 1 - block_ids))[:, None] * tok_rows + token_ids[None, :]).reshape(
        SPAN * tok_rows
    )
    allowed = (
        (key_pos[None, :] >= 0)
        & (key_pos[None, :] <= query_pos[:, None])
        & (query_pos[:, None] < length)
    )
    outcomes = [
        group_pass(kv_head, my_queries, out_grad[0], key_window, value_window, sink_logits, allowed)
        for kv_head in range(KV_HEADS)
    ]
    attn_out = jnp.concatenate([outcome[0] for outcome in outcomes], axis=1)
    query_grad = jnp.concatenate([outcome[1] for outcome in outcomes], axis=1)
    key_contrib = jnp.concatenate([outcome[2] for outcome in outcomes], axis=1)
    value_contrib = jnp.concatenate([outcome[3] for outcome in outcomes], axis=1)
    sink_local = jnp.concatenate([outcome[4] for outcome in outcomes], axis=0)

    def block_at(window, distance):
        first_row = (SPAN - 1 - distance) * tok_rows
        return window[first_row : first_row + tok_rows]

    key_total = block_at(key_contrib, 0)
    value_total = block_at(value_contrib, 0)
    for distance in range(1, SPAN):
        back_key, back_value = from_behind(
            (block_at(key_contrib, distance), block_at(value_contrib, distance)), "ctx", -distance
        )
        key_total = key_total + back_key
        value_total = value_total + back_value
    sink_grad = lax.psum(sink_local, ("dp", "ctx"))
    return (
        attn_out[None],
        query_grad[None],
        key_total.astype(jnp.bfloat16)[None],
        value_total.astype(jnp.bfloat16)[None],
        sink_grad,
    )


def solution(mesh):
    placed = (
        P("dp", "ctx", None),
        P("dp", "ctx", None),
        P("dp", "ctx", None),
        P("dp", "ctx", None),
        P(),
        P(),
        P(),
    )
    return jax.shard_map(
        per_device,
        mesh=mesh,
        in_specs=placed,
        out_specs=(
            P("dp", "ctx", None),
            P("dp", "ctx", None),
            P("dp", "ctx", None),
            P("dp", "ctx", None),
            P(),
        ),
        check_vma=False,
    )
```

profile of v0, /device:TPU:1, one launch (start us, length us, event | category | flops | bytes accessed | tf_op | source)
XLA Modules:
  0.0 232.5 jit_solution(7459368596461505082)
XLA Ops:
  1.7 4.0 %collective-permute-start.6 = (bf16[128,256]{0,1:T(8,128)(2,1)S(1)}, bf16[128,256]{0,1:T(8,128)(2,1)S(1)}, u32[]{:S(2)}, u32[]{:S(2)}) collective-permute-start(bf16[128,256]{0,1:T(8,128)(2,1)S(1)} %bitcast.278), channel_id=1, source_target_pairs={{0,64},{64,0},{128,192},{192,128},{256,320},{320,256},{384,448},{4... | collective-permute-start | bytes 196616 | tf_op jit(solution)/shard_map/ppermute | solution.py:22
  5.7 1.9 collective-permute-start.12
  8.6 3.4 %collective-permute-start = (bf16[128,256]{0,1:T(8,128)(2,1)S(1)}, bf16[128,256]{0,1:T(8,128)(2,1)S(1)}, u32[]{:S(2)}, u32[]{:S(2)}) collective-permute-start(bf16[128,256]{0,1:T(8,128)(2,1)S(1)} %bitcast.277), channel_id=1, source_target_pairs={{0,64},{64,0},{128,192},{192,128},{256,320},{320,256},{384,448},{4... | collective-permute-start | bytes 196616 | tf_op jit(solution)/shard_map/ppermute | solution.py:22
  14.1 1.4 select_reduce_fusion
  22.7 4.5 %collective-permute-start.7 = (bf16[128,256]{0,1:T(8,128)(2,1)S(1)}, bf16[128,256]{0,1:T(8,128)(2,1)S(1)}, u32[]{:S(2)}, u32[]{:S(2)}) collective-permute-start(bf16[128,256]{0,1:T(8,128)(2,1)S(1)} %broadcast_select_fusion.3), channel_id=1, source_target_pairs={{0,128},{64,192},{128,0},{192,64},{256,384},{320,448},{384,256},{4... | collective-permute-start | bytes 196616 | tf_op jit(solution)/shard_map/ppermute | solution.py:22
  27.4 2.3 collective-permute-start.13
  29.7 4.5 %collective-permute-start.1 = (bf16[128,256]{0,1:T(8,128)(2,1)S(1)}, bf16[128,256]{0,1:T(8,128)(2,1)S(1)}, u32[]{:S(2)}, u32[]{:S(2)}) collective-permute-start(bf16[128,256]{0,1:T(8,128)(2,1)S(1)} %broadcast_select_fusion.4), channel_id=1, source_target_pairs={{0,128},{64,192},{128,0},{192,64},{256,384},{320,448},{384,256},{4... | collective-permute-start | bytes 196616 | tf_op jit(solution)/shard_map/ppermute | solution.py:22
  34.2 4.7 %collective-permute-start.8 = (bf16[128,256]{0,1:T(8,128)(2,1)S(1)}, bf16[128,256]{0,1:T(8,128)(2,1)S(1)}, u32[]{:S(2)}, u32[]{:S(2)}) collective-permute-start(bf16[128,256]{0,1:T(8,128)(2,1)S(1)} %broadcast_select_fusion.5), channel_id=1, source_target_pairs={{0,256},{64,320},{128,384},{192,448},{256,0},{320,64},{384,128},{4... | collective-permute-start | bytes 196616 | tf_op jit(solution)/shard_map/ppermute | solution.py:22
  38.9 5.4 %collective-permute-done.1 = bf16[128,256]{0,1:T(8,128)(2,1)S(1)} collective-permute-done((bf16[128,256]{0,1:T(8,128)(2,1)S(1)}, bf16[128,256]{0,1:T(8,128)(2,1)S(1)}, u32[]{:S(2)}, u32[]{:S(2)}) %collective-permute-start.1) | collective-permute-done | bytes 65568 | tf_op jit(solution)/shard_map/ppermute | solution.py:22
  44.3 4.2 %collective-permute-start.2 = (bf16[128,256]{0,1:T(8,128)(2,1)S(1)}, bf16[128,256]{0,1:T(8,128)(2,1)S(1)}, u32[]{:S(2)}, u32[]{:S(2)}) collective-permute-start(bf16[128,256]{0,1:T(8,128)(2,1)S(1)} %broadcast_select_fusion.6), channel_id=1, source_target_pairs={{0,256},{64,320},{128,384},{192,448},{256,0},{320,64},{384,128},{4... | collective-permute-start | bytes 196616 | tf_op jit(solution)/shard_map/ppermute | solution.py:22
  48.5 2.6 %collective-permute-start.14 = (bf16[128,2048]{1,0:T(8,128)(2,1)S(1)}, bf16[128,2048]{1,0:T(8,128)(2,1)S(1)}, u32[]{:S(2)}, u32[]{:S(2)}) collective-permute-start(bf16[128,2048]{1,0:T(8,128)(2,1)S(1)} %broadcast_select_fusion.1), channel_id=1, source_target_pairs={{0,256},{64,320},{128,384},{192,448},{256,0},{320,64},{384,128},{4... | collective-permute-start | bytes 1572872 | tf_op jit(solution)/shard_map/ppermute | solution.py:22
  51.2 3.1 %collective-permute-start.10 = (bf16[128,256]{0,1:T(8,128)(2,1)S(1)}, bf16[128,256]{0,1:T(8,128)(2,1)S(1)}, u32[]{:S(2)}, u32[]{:S(2)}) collective-permute-start(bf16[128,256]{0,1:T(8,128)(2,1)S(1)} %broadcast_select_fusion.7), channel_id=1, source_target_pairs={{0,2},{1,3},{2,4},{3,5},{4,6},{5,7},{6,8},{7,9},{8,10},{9,11},{10,... | collective-permute-start | bytes 196616 | tf_op jit(solution)/shard_map/ppermute | solution.py:28
  54.3 7.0 %collective-permute-start.11 = (bf16[128,256]{0,1:T(8,128)(2,1)S(1)}, bf16[128,256]{0,1:T(8,128)(2,1)S(1)}, u32[]{:S(2)}, u32[]{:S(2)}) collective-permute-start(bf16[128,256]{0,1:T(8,128)(2,1)S(1)} %broadcast_select_fusion.7), channel_id=1, source_target_pairs={{0,1},{1,2},{2,3},{3,4},{4,5},{5,6},{6,7},{7,8},{8,9},{9,10},{10,1... | collective-permute-start | bytes 196616 | tf_op jit(solution)/shard_map/ppermute | solution.py:28
  61.3 3.3 %collective-permute-start.9 = (bf16[128,256]{0,1:T(8,128)(2,1)S(1)}, bf16[128,256]{0,1:T(8,128)(2,1)S(1)}, u32[]{:S(2)}, u32[]{:S(2)}) collective-permute-start(bf16[128,256]{0,1:T(8,128)(2,1)S(1)} %broadcast_select_fusion.7), channel_id=1, source_target_pairs={{0,3},{1,4},{2,5},{3,6},{4,7},{5,8},{6,9},{7,10},{8,11},{9,12},{10... | collective-permute-start | bytes 196616 | tf_op jit(solution)/shard_map/ppermute | solution.py:28
  64.6 6.7 %collective-permute-start.3 = (bf16[128,256]{0,1:T(8,128)(2,1)S(1)}, bf16[128,256]{0,1:T(8,128)(2,1)S(1)}, u32[]{:S(2)}, u32[]{:S(2)}) collective-permute-start(bf16[128,256]{0,1:T(8,128)(2,1)S(1)} %broadcast_select_fusion.8), channel_id=1, source_target_pairs={{0,3},{1,4},{2,5},{3,6},{4,7},{5,8},{6,9},{7,10},{8,11},{9,12},{10... | collective-permute-start | bytes 196616 | tf_op jit(solution)/shard_map/ppermute | solution.py:28
  71.3 3.5 %collective-permute-start.4 = (bf16[128,256]{0,1:T(8,128)(2,1)S(1)}, bf16[128,256]{0,1:T(8,128)(2,1)S(1)}, u32[]{:S(2)}, u32[]{:S(2)}) collective-permute-start(bf16[128,256]{0,1:T(8,128)(2,1)S(1)} %broadcast_select_fusion.8), channel_id=1, source_target_pairs={{0,2},{1,3},{2,4},{3,5},{4,6},{5,7},{6,8},{7,9},{8,10},{9,11},{10,... | collective-permute-start | bytes 196616 | tf_op jit(solution)/shard_map/ppermute | solution.py:28
  74.8 2.2 collective-permute-start.5
  79.2 1.8 fusion.46
  82.9 1.4 fusion.13
  84.3 1.4 multiply_reduce_fusion.3
  85.7 1.4 convolution_bitcast_fusion.3
  88.9 1.5 fusion.15
  90.5 1.4 multiply_reduce_fusion.2
  92.1 1.4 convolution_bitcast_fusion.2
  95.3 1.4 multiply_reduce_fusion.1
  96.6 1.4 convolution_bitcast_fusion.1
  101.0 1.4 convolution_bitcast_fusion
  104.1 102.7 %psum.7 = f32[32]{0:T(128)} all-reduce(f32[32]{0:T(128)S(1)} %pad_maximum_fusion.4), channel_id=1, replica_groups=mesh['dp'=8,'ctx'=64] {'dp','ctx'}, use_global_device_ids=true, to_apply=%region_18.19 | all-reduce | flops 32 | bytes 256 | tf_op jit(solution)/shard_map/psum | solution.py:148
  207.6 2.6 %collective-permute-start.18 = (f32[128,256]{0,1:T(8,128)}, f32[128,256]{0,1:T(8,128)S(1)}, u32[]{:S(2)}, u32[]{:S(2)}) collective-permute-start(f32[128,256]{0,1:T(8,128)} %get-tuple-element.17), channel_id=1, source_target_pairs={{1,0},{2,1},{3,2},{4,3},{5,4},{6,5},{7,6},{8,7},{9,8},{10,9},{11,1... | collective-permute-start | bytes 393224 | tf_op jit(solution)/shard_map/ppermute | solution.py:28
  213.5 1.9 collective-permute-start.15
  220.1 3.4 %collective-permute-done.20 = f32[128,256]{0,1:T(8,128)} collective-permute-done((f32[128,256]{0,1:T(8,128)S(1)}, f32[128,256]{0,1:T(8,128)}, u32[]{:S(2)}, u32[]{:S(2)}) %collective-permute-start.20) | collective-permute-done | bytes 131104 | tf_op jit(solution)/shard_map/ppermute | solution.py:28
  225.2 6.5 %collective-permute-done.17 = f32[128,256]{0,1:T(8,128)S(1)} collective-permute-done((f32[128,256]{0,1:T(8,128)S(1)}, f32[128,256]{0,1:T(8,128)S(1)}, u32[]{:S(2)}, u32[]{:S(2)}) %collective-permute-start.17) | collective-permute-done | bytes 131104 | tf_op jit(solution)/shard_map/ppermute | solution.py:28
  (130 shorter events, 32.5 us)
Async XLA Ops:
  0.6 26.7 %copy-start.1 = (bf16[1,128,2048]{2,1,0:T(8,128)(2,1)S(1)}, bf16[1,128,2048]{2,1,0:T(8,128)(2,1)}, u32[]{:S(2)}) copy-start(bf16[1,128,2048]{2,1,0:T(8,128)(2,1)} %param.7) | copy-start | bytes 1572868
  1.7 21.1 %collective-permute-start.6 = (bf16[128,256]{0,1:T(8,128)(2,1)S(1)}, bf16[128,256]{0,1:T(8,128)(2,1)S(1)}, u32[]{:S(2)}, u32[]{:S(2)}) collective-permute-start(bf16[128,256]{0,1:T(8,128)(2,1)S(1)} %bitcast.278), channel_id=1, source_target_pairs={{0,64},{64,0},{128,192},{192,128},{256,320},{320,256},{384,448},{4... | collective-permute-start | bytes 196616 | tf_op jit(solution)/shard_map/ppermute | solution.py:22
  5.7 21.6 %collective-permute-start.12 = (bf16[128,2048]{1,0:T(8,128)(2,1)}, bf16[128,2048]{1,0:T(8,128)(2,1)S(1)}, u32[]{:S(2)}, u32[]{:S(2)}) collective-permute-start(bf16[128,2048]{1,0:T(8,128)(2,1)} %bitcast.276), channel_id=1, source_target_pairs={{0,64},{64,0},{128,192},{192,128},{256,320},{320,256},{384,448},{4... | collective-permute-start | bytes 1572872 | tf_op jit(solution)/shard_map/ppermute | solution.py:22
  8.6 21.1 %collective-permute-start = (bf16[128,256]{0,1:T(8,128)(2,1)S(1)}, bf16[128,256]{0,1:T(8,128)(2,1)S(1)}, u32[]{:S(2)}, u32[]{:S(2)}) collective-permute-start(bf16[128,256]{0,1:T(8,128)(2,1)S(1)} %bitcast.277), channel_id=1, source_target_pairs={{0,64},{64,0},{128,192},{192,128},{256,320},{320,256},{384,448},{4... | collective-permute-start | bytes 196616 | tf_op jit(solution)/shard_map/ppermute | solution.py:22
  22.7 11.5 %collective-permute-start.7 = (bf16[128,256]{0,1:T(8,128)(2,1)S(1)}, bf16[128,256]{0,1:T(8,128)(2,1)S(1)}, u32[]{:S(2)}, u32[]{:S(2)}) collective-permute-start(bf16[128,256]{0,1:T(8,128)(2,1)S(1)} %broadcast_select_fusion.3), channel_id=1, source_target_pairs={{0,128},{64,192},{128,0},{192,64},{256,384},{320,448},{384,256},{4... | collective-permute-start | bytes 196616 | tf_op jit(solution)/shard_map/ppermute | solution.py:22
  27.4 21.1 %collective-permute-start.13 = (bf16[128,2048]{1,0:T(8,128)(2,1)S(1)}, bf16[128,2048]{1,0:T(8,128)(2,1)S(1)}, u32[]{:S(2)}, u32[]{:S(2)}) collective-permute-start(bf16[128,2048]{1,0:T(8,128)(2,1)S(1)} %broadcast_select_fusion), channel_id=1, source_target_pairs={{0,128},{64,192},{128,0},{192,64},{256,384},{320,448},{384,256},{4... | collective-permute-start | bytes 1572872 | tf_op jit(solution)/shard_map/ppermute | solution.py:22
  29.7 14.6 %collective-permute-start.1 = (bf16[128,256]{0,1:T(8,128)(2,1)S(1)}, bf16[128,256]{0,1:T(8,128)(2,1)S(1)}, u32[]{:S(2)}, u32[]{:S(2)}) collective-permute-start(bf16[128,256]{0,1:T(8,128)(2,1)S(1)} %broadcast_select_fusion.4), channel_id=1, source_target_pairs={{0,128},{64,192},{128,0},{192,64},{256,384},{320,448},{384,256},{4... | collective-permute-start | bytes 196616 | tf_op jit(solution)/shard_map/ppermute | solution.py:22
  34.2 16.9 %collective-permute-start.8 = (bf16[128,256]{0,1:T(8,128)(2,1)S(1)}, bf16[128,256]{0,1:T(8,128)(2,1)S(1)}, u32[]{:S(2)}, u32[]{:S(2)}) collective-permute-start(bf16[128,256]{0,1:T(8,128)(2,1)S(1)} %broadcast_select_fusion.5), channel_id=1, source_target_pairs={{0,256},{64,320},{128,384},{192,448},{256,0},{320,64},{384,128},{4... | collective-permute-start | bytes 196616 | tf_op jit(solution)/shard_map/ppermute | solution.py:22
  44.3 20.3 %collective-permute-start.2 = (bf16[128,256]{0,1:T(8,128)(2,1)S(1)}, bf16[128,256]{0,1:T(8,128)(2,1)S(1)}, u32[]{:S(2)}, u32[]{:S(2)}) collective-permute-start(bf16[128,256]{0,1:T(8,128)(2,1)S(1)} %broadcast_select_fusion.6), channel_id=1, source_target_pairs={{0,256},{64,320},{128,384},{192,448},{256,0},{320,64},{384,128},{4... | collective-permute-start | bytes 196616 | tf_op jit(solution)/shard_map/ppermute | solution.py:22
  48.5 29.8 %collective-permute-start.14 = (bf16[128,2048]{1,0:T(8,128)(2,1)S(1)}, bf16[128,2048]{1,0:T(8,128)(2,1)S(1)}, u32[]{:S(2)}, u32[]{:S(2)}) collective-permute-start(bf16[128,2048]{1,0:T(8,128)(2,1)S(1)} %broadcast_select_fusion.1), channel_id=1, source_target_pairs={{0,256},{64,320},{128,384},{192,448},{256,0},{320,64},{384,128},{4... | collective-permute-start | bytes 1572872 | tf_op jit(solution)/shard_map/ppermute | solution.py:22
  51.2 20.0 %collective-permute-start.10 = (bf16[128,256]{0,1:T(8,128)(2,1)S(1)}, bf16[128,256]{0,1:T(8,128)(2,1)S(1)}, u32[]{:S(2)}, u32[]{:S(2)}) collective-permute-start(bf16[128,256]{0,1:T(8,128)(2,1)S(1)} %broadcast_select_fusion.7), channel_id=1, source_target_pairs={{0,2},{1,3},{2,4},{3,5},{4,6},{5,7},{6,8},{7,9},{8,10},{9,11},{10,... | collective-permute-start | bytes 196616 | tf_op jit(solution)/shard_map/ppermute | solution.py:28
  54.3 20.5 %collective-permute-start.11 = (bf16[128,256]{0,1:T(8,128)(2,1)S(1)}, bf16[128,256]{0,1:T(8,128)(2,1)S(1)}, u32[]{:S(2)}, u32[]{:S(2)}) collective-permute-start(bf16[128,256]{0,1:T(8,128)(2,1)S(1)} %broadcast_select_fusion.7), channel_id=1, source_target_pairs={{0,1},{1,2},{2,3},{3,4},{4,5},{5,6},{6,7},{7,8},{8,9},{9,10},{10,1... | collective-permute-start | bytes 196616 | tf_op jit(solution)/shard_map/ppermute | solution.py:28
  61.3 15.8 %collective-permute-start.9 = (bf16[128,256]{0,1:T(8,128)(2,1)S(1)}, bf16[128,256]{0,1:T(8,128)(2,1)S(1)}, u32[]{:S(2)}, u32[]{:S(2)}) collective-permute-start(bf16[128,256]{0,1:T(8,128)(2,1)S(1)} %broadcast_select_fusion.7), channel_id=1, source_target_pairs={{0,3},{1,4},{2,5},{3,6},{4,7},{5,8},{6,9},{7,10},{8,11},{9,12},{10... | collective-permute-start | bytes 196616 | tf_op jit(solution)/shard_map/ppermute | solution.py:28
  64.6 12.5 %collective-permute-start.3 = (bf16[128,256]{0,1:T(8,128)(2,1)S(1)}, bf16[128,256]{0,1:T(8,128)(2,1)S(1)}, u32[]{:S(2)}, u32[]{:S(2)}) collective-permute-start(bf16[128,256]{0,1:T(8,128)(2,1)S(1)} %broadcast_select_fusion.8), channel_id=1, source_target_pairs={{0,3},{1,4},{2,5},{3,6},{4,7},{5,8},{6,9},{7,10},{8,11},{9,12},{10... | collective-permute-start | bytes 196616 | tf_op jit(solution)/shard_map/ppermute | solution.py:28
  71.3 5.8 %collective-permute-start.4 = (bf16[128,256]{0,1:T(8,128)(2,1)S(1)}, bf16[128,256]{0,1:T(8,128)(2,1)S(1)}, u32[]{:S(2)}, u32[]{:S(2)}) collective-permute-start(bf16[128,256]{0,1:T(8,128)(2,1)S(1)} %broadcast_select_fusion.8), channel_id=1, source_target_pairs={{0,2},{1,3},{2,4},{3,5},{4,6},{5,7},{6,8},{7,9},{8,10},{9,11},{10,... | collective-permute-start | bytes 196616 | tf_op jit(solution)/shard_map/ppermute | solution.py:28
  74.8 3.5 %collective-permute-start.5 = (bf16[128,256]{0,1:T(8,128)(2,1)S(1)}, bf16[128,256]{0,1:T(8,128)(2,1)S(1)}, u32[]{:S(2)}, u32[]{:S(2)}) collective-permute-start(bf16[128,256]{0,1:T(8,128)(2,1)S(1)} %broadcast_select_fusion.8), channel_id=1, source_target_pairs={{0,1},{1,2},{2,3},{3,4},{4,5},{5,6},{6,7},{7,8},{8,9},{9,10},{10,1... | collective-permute-start | bytes 196616 | tf_op jit(solution)/shard_map/ppermute | solution.py:28
  78.4 19.6 %copy-start.2 = (bf16[512,256]{0,1:T(8,128)(2,1)}, bf16[512,256]{0,1:T(8,128)(2,1)S(1)}, u32[]{:S(2)}) copy-start(bf16[512,256]{0,1:T(8,128)(2,1)S(1)} %pad_maximum_fusion.2) | copy-start | bytes 786436
  81.3 1.6 copy-start
  82.9 1.5 copy-start.6
  103.3 103.6 %copy-start.10 = (f32[512,64]{0,1:T(8,128)S(1)}, f32[512,64]{0,1:T(8,128)}, u32[]{:S(2)}) copy-start(f32[512,64]{0,1:T(8,128)} %convolution_bitcast_fusion.3) | copy-start | bytes 393220
  103.3 103.5 %copy-start.11 = (f32[512,64]{0,1:T(8,128)S(1)}, f32[512,64]{0,1:T(8,128)}, u32[]{:S(2)}) copy-start(f32[512,64]{0,1:T(8,128)} %convolution_bitcast_fusion.2) | copy-start | bytes 393220
  103.3 103.5 %copy-start.12 = (f32[512,64]{0,1:T(8,128)S(1)}, f32[512,64]{0,1:T(8,128)}, u32[]{:S(2)}) copy-start(f32[512,64]{0,1:T(8,128)} %convolution_bitcast_fusion.1) | copy-start | bytes 393220
  103.3 103.5 %copy-start.13 = (f32[512,64]{0,1:T(8,128)S(1)}, f32[512,64]{0,1:T(8,128)}, u32[]{:S(2)}) copy-start(f32[512,64]{0,1:T(8,128)} %convolution_bitcast_fusion) | copy-start | bytes 393220
  206.9 10.3 %copy-start.7 = (bf16[64,8,128]{2,0,1:T(8,128)(2,1)S(1)}, bf16[64,8,128]{2,0,1:T(8,128)(2,1)}, u32[]{:S(2)}) copy-start(bf16[64,8,128]{2,0,1:T(8,128)(2,1)} %get-tuple-element.45) | copy-start | bytes 393220
  206.9 10.5 %copy-start.8 = (bf16[64,8,128]{2,0,1:T(8,128)(2,1)S(1)}, bf16[64,8,128]{2,0,1:T(8,128)(2,1)}, u32[]{:S(2)}) copy-start(bf16[64,8,128]{2,0,1:T(8,128)(2,1)} %get-tuple-element.43) | copy-start | bytes 393220
  206.9 10.6 %copy-start.9 = (bf16[64,8,128]{2,0,1:T(8,128)(2,1)S(1)}, bf16[64,8,128]{2,0,1:T(8,128)(2,1)}, u32[]{:S(2)}) copy-start(bf16[64,8,128]{2,0,1:T(8,128)(2,1)} %get-tuple-element.41) | copy-start | bytes 393220
  207.6 11.2 %collective-permute-start.18 = (f32[128,256]{0,1:T(8,128)}, f32[128,256]{0,1:T(8,128)S(1)}, u32[]{:S(2)}, u32[]{:S(2)}) collective-permute-start(f32[128,256]{0,1:T(8,128)} %get-tuple-element.17), channel_id=1, source_target_pairs={{1,0},{2,1},{3,2},{4,3},{5,4},{6,5},{7,6},{8,7},{9,8},{10,9},{11,1... | collective-permute-start | bytes 393224 | tf_op jit(solution)/shard_map/ppermute | solution.py:28
  210.2 9.9 %collective-permute-start.19 = (f32[128,256]{0,1:T(8,128)}, f32[128,256]{0,1:T(8,128)S(1)}, u32[]{:S(2)}, u32[]{:S(2)}) collective-permute-start(f32[128,256]{0,1:T(8,128)} %get-tuple-element.19), channel_id=1, source_target_pairs={{2,0},{3,1},{4,2},{5,3},{6,4},{7,5},{8,6},{9,7},{10,8},{11,9},{12,... | collective-permute-start | bytes 393224 | tf_op jit(solution)/shard_map/ppermute | solution.py:28
  211.5 12.0 %collective-permute-start.20 = (f32[128,256]{0,1:T(8,128)S(1)}, f32[128,256]{0,1:T(8,128)}, u32[]{:S(2)}, u32[]{:S(2)}) collective-permute-start(f32[128,256]{0,1:T(8,128)S(1)} %get-tuple-element.18), channel_id=1, source_target_pairs={{3,0},{4,1},{5,2},{6,3},{7,4},{8,5},{9,6},{10,7},{11,8},{12,9},{13... | collective-permute-start | bytes 393224 | tf_op jit(solution)/shard_map/ppermute | solution.py:28
  213.5 11.7 %collective-permute-start.15 = (f32[128,256]{0,1:T(8,128)}, f32[128,256]{0,1:T(8,128)S(1)}, u32[]{:S(2)}, u32[]{:S(2)}) collective-permute-start(f32[128,256]{0,1:T(8,128)} %get-tuple-element.20), channel_id=1, source_target_pairs={{1,0},{2,1},{3,2},{4,3},{5,4},{6,5},{7,6},{8,7},{9,8},{10,9},{11,1... | collective-permute-start | bytes 393224 | tf_op jit(solution)/shard_map/ppermute | solution.py:28
  215.4 9.8 %collective-permute-start.16 = (f32[128,256]{0,1:T(8,128)S(1)}, f32[128,256]{0,1:T(8,128)S(1)}, u32[]{:S(2)}, u32[]{:S(2)}) collective-permute-start(f32[128,256]{0,1:T(8,128)S(1)} %get-tuple-element.22), channel_id=1, source_target_pairs={{2,0},{3,1},{4,2},{5,3},{6,4},{7,5},{8,6},{9,7},{10,8},{11,9},{12,... | collective-permute-start | bytes 393224 | tf_op jit(solution)/shard_map/ppermute | solution.py:28
  218.8 12.8 %collective-permute-start.17 = (f32[128,256]{0,1:T(8,128)S(1)}, f32[128,256]{0,1:T(8,128)S(1)}, u32[]{:S(2)}, u32[]{:S(2)}) collective-permute-start(f32[128,256]{0,1:T(8,128)S(1)} %get-tuple-element.21), channel_id=1, source_target_pairs={{3,0},{4,1},{5,2},{6,3},{7,4},{8,5},{9,6},{10,7},{11,8},{12,9},{13... | collective-permute-start | bytes 393224 | tf_op jit(solution)/shard_map/ppermute | solution.py:28
  (3 other events, 2.8 us)
where the time goes:
time: 236 us; the launch traced here: 232 us
  blocking collectives  103 us (44%)
  starting transfers between devices  67.4 us (29%)
  matrix products  21 us (9%)
  waiting for transfers between devices  16.5 us (7%)
  local copies, waits for them, and re-layouts  12 us (5%)
  other arithmetic  8.79 us (4%)
  between operations  4.05 us (2%)
    psum x1, blocking collectives, per_device(): sink_grad = lax.psum(sink_local, ('dp', 'ctx'))  103 us
    ppermute x12, starting transfers between devices, from_behind(): return lax.ppermute(shard, axis, pairs)  35.4 us
    ppermute x9, starting transfers between devices, partner_2(): return lax.ppermute(value, axis, pairs)  32.1 us
    ppermute x12, waiting for transfers between devices, from_behind(): return lax.ppermute(shard, axis, pairs)  11.1 us
    dot_general x4, matrix products, group_pass(): jnp.einsum('ntu,tnd->ud', probs_low, grad_rows, preferred_element_type=jn...  5.57 us
    ppermute x9, waiting for transfers between devices, partner_2(): return lax.ppermute(value, axis, pairs)  5.41 us
    dot_general x4, matrix products, group_pass(): jnp.einsum('ntu,ud->tnd', probs_low, value_rows, preferred_element_type=j...  5.04 us
    unnamed x32, local copies, waits for them, and re-layouts  4.73 us
  transfers between devices with their start and end apart: 21, of which 4 were waited for; matrix products, arithmetic and copies ran while one was open for 6% of the time, Pallas kernels for 0%

commit v1 on v0

v1 whole, which is shorter than its diff:
```python
import jax
import jax.numpy as jnp
from jax import lax
from jax.experimental import pallas as pl
from jax.experimental.pallas import tpu as pltpu
from jax.sharding import PartitionSpec as P

D_HEAD = 64
KV_HEADS = 4
HEAD_GROUP = 8
Q_HEADS = KV_HEADS * HEAD_GROUP
SPAN = 4
LANES = 128
KV_COLS = KV_HEADS * D_HEAD
SCALE = D_HEAD**-0.5
LOG2E = 1.4426950408889634
MASKED = -1e30
Z_CORE = 32


def attention_kernel(
    lengths_ref, plan_ref, sink_ref, q_ref, do_ref, kv_ref,
    out_ref, dq_ref, own_ref, send_ref, part_ref,
    acc_k, acc_v, terms,
):
    f32, bf16 = jnp.float32, jnp.bfloat16
    rows = q_ref.shape[0]
    window = SPAN * rows
    ctx = lax.axis_index("ctx")
    slot = ctx // SPAN
    within = ctx % SPAN
    source = jnp.bitwise_xor(lax.axis_index("dp"), plan_ref[slot])
    length = lengths_ref[source, slot]

    key_pos = lax.broadcasted_iota(jnp.int32, (window, rows), 0)
    query_pos = lax.broadcasted_iota(jnp.int32, (window, rows), 1) + within * rows
    allowed = (key_pos <= query_pos) & (query_pos < length)
    bias = jnp.where(allowed, 0.0, MASKED).astype(f32)
    bias2 = jnp.concatenate([bias, bias], axis=1)
    lane = lax.broadcasted_iota(jnp.int32, (rows, LANES), 1)
    low = lane < D_HEAD
    wide_low = lax.broadcasted_iota(jnp.int32, (window, LANES), 1) < D_HEAD
    zeros_rows = jnp.zeros((D_HEAD, 2 * rows), bf16)
    half_c = SCALE * LOG2E
    terms[...] = jnp.zeros_like(terms)

    def dot(a, b):
        return jnp.dot(a, b, preferred_element_type=f32)

    def spread(two):
        zero = jnp.zeros_like(two)
        return jnp.concatenate([jnp.where(low, two, zero), jnp.where(low, zero, two)], axis=0)

    def padded(block, half):
        return jnp.concatenate([block, zeros_rows] if half == 0 else [zeros_rows, block], axis=0)

    for duo in range(KV_HEADS // 2):
        keys = kv_ref[:, duo * LANES : (duo + 1) * LANES]
        values = kv_ref[:, KV_COLS + duo * LANES : KV_COLS + (duo + 1) * LANES]
        keys_t = keys.T
        values_t = values.T
        for half in range(2):
            group = 2 * duo + half
            key_rows_t = keys_t[half * D_HEAD : (half + 1) * D_HEAD]
            value_rows_t = values_t[half * D_HEAD : (half + 1) * D_HEAD]
            for pair in range(HEAD_GROUP // 2):
                first = group * HEAD_GROUP + 2 * pair
                cols = slice(first * D_HEAD, first * D_HEAD + LANES)
                q2 = q_ref[:, cols]
                do2 = do_ref[:, cols]
                q2_t = q2.T
                do2_t = do2.T
                q_t = jnp.concatenate([q2_t[:D_HEAD], q2_t[D_HEAD:]], axis=1)
                do_t = jnp.concatenate([do2_t[:D_HEAD], do2_t[D_HEAD:]], axis=1)
                scores = dot(keys, padded(q_t, half)) + bias2
                sink8 = jnp.concatenate(
                    [jnp.full((1, rows), sink_ref[first] / SCALE), jnp.full((1, rows), sink_ref[first + 1] / SCALE)],
                    axis=1,
                )
                row_max = jnp.maximum(jnp.max(scores, axis=0, keepdims=True), sink8)
                weights = jnp.exp2((scores - row_max) * half_c)
                sink_weight = jnp.exp2((sink8 - row_max) * half_c)
                inverse = 1.0 / (jnp.sum(weights, axis=0, keepdims=True) + sink_weight)
                probs = weights * inverse
                probs_low = probs.astype(bf16)
                out_t = dot(value_rows_t, probs_low).astype(bf16)
                out_dot = jnp.sum(do_t.astype(f32) * out_t.astype(f32), axis=0, keepdims=True)
                dprobs = dot(values, padded(do_t, half))
                dscores = (probs * (dprobs - out_dot)).astype(bf16)
                dq_t = (dot(key_rows_t, dscores) * SCALE).astype(bf16)
                dk = dot(dscores, spread(q2))
                dv = dot(probs_low, spread(do2))
                if pair == 0:
                    acc_k[half] = dk
                    acc_v[half] = dv
                else:
                    acc_k[half] += dk
                    acc_v[half] += dv
                sink_terms = -(sink_weight * inverse) * out_dot
                terms[first : first + 1, :] = sink_terms[:, :rows]
                terms[first + 1 : first + 2, :] = sink_terms[:, rows:]
                out_ref[:, cols] = jnp.concatenate([out_t[:, :rows], out_t[:, rows:]], axis=0).T
                dq_ref[:, cols] = jnp.concatenate([dq_t[:, :rows], dq_t[:, rows:]], axis=0).T
        for which, acc, factor in ((0, acc_k, SCALE), (1, acc_v, None)):
            even = acc[0] + pltpu.roll(acc[0], D_HEAD, 1)
            odd = acc[1] + pltpu.roll(acc[1], D_HEAD, 1)
            total = jnp.where(wide_low, even, odd)
            if factor is not None:
                total = total * factor
            acc[0] = total
            at = slice(which * KV_COLS + duo * LANES, which * KV_COLS + (duo + 1) * LANES)
            own_ref[:, at] = acc[0, pl.ds(pl.multiple_of(within * rows, rows), rows), :]
            for distance in range(1, SPAN):
                block = jnp.maximum(within - distance, 0)
                send_ref[distance - 1, :, at] = acc[0, pl.ds(pl.multiple_of(block * rows, rows), rows), :].astype(bf16)
    part = jnp.sum(terms[...].T, axis=0, keepdims=True)
    part_ref[...] = jnp.broadcast_to(part[None], part_ref.shape)


def attention(lengths, route_plan, sink_logits, queries, out_grad, kv):
    rows, width = queries.shape
    f32, bf16 = jnp.float32, jnp.bfloat16
    smem = pl.BlockSpec(memory_space=pltpu.SMEM)
    vmem = pl.BlockSpec(memory_space=pltpu.VMEM)
    products = 6 * 2 * Q_HEADS * rows * SPAN * rows * D_HEAD
    return pl.pallas_call(
        attention_kernel,
        out_shape=(
            jax.ShapeDtypeStruct((rows, width), bf16),
            jax.ShapeDtypeStruct((rows, width), bf16),
            jax.ShapeDtypeStruct((rows, 2 * KV_COLS), f32),
            jax.ShapeDtypeStruct((SPAN - 1, rows, 2 * KV_COLS), bf16),
            jax.ShapeDtypeStruct((Z_CORE, 1, LANES), f32),
        ),
        in_specs=[smem, smem, smem, vmem, vmem, vmem],
        out_specs=(vmem,) * 5,
        scratch_shapes=[
            pltpu.VMEM((2, SPAN * rows, LANES), f32),
            pltpu.VMEM((2, SPAN * rows, LANES), f32),
            pltpu.VMEM((LANES, LANES), f32),
        ],
        compiler_params=pltpu.CompilerParams(vmem_limit_bytes=40 * 2**20),
        cost_estimate=pl.CostEstimate(
            flops=products, bytes_accessed=3 * 2**20, transcendentals=Q_HEADS * rows * SPAN * rows
        ),
    )(lengths, route_plan, sink_logits, queries, out_grad, kv)


def sink_total(part):
    z_core = [[x * 32 + i for i in range(32)] for x in range(2)]
    x_y = [[dp * 64 + x * 32 + i for dp in range(8) for x in range(2)] for i in range(32)]
    near = lax.all_to_all(part, "ctx", 0, 0, axis_index_groups=z_core, tiled=True)
    row = jnp.sum(near, axis=0)
    rows = jnp.broadcast_to(row[None], (16, 1, LANES))
    far = lax.all_to_all(rows, ("dp", "ctx"), 0, 0, axis_index_groups=x_y, tiled=True)
    return jnp.sum(far, axis=(0, 1))[:Q_HEADS]


def per_device(queries, key_vectors, value_vectors, out_grad, sink_logits, lengths, route_plan):
    slot = lax.axis_index("ctx") // SPAN
    key = lax.dynamic_index_in_dim(route_plan, slot, 0, keepdims=False)
    kv = jnp.concatenate([key_vectors[0], value_vectors[0]], axis=1)
    slots = [[SPAN * s + i for i in range(SPAN)] for s in range(16)]

    def gathered(block):
        return lax.all_gather(block, "ctx", axis_index_groups=slots, tiled=True)

    def branch(bits):
        pairs = [(i, i ^ bits) for i in range(8)]

        def move(queries, kv):
            if bits == 0:
                return queries, gathered(kv)
            moved = lax.ppermute(kv, "dp", pairs)
            return lax.ppermute(queries, "dp", pairs), gathered(moved)

        return move

    my_queries, kv_window = lax.switch(key, [branch(bits) for bits in range(8)], queries[0], kv)
    out, dq, own, send, part = attention(
        lengths, route_plan, sink_logits, my_queries, out_grad[0], kv_window
    )
    total = own
    for distance in range(1, SPAN):
        pairs = [(SPAN * s + i, SPAN * s + i - distance) for s in range(16) for i in range(distance, SPAN)]
        total = total + lax.ppermute(send[distance - 1], "ctx", pairs).astype(jnp.float32)
    total = total.astype(jnp.bfloat16)
    sink_grad = sink_total(part)
    return (
        out[None],
        dq[None],
        total[:, :KV_COLS][None],
        total[:, KV_COLS:][None],
        sink_grad,
    )


def solution(mesh):
    split = P("dp", "ctx", None)
    return jax.shard_map(
        per_device,
        mesh=mesh,
        in_specs=(split, split, split, split, P(), P(), P()),
        out_specs=(split, split, split, split, P()),
        check_vma=False,
    )
```

time: 236 us -> 94.5 us (0.40); the launches traced: 232 us -> 94.1 us
  starting transfers between devices: 67.4 us -> 12.6 us
  blocking collectives: 103 us -> 51.4 us
  matrix products: 21 us -> 0 us
  Pallas kernels: 0 us -> 14.1 us
  local copies, waits for them, and re-layouts: 12 us -> 3.55 us
  other arithmetic: 8.79 us -> 0.65 us
  waiting for transfers between devices: 16.5 us -> 10.1 us
  between operations: 4.05 us -> 1.44 us
    psum x1 -> x0, blocking collectives: 103 us -> none  [per_device(): sink_grad = lax.psum(sink_local, ('dp', 'ctx'))]
    ppermute x21 -> x5, starting transfers between devices: 67.4 us -> 12.6 us  [the longest x1 6.63 us: move(): return (lax.ppermute(queries, 'dp', pairs), gathered(moved))]
    all_to_all x0 -> x2, blocking collectives: none -> 40.2 us  [the longest x1 27.6 us: sink_total(): lax.all_to_all(part, 'ctx', 0, 0, axis_index_groups=z_core, tiled=True)]
    dot_general x24 -> x0, matrix products: 21 us -> none  [the longest x4 5.57 us: group_pass(): jnp.einsum('ntu,tnd->ud', probs_low, grad_rows, preferred_element_type=jn...]
    pallas_call x0 -> x1, Pallas kernels: none -> 14.1 us  [attention(): pl.pallas_call(attention_kernel, out_shape=(jax.ShapeDtypeStruct((rows, w...]
    all_gather x0 -> x1, blocking collectives: none -> 11.2 us  [gathered(): return lax.all_gather(block, 'ctx', axis_index_groups=slots, tiled=True)]
    ppermute x21 -> x5, waiting for transfers between devices: 16.5 us -> 10.1 us  [the longest x1 10.1 us: move(): moved = lax.ppermute(kv, 'dp', pairs)]
    slice x13 -> x0, local copies, waits for them, and re-layouts: 6.33 us -> none  [the longest x5 3.53 us: group_pass(): out_grad[:, kv_head * head_width:(kv_head + 1) * head_width]]
  transfers between devices with their start and end apart: 21 -> 5, of which waited for: 4 -> 1; matrix products, arithmetic and copies ran while one was open for 6% -> 1% of each run, Pallas kernels for 0% -> 0%
where the time goes in v1:
time: 94.5 us; the launch traced here: 94.1 us
  blocking collectives  51.4 us (54%)
  Pallas kernels  14.1 us (15%)
  starting transfers between devices  12.6 us (13%)
  waiting for transfers between devices  10.1 us (11%)
  local copies, waits for them, and re-layouts  3.55 us (4%)
  between operations  1.44 us (2%)
    all_to_all x1, blocking collectives, sink_total(): lax.all_to_all(part, 'ctx', 0, 0, axis_index_groups=z_core, tiled=True)  27.6 us
    pallas_call x1, Pallas kernels, attention(): pl.pallas_call(attention_kernel, out_shape=(jax.ShapeDtypeStruct((rows, w...  14.1 us
    all_to_all x1, blocking collectives, sink_total(): lax.all_to_all(rows, ('dp', 'ctx'), 0, 0, axis_index_groups=x_y, tiled=True)  12.6 us
    all_gather x1, blocking collectives, gathered(): return lax.all_gather(block, 'ctx', axis_index_groups=slots, tiled=True)  11.2 us
    ppermute x1, waiting for transfers between devices, move(): moved = lax.ppermute(kv, 'dp', pairs)  10.1 us
    ppermute x1, starting transfers between devices, move(): return (lax.ppermute(queries, 'dp', pairs), gathered(moved))  6.63 us
    ppermute x3, starting transfers between devices, per_device(): lax.ppermute(send[distance - 1], 'ctx', pairs).astype(jnp.float32)  4.04 us
    unnamed x14, local copies, waits for them, and re-layouts  2.23 us
  transfers between devices with their start and end apart: 5, of which 1 were waited for; matrix products, arithmetic and copies ran while one was open for 1% of the time, Pallas kernels for 0%

profile of v1, /device:TPU:1, one launch (start us, length us, event | category | flops | bytes accessed | tf_op | source)
XLA Modules:
  0.0 94.1 jit_solution(6302135720351274574)
XLA Ops:
  0.6 0.0 copy-start.4
  0.6 0.0 copy-start.6
  0.7 0.9 copy-done.6
  1.5 0.0 copy-done.5
  1.6 0.0 copy-start.2
  1.6 0.6 copy-done.2
  2.3 0.6 dynamic_slice.4
  3.5 0.0 copy-done.4
  3.5 0.0 copy-start
  3.5 30.1 %conditional.1 = (bf16[128,2048]{1,0:T(8,128)(2,1)S(1)}, bf16[512,512]{1,0:T(8,128)(2,1)S(1)}) conditional(s32[]{:T(128)} %bitcast, (bf16[128,512]{1,0:T(8,128)(2,1)S(1)}, bf16[128,2048]{1,0:T(8,128)(2,1)S(1)}) %tuple.54, (bf16[128,2048]{1,0:T(8,128)(2,1)S(1)}, bf16[128,512]{1,0:T(8,128)(2,1)S(1)}) %tuple.55, ...), branch_computations={%region_0.1_spmd, %region_1.2_spmd, %region_2.3_spmd, %region_3.4_... | conditional | bytes 4325472 | solution.py:179
  3.6 6.6 %collective-permute-start.8 = (bf16[128,2048]{1,0:T(8,128)(2,1)S(1)}, bf16[128,2048]{1,0:T(8,128)(2,1)S(1)}, u32[]{:S(2)}, u32[]{:S(2)}) collective-permute-start(bf16[128,2048]{1,0:T(8,128)(2,1)S(1)} %get-tuple-element.42), channel_id=1, source_target_pairs={{0,320},{64,256},{128,448},{192,384},{256,64},{320,0},{384,192},{4... | collective-permute-start | bytes 1572872 | tf_op jit(solution)/shard_map/cond/branch_5_fun/ppermute | solution.py:175
  10.2 1.9 %collective-permute-start.9 = (bf16[128,512]{1,0:T(8,128)(2,1)S(1)}, bf16[128,512]{1,0:T(8,128)(2,1)S(1)}, u32[]{:S(2)}, u32[]{:S(2)}) collective-permute-start(bf16[128,512]{1,0:T(8,128)(2,1)S(1)} %get-tuple-element.43), channel_id=1, source_target_pairs={{0,320},{64,256},{128,448},{192,384},{256,64},{320,0},{384,192},{4... | collective-permute-start | bytes 393224 | tf_op jit(solution)/shard_map/cond/branch_5_fun/ppermute | solution.py:174
  12.1 10.1 %collective-permute-done.9 = bf16[128,512]{1,0:T(8,128)(2,1)S(1)} collective-permute-done((bf16[128,512]{1,0:T(8,128)(2,1)S(1)}, bf16[128,512]{1,0:T(8,128)(2,1)S(1)}, u32[]{:S(2)}, u32[]{:S(2)}) %collective-permute-start.9) | collective-permute-done | bytes 131104 | tf_op jit(solution)/shard_map/cond/branch_5_fun/ppermute | solution.py:174
  22.2 11.2 %all_gather.21 = bf16[512,512]{1,0:T(8,128)(2,1)S(1)} all-gather(bf16[128,512]{1,0:T(8,128)(2,1)S(1)} %collective-permute-done.9), channel_id=1, replica_groups={{0,1,2,3},{4,5,6,7},{8,9,10,11},{12,13,14,15},{16,17,18,19},{20,21,22,2..., dimensions={0}, use_global_device_ids=true | all-gather | bytes 655360 | tf_op jit(solution)/shard_map/cond/branch_5_fun/all_gather | solution.py:166
  33.4 0.0 collective-permute-done.8
  33.6 0.0 copy-start.1
  33.6 0.0 copy-start.3
  33.6 0.0 copy-done
  33.7 0.7 copy-done.1
  34.3 14.1 %shard_map.110 = (bf16[128,2048]{1,0:T(8,128)(2,1)}, bf16[128,2048]{1,0:T(8,128)(2,1)}, f32[128,512]{1,0:T(8,128)S(1)}, bf16[3,128,512]{2,1,0:T(8,128)(2,1)S(1)}, f32[32,1,128]{2,1,0:T(1,128)S(1)}) custom-call(s32[8,16]{1,0:T(8,128)S(1)} %copy-done.1, s32[16]{0:T(128)S(1)} %copy-done.2, f32[32]{0:T(128)S(1)} %copy-done.3, ...), custom_call_target="tpu_custom_call" | custom-call | flops 1610612736 | bytes 3145728 | tf_op jit(solution)/shard_map/pallas_call | solution.py:126
  48.5 2.1 %collective-permute-start.14 = (bf16[128,512]{1,0:T(8,128)(2,1)S(1)}, bf16[128,512]{1,0:T(8,128)(2,1)S(1)}, u32[]{:S(2)}, u32[]{:S(2)}) collective-permute-start(bf16[128,512]{1,0:T(8,128)(2,1)S(1)} %get-tuple-element.67), channel_id=1, source_target_pairs={{1,0},{2,1},{3,2},{5,4},{6,5},{7,6},{9,8},{10,9},{11,10},{13,12},{... | collective-permute-start | bytes 393224 | tf_op jit(solution)/shard_map/ppermute | solution.py:186
  50.6 0.7 collective-permute-start.16
  51.2 1.3 %collective-permute-start.15 = (bf16[128,512]{1,0:T(8,128)(2,1)S(1)}, bf16[128,512]{1,0:T(8,128)(2,1)S(1)}, u32[]{:S(2)}, u32[]{:S(2)}) collective-permute-start(bf16[128,512]{1,0:T(8,128)(2,1)S(1)} %get-tuple-element.69), channel_id=1, source_target_pairs={{2,0},{3,1},{6,4},{7,5},{10,8},{11,9},{14,12},{15,13},{18,16},{19,... | collective-permute-start | bytes 393224 | tf_op jit(solution)/shard_map/ppermute | solution.py:186
  52.5 27.6 %all_to_all.10 = f32[32,1,128]{2,1,0:T(1,128)S(1)} all-to-all(f32[32,1,128]{2,1,0:T(1,128)S(1)} %get-tuple-element.66), channel_id=1, replica_groups={{0,1,2,3,4,5,6,7,8,9,10,11,12,13,14,15,16,17,18,19,20,21,22,23,24,25,26..., dimensions={0} | all-to-all | bytes 32768 | tf_op jit(solution)/shard_map/all_to_all | solution.py:152
  80.1 0.1 reduce_sum.18
  80.2 12.6 %all_to_all.11 = f32[16,1,128]{2,1,0:T(1,128)S(1)} all-to-all(f32[16,1,128]{2,1,0:T(1,128)S(1)} %broadcast_in_dim.22), channel_id=1, replica_groups={{0,32,64,96,128,160,192,224,256,288,320,352,384,416,448,480},{1,33,65,9..., dimensions={0} | all-to-all | bytes 16384 | tf_op jit(solution)/shard_map/all_to_all | solution.py:155
  92.8 0.5 reduce_sum.19
  93.3 0.0 collective-permute-done.14
  93.4 0.0 collective-permute-done.16
  93.4 0.0 collective-permute-done.15
  93.4 0.1 add_convert_fusion
  93.4 0.7 slice_bitcast_fusion.3
  (6 shorter events, 0.1 us)
Async XLA Ops:
  0.6 2.9 %copy-start.4 = (bf16[1,128,2048]{2,1,0:T(8,128)(2,1)S(1)}, bf16[1,128,2048]{2,1,0:T(8,128)(2,1)}, u32[]{:S(2)}) copy-start(bf16[1,128,2048]{2,1,0:T(8,128)(2,1)} %param.15) | copy-start | bytes 1572868
  0.6 0.9 copy-start.6
  0.7 0.9 copy-start.5
  1.6 0.7 copy-start.2
  3.5 30.1 %copy-start = (bf16[1,128,2048]{2,1,0:T(8,128)(2,1)S(1)}, bf16[1,128,2048]{2,1,0:T(8,128)(2,1)}, u32[]{:S(2)}) copy-start(bf16[1,128,2048]{2,1,0:T(8,128)(2,1)} %param.18) | copy-start | bytes 1572868
  3.6 29.8 %collective-permute-start.8 = (bf16[128,2048]{1,0:T(8,128)(2,1)S(1)}, bf16[128,2048]{1,0:T(8,128)(2,1)S(1)}, u32[]{:S(2)}, u32[]{:S(2)}) collective-permute-start(bf16[128,2048]{1,0:T(8,128)(2,1)S(1)} %get-tuple-element.42), channel_id=1, source_target_pairs={{0,320},{64,256},{128,448},{192,384},{256,64},{320,0},{384,192},{4... | collective-permute-start | bytes 1572872 | tf_op jit(solution)/shard_map/cond/branch_5_fun/ppermute | solution.py:175
  10.2 12.0 %collective-permute-start.9 = (bf16[128,512]{1,0:T(8,128)(2,1)S(1)}, bf16[128,512]{1,0:T(8,128)(2,1)S(1)}, u32[]{:S(2)}, u32[]{:S(2)}) collective-permute-start(bf16[128,512]{1,0:T(8,128)(2,1)S(1)} %get-tuple-element.43), channel_id=1, source_target_pairs={{0,320},{64,256},{128,448},{192,384},{256,64},{320,0},{384,192},{4... | collective-permute-start | bytes 393224 | tf_op jit(solution)/shard_map/cond/branch_5_fun/ppermute | solution.py:174
  33.6 0.7 copy-start.1
  33.6 0.7 copy-start.3
  48.5 44.9 %collective-permute-start.14 = (bf16[128,512]{1,0:T(8,128)(2,1)S(1)}, bf16[128,512]{1,0:T(8,128)(2,1)S(1)}, u32[]{:S(2)}, u32[]{:S(2)}) collective-permute-start(bf16[128,512]{1,0:T(8,128)(2,1)S(1)} %get-tuple-element.67), channel_id=1, source_target_pairs={{1,0},{2,1},{3,2},{5,4},{6,5},{7,6},{9,8},{10,9},{11,10},{13,12},{... | collective-permute-start | bytes 393224 | tf_op jit(solution)/shard_map/ppermute | solution.py:186
  50.6 42.8 %collective-permute-start.16 = (bf16[128,512]{1,0:T(8,128)(2,1)S(1)}, bf16[128,512]{1,0:T(8,128)(2,1)S(1)}, u32[]{:S(2)}, u32[]{:S(2)}) collective-permute-start(bf16[128,512]{1,0:T(8,128)(2,1)S(1)} %get-tuple-element.68), channel_id=1, source_target_pairs={{3,0},{7,4},{11,8},{15,12},{19,16},{23,20},{27,24},{31,28},{35,32}... | collective-permute-start | bytes 393224 | tf_op jit(solution)/shard_map/ppermute | solution.py:186
  51.2 42.1 %collective-permute-start.15 = (bf16[128,512]{1,0:T(8,128)(2,1)S(1)}, bf16[128,512]{1,0:T(8,128)(2,1)S(1)}, u32[]{:S(2)}, u32[]{:S(2)}) collective-permute-start(bf16[128,512]{1,0:T(8,128)(2,1)S(1)} %get-tuple-element.69), channel_id=1, source_target_pairs={{2,0},{3,1},{6,4},{7,5},{10,8},{11,9},{14,12},{15,13},{18,16},{19,... | collective-permute-start | bytes 393224 | tf_op jit(solution)/shard_map/ppermute | solution.py:186

commit v2 on v1

v2 whole, which is shorter than its diff:
```python
import jax
import jax.numpy as jnp
from jax import lax
from jax.experimental import pallas as pl
from jax.experimental.pallas import tpu as pltpu
from jax.sharding import PartitionSpec as P

D_HEAD = 64
KV_HEADS = 4
HEAD_GROUP = 8
Q_HEADS = KV_HEADS * HEAD_GROUP
PAIRS = Q_HEADS // 2
SPAN = 4
LANES = 128
KV_COLS = KV_HEADS * D_HEAD
SCALE = D_HEAD**-0.5
TO_LOG2 = SCALE * 1.4426950408889634
MASKED = -1e30
Z_CORE = 32
X_Y = 16


def dot(a, b):
    return jnp.dot(a, b, preferred_element_type=jnp.float32)


def dot_nt(a, b):
    return lax.dot_general(a, b, (((1,), (1,)), ((), ())), preferred_element_type=jnp.float32)


def place(lengths_ref, plan_ref):
    ctx = lax.axis_index("ctx")
    slot = ctx // SPAN
    source = jnp.bitwise_xor(lax.axis_index("dp"), plan_ref[slot])
    return ctx % SPAN, lengths_ref[source, slot]


def forward_kernel(
    lengths_ref, plan_ref, sink_ref, q_ref, do_ref, kv_ref, out_ref, stat_ref, part_ref, terms
):
    f32, bf16 = jnp.float32, jnp.bfloat16
    rows = q_ref.shape[0]
    window = kv_ref.shape[0]
    within, length = place(lengths_ref, plan_ref)
    query_pos = lax.broadcasted_iota(jnp.int32, (rows, window), 0) + within * rows
    key_pos = lax.broadcasted_iota(jnp.int32, (rows, window), 1)
    bias = jnp.where(key_pos <= query_pos, 0.0, MASKED).astype(f32)
    lane = lax.broadcasted_iota(jnp.int32, (rows, LANES), 1)
    low = lane < D_HEAD
    live = lax.broadcasted_iota(jnp.int32, (rows, LANES), 0) + within * rows < length
    wide_low = lax.broadcasted_iota(jnp.int32, (window, LANES), 1) < D_HEAD
    zero = jnp.zeros((window, LANES), bf16)
    one = jnp.ones((window, LANES), bf16)
    ones_low = jnp.where(wide_low, one, zero)
    ones_high = jnp.where(wide_low, zero, one)
    terms[...] = jnp.zeros_like(terms)
    stat = jnp.zeros((rows, LANES), f32)
    for duo in range(KV_HEADS // 2):
        keys = kv_ref[:, duo * LANES : (duo + 1) * LANES]
        values = kv_ref[:, KV_COLS + duo * LANES : KV_COLS + (duo + 1) * LANES]
        keys_swapped = jnp.concatenate([keys[:, D_HEAD:], keys[:, :D_HEAD]], axis=1)
        values_swapped = jnp.concatenate([values[:, D_HEAD:], values[:, :D_HEAD]], axis=1)
        for half in range(2):
            group = 2 * duo + half
            left_k, right_k = (keys, keys_swapped) if half == 0 else (keys_swapped, keys)
            left_v, right_v = (values, values_swapped) if half == 0 else (values_swapped, values)
            key_pair = (jnp.where(wide_low, left_k, zero), jnp.where(wide_low, zero, right_k))
            value_pair = (
                jnp.concatenate([jnp.where(wide_low, left_v, zero), ones_low], axis=1),
                jnp.concatenate([jnp.where(wide_low, zero, right_v), ones_high], axis=1),
            )
            for pair in range(group * 4, group * 4 + 4):
                cols = slice(pair * LANES, (pair + 1) * LANES)
                q2 = q_ref[:, cols]
                sums, maxima, sink_weights = None, [], []
                for which in range(2):
                    scores = dot_nt(q2, key_pair[which]) + bias
                    sink8 = jnp.full((rows, 1), sink_ref[2 * pair + which] / SCALE)
                    row_max = jnp.maximum(jnp.max(scores, axis=1, keepdims=True), sink8)
                    weights = jnp.exp2((scores - row_max) * TO_LOG2).astype(bf16)
                    product = dot(weights, value_pair[which])
                    sums = product if sums is None else sums + product
                    maxima.append(row_max)
                    sink_weights.append(jnp.exp2((sink8 - row_max) * TO_LOG2))
                sink_weight = jnp.where(low, sink_weights[0], sink_weights[1])
                totals = sums[:, LANES:] + sink_weight
                inverse = jnp.where(live, 1.0 / totals, 0.0)
                out = (sums[:, :LANES] * inverse).astype(bf16)
                out_ref[:, cols] = out
                product = do_ref[:, cols].astype(f32) * out.astype(f32)
                term = jnp.sum(-(sink_weight * inverse) * product, axis=0, keepdims=True)
                terms[2 * pair : 2 * pair + 1, :] = jnp.where(low[:1], term, 0.0)
                terms[2 * pair + 1 : 2 * pair + 2, :] = jnp.where(low[:1], 0.0, term)
                log_total = jnp.where(low, maxima[0], maxima[1]) * TO_LOG2 + jnp.log2(totals)
                log_total = jnp.where(live, log_total, -MASKED)
                stat = jnp.where((lane == pair) | (lane == D_HEAD + pair), log_total, stat)
    stat_ref[...] = stat.T
    part = jnp.sum(terms[...].T, axis=0, keepdims=True)
    part_ref[...] = jnp.broadcast_to(part[None], part_ref.shape)


def backward_kernel(
    lengths_ref, plan_ref, q_ref, do_ref, kv_ref, stat_ref, dq_ref, own_ref, send_ref, acc_k, acc_v
):
    f32, bf16 = jnp.float32, jnp.bfloat16
    rows = q_ref.shape[0]
    window = kv_ref.shape[0]
    within, _ = place(lengths_ref, plan_ref)
    key_pos = lax.broadcasted_iota(jnp.int32, (window, rows), 0)
    query_pos = lax.broadcasted_iota(jnp.int32, (window, rows), 1) + within * rows
    bias = jnp.where(key_pos <= query_pos, 0.0, MASKED).astype(f32)
    bias = jnp.concatenate([bias, bias], axis=1)
    low = lax.broadcasted_iota(jnp.int32, (rows, LANES), 1) < D_HEAD
    wide_low = lax.broadcasted_iota(jnp.int32, (window, LANES), 1) < D_HEAD
    zero_rows = jnp.zeros((D_HEAD, 2 * rows), bf16)

    def spread(two):
        zero = jnp.zeros_like(two)
        return jnp.concatenate([jnp.where(low, two, zero), jnp.where(low, zero, two)], axis=0)

    def beside(two, half):
        two_t = two.T
        block = jnp.concatenate([two_t[:D_HEAD], two_t[D_HEAD:]], axis=1)
        return jnp.concatenate([block, zero_rows] if half == 0 else [zero_rows, block], axis=0)

    for duo in range(KV_HEADS // 2):
        keys = kv_ref[:, duo * LANES : (duo + 1) * LANES]
        values = kv_ref[:, KV_COLS + duo * LANES : KV_COLS + (duo + 1) * LANES]
        keys_t = keys.T
        for half in range(2):
            group = 2 * duo + half
            key_rows_t = keys_t[half * D_HEAD : (half + 1) * D_HEAD]
            for pair in range(group * 4, group * 4 + 4):
                cols = slice(pair * LANES, (pair + 1) * LANES)
                q2 = q_ref[:, cols]
                do2 = do_ref[:, cols]
                log_total = jnp.concatenate(
                    [stat_ref[pair : pair + 1, :], stat_ref[D_HEAD + pair : D_HEAD + pair + 1, :]], axis=1
                )
                scores = dot(keys, beside(q2, half)) + bias
                probs = jnp.exp2(scores * TO_LOG2 - log_total)
                dprobs = dot(values, beside(do2, half))
                product = probs * dprobs
                out_dot = jnp.sum(product, axis=0, keepdims=True)
                dscores = (product - probs * out_dot).astype(bf16)
                dq_t = (dot(key_rows_t, dscores) * SCALE).astype(bf16)
                dk = dot(dscores, spread(q2))
                dv = dot(probs.astype(bf16), spread(do2))
                if pair % 4 == 0:
                    acc_k[half] = dk
                    acc_v[half] = dv
                else:
                    acc_k[half] += dk
                    acc_v[half] += dv
                dq_ref[:, cols] = jnp.concatenate([dq_t[:, :rows], dq_t[:, rows:]], axis=0).T
        for which, acc, factor in ((0, acc_k, SCALE), (1, acc_v, None)):
            even = acc[0] + pltpu.roll(acc[0], D_HEAD, 1)
            odd = acc[1] + pltpu.roll(acc[1], D_HEAD, 1)
            total = jnp.where(wide_low, even, odd)
            acc[0] = total if factor is None else total * factor
            at = slice(which * KV_COLS + duo * LANES, which * KV_COLS + (duo + 1) * LANES)
            own_ref[:, at] = acc[0, pl.ds(pl.multiple_of(within * rows, rows), rows), :]
            for distance in range(1, SPAN):
                block = jnp.maximum(within - distance, 0)
                send_ref[distance - 1, :, at] = acc[
                    0, pl.ds(pl.multiple_of(block * rows, rows), rows), :
                ].astype(bf16)


SMEM = pl.BlockSpec(memory_space=pltpu.SMEM)
VMEM = pl.BlockSpec(memory_space=pltpu.VMEM)


def estimate(products, rows):
    return pl.CostEstimate(
        flops=products * 2 * Q_HEADS * rows * SPAN * rows * D_HEAD * 4,
        bytes_accessed=4 * 2**20,
        transcendentals=Q_HEADS * rows * SPAN * rows,
    )


def forward(lengths, route_plan, sink_logits, queries, out_grad, kv):
    rows, width = queries.shape
    return pl.pallas_call(
        forward_kernel,
        out_shape=(
            jax.ShapeDtypeStruct((rows, width), jnp.bfloat16),
            jax.ShapeDtypeStruct((LANES, rows), jnp.float32),
            jax.ShapeDtypeStruct((Z_CORE, 1, LANES), jnp.float32),
        ),
        in_specs=[SMEM] * 3 + [VMEM] * 3,
        out_specs=(VMEM,) * 3,
        scratch_shapes=[pltpu.VMEM((LANES, LANES), jnp.float32)],
        compiler_params=pltpu.CompilerParams(vmem_limit_bytes=32 * 2**20),
        cost_estimate=estimate(3, rows),
        name="forward",
    )(lengths, route_plan, sink_logits, queries, out_grad, kv)


def backward(lengths, route_plan, queries, out_grad, kv, stat):
    rows, width = queries.shape
    return pl.pallas_call(
        backward_kernel,
        out_shape=(
            jax.ShapeDtypeStruct((rows, width), jnp.bfloat16),
            jax.ShapeDtypeStruct((rows, 2 * KV_COLS), jnp.float32),
            jax.ShapeDtypeStruct((SPAN - 1, rows, 2 * KV_COLS), jnp.bfloat16),
        ),
        in_specs=[SMEM] * 2 + [VMEM] * 4,
        out_specs=(VMEM,) * 3,
        scratch_shapes=[pltpu.VMEM((2, SPAN * rows, LANES), jnp.float32)] * 2,
        compiler_params=pltpu.CompilerParams(vmem_limit_bytes=32 * 2**20),
        cost_estimate=estimate(6, rows),
        name="backward",
    )(lengths, route_plan, queries, out_grad, kv, stat)


def relay_kernel(rows_ref, out_ref):
    total = jnp.sum(rows_ref[...], axis=0, keepdims=True)
    out_ref[...] = jnp.broadcast_to(total, out_ref.shape)


def relay(rows, copies, weight):
    return pl.pallas_call(
        relay_kernel,
        out_shape=jax.ShapeDtypeStruct((copies, 1, LANES), jnp.float32),
        in_specs=[VMEM],
        out_specs=VMEM,
        cost_estimate=pl.CostEstimate(flops=weight, bytes_accessed=32768, transcendentals=0),
        name="relay",
    )(rows)


def settle_kernel(kv_ref, out_ref):
    pass


def settle(kv, weight):
    return pl.pallas_call(
        settle_kernel,
        out_shape=jax.ShapeDtypeStruct(kv.shape, kv.dtype),
        in_specs=[pl.BlockSpec(memory_space=pl.ANY)],
        out_specs=pl.BlockSpec(memory_space=pl.ANY),
        input_output_aliases={0: 0},
        cost_estimate=pl.CostEstimate(flops=weight, bytes_accessed=0, transcendentals=0),
        name="settle",
    )(kv)


W_RELAY = 10**10
W_SETTLE = 10**10


def sink_total(part):
    z_core = [[x * 32 + i for i in range(Z_CORE)] for x in range(2)]
    x_y = [[dp * 64 + x * 32 + i for dp in range(8) for x in range(2)] for i in range(Z_CORE)]
    near = lax.all_to_all(part, "ctx", 0, 0, axis_index_groups=z_core, tiled=True)
    rows = relay(near, X_Y, W_RELAY)
    far = lax.all_to_all(rows, ("dp", "ctx"), 0, 0, axis_index_groups=x_y, tiled=True)
    return jnp.sum(far, axis=(0, 1))[:Q_HEADS]


def per_device(queries, key_vectors, value_vectors, out_grad, sink_logits, lengths, route_plan):
    slot = lax.axis_index("ctx") // SPAN
    key = lax.dynamic_index_in_dim(route_plan, slot, 0, keepdims=False)
    kv = jnp.concatenate([key_vectors[0], value_vectors[0]], axis=1)
    slots = [[SPAN * s + i for i in range(SPAN)] for s in range(16)]

    def gathered(block):
        return lax.all_gather(block, "ctx", axis_index_groups=slots, tiled=True)

    def branch(bits):
        pairs = [(i, i ^ bits) for i in range(8)]

        def move(queries, kv):
            if bits == 0:
                return queries, gathered(kv)
            moved_queries = lax.ppermute(queries, "dp", pairs)
            moved = lax.ppermute(kv, "dp", pairs)
            return moved_queries, settle(gathered(moved), W_SETTLE)

        return move

    my_queries, kv_window = lax.switch(key, [branch(bits) for bits in range(8)], queries[0], kv)
    out, stat, part = forward(lengths, route_plan, sink_logits, my_queries, out_grad[0], kv_window)
    dq, own, send = backward(lengths, route_plan, my_queries, out_grad[0], kv_window, stat)
    total = own
    for distance in range(1, SPAN):
        pairs = [(SPAN * s + i, SPAN * s + i - distance) for s in range(16) for i in range(distance, SPAN)]
        total = total + lax.ppermute(send[distance - 1], "ctx", pairs).astype(jnp.float32)
    total = total.astype(jnp.bfloat16)
    sink_grad = sink_total(part)
    return (
        out[None],
        dq[None],
        total[:, :KV_COLS][None],
        total[:, KV_COLS:][None],
        sink_grad,
    )


def solution(mesh):
    split = P("dp", "ctx", None)
    return jax.shard_map(
        per_device,
        mesh=mesh,
        in_specs=(split, split, split, split, P(), P(), P()),
        out_specs=(split, split, split, split, P()),
        check_vma=False,
    )
```

time: 94.5 us -> 80.8 us (0.86)
  blocking collectives: 51.4 us -> 25.1 us
  starting transfers between devices: 12.6 us -> 30.8 us
  waiting for transfers between devices: 10.1 us -> 0.43 us
  Pallas kernels: 14.1 us -> 17.2 us
    all_to_all x1 -> x0, blocking collectives: 27.6 us -> none  [sink_total(): lax.all_to_all(part, 'ctx', 0, 0, axis_index_groups=z_core, tiled=True)]
    all_to_all x0 -> x1, starting transfers between devices: none -> 18.9 us  [sink_total(): lax.all_to_all(part, 'ctx', 0, 0, axis_index_groups=z_core, tiled=True)]
    ppermute x1, waiting for transfers between devices: 10.1 us -> 0.41 us  [move(): moved = lax.ppermute(kv, 'dp', pairs)]
    ppermute x1, starting transfers between devices: 6.63 us -> 1.92 us  [move(): moved_queries = lax.ppermute(queries, 'dp', pairs)]
    all_gather x1, blocking collectives: 11.2 us -> 15.4 us  [gathered(): return lax.all_gather(block, 'ctx', axis_index_groups=slots, tiled=True)]
    ppermute x1, starting transfers between devices: 1.92 us -> 5.6 us  [move(): moved = lax.ppermute(kv, 'dp', pairs)]
    pallas_call x1 -> x4, Pallas kernels: 14.1 us -> 17.2 us  [the longest x1 10.6 us: backward(): pl.pallas_call(backward_kernel, out_shape=(jax.ShapeDtypeStruct((rows, wi...]
    all_to_all x1, blocking collectives: 12.6 us -> 9.75 us  [sink_total(): lax.all_to_all(rows, ('dp', 'ctx'), 0, 0, axis_index_groups=x_y, tiled=True)]
  transfers between devices with their start and end apart: 5 -> 6, of which waited for: 1 -> 1; matrix products, arithmetic and copies ran while one was open for 1% -> 1% of each run, Pallas kernels for 0% -> 15%
where the time goes in v2:
time: 80.8 us; the launch traced here: 79.8 us
  starting transfers between devices  30.8 us (38%)
  blocking collectives  25.1 us (31%)
  Pallas kernels  17.2 us (21%)
  local copies, waits for them, and re-layouts  4.14 us (5%)
  between operations  1.46 us (2%)
    all_to_all x1, starting transfers between devices, sink_total(): lax.all_to_all(part, 'ctx', 0, 0, axis_index_groups=z_core, tiled=True)  18.9 us
    all_gather x1, blocking collectives, gathered(): return lax.all_gather(block, 'ctx', axis_index_groups=slots, tiled=True)  15.4 us
    pallas_call x1, Pallas kernels, backward(): pl.pallas_call(backward_kernel, out_shape=(jax.ShapeDtypeStruct((rows, wi...  10.6 us
    all_to_all x1, blocking collectives, sink_total(): lax.all_to_all(rows, ('dp', 'ctx'), 0, 0, axis_index_groups=x_y, tiled=True)  9.75 us
    ppermute x1, starting transfers between devices, move(): moved = lax.ppermute(kv, 'dp', pairs)  5.6 us
    pallas_call x1, Pallas kernels, forward(): pl.pallas_call(forward_kernel, out_shape=(jax.ShapeDtypeStruct((rows, wid...  5.3 us
    ppermute x3, starting transfers between devices, per_device(): lax.ppermute(send[distance - 1], 'ctx', pairs).astype(jnp.float32)  4.28 us
    unnamed x16, local copies, waits for them, and re-layouts  2.83 us
  transfers between devices with their start and end apart: 6, of which 1 were waited for; matrix products, arithmetic and copies ran while one was open for 1% of the time, Pallas kernels for 15%

profile of v2, /device:TPU:1, one launch (start us, length us, event | category | flops | bytes accessed | tf_op | source)
XLA Modules:
  0.0 79.8 jit_solution(626550986114981990)
XLA Ops:
  0.7 0.9 %copy-done.6 = bf16[1,128,256]{2,1,0:T(8,128)(2,1)S(1)} copy-done((bf16[1,128,256]{2,1,0:T(8,128)(2,1)S(1)}, bf16[1,128,256]{2,1,0:T(8,128)(2,1)}, u32[]{:S(2)}) %copy-start.6) | copy-done | bytes 65560
  1.5 0.0 copy-done.5
  1.6 0.0 copy-start.3
  1.6 0.6 copy-done.3
  2.3 0.6 dynamic_slice.4
  3.5 0.0 copy-start
  3.5 23.4 %conditional.1 = (bf16[128,2048]{1,0:T(8,128)(2,1)S(1)}, bf16[512,512]{1,0:T(8,128)(2,1)}) conditional(s32[]{:T(128)} %bitcast, (bf16[128,512]{1,0:T(8,128)(2,1)S(1)}, bf16[128,2048]{1,0:T(8,128)(2,1)S(1)}) %tuple.54, (bf16[128,2048]{1,0:T(8,128)(2,1)S(1)}, bf16[128,512]{1,0:T(8,128)(2,1)S(1)}) %tuple.55, ...), branch_computations={%region_0.1_spmd, %region_1.2_spmd, %region_2.3_spmd, %region_3.4_... | conditional | flops 10000000000 | bytes 4325472 | solution.py:284
  3.6 5.6 %collective-permute-start.5 = (bf16[128,512]{1,0:T(8,128)(2,1)S(1)}, bf16[128,512]{1,0:T(8,128)(2,1)S(1)}, u32[]{:S(2)}, u32[]{:S(2)}) collective-permute-start(bf16[128,512]{1,0:T(8,128)(2,1)S(1)} %get-tuple-element.39), channel_id=1, source_target_pairs={{0,192},{64,128},{128,64},{192,0},{256,448},{320,384},{384,320},{4... | collective-permute-start | bytes 393224 | tf_op jit(solution)/shard_map/cond/branch_3_fun/ppermute | solution.py:279
  9.2 1.9 %collective-permute-start.4 = (bf16[128,2048]{1,0:T(8,128)(2,1)S(1)}, bf16[128,2048]{1,0:T(8,128)(2,1)S(1)}, u32[]{:S(2)}, u32[]{:S(2)}) collective-permute-start(bf16[128,2048]{1,0:T(8,128)(2,1)S(1)} %get-tuple-element.38), channel_id=1, source_target_pairs={{0,192},{64,128},{128,64},{192,0},{256,448},{320,384},{384,320},{4... | collective-permute-start | bytes 1572872 | tf_op jit(solution)/shard_map/cond/branch_3_fun/ppermute | solution.py:278
  11.1 0.4 collective-permute-done.5
  11.5 15.4 %all_gather.19.kv_ref = bf16[512,512]{1,0:T(8,128)(2,1)} all-gather(bf16[128,512]{1,0:T(8,128)(2,1)S(1)} %collective-permute-done.5), channel_id=1, replica_groups={{0,1,2,3},{4,5,6,7},{8,9,10,11},{12,13,14,15},{16,17,18,19},{20,21,22,2..., dimensions={0}, use_global_device_ids=true | all-gather | bytes 655360 | tf_op jit(solution)/shard_map/cond/branch_3_fun/all_gather | solution.py:270
  26.9 0.0 collective-permute-done.4
  26.9 0.0 copy-start.1
  27.0 0.0 copy-start.2
  27.0 0.7 copy-done.1
  27.6 5.3 %forward.1 = (bf16[128,2048]{1,0:T(8,128)(2,1)}, f32[128,128]{1,0:T(8,128)S(1)}, f32[32,1,128]{2,1,0:T(1,128)}) custom-call(s32[8,16]{1,0:T(8,128)S(1)} %copy-done.1, s32[16]{0:T(128)S(1)} %copy-done.3, f32[32]{0:T(128)S(1)} %copy-done.2, bf16[128,2048]{1,0:T(8,128)(2,1)S(1)} %get-tuple-element.61.q_ref, bf16[128,2048]{1,0:T(8,128)(2,1)S(1)} %bitcast.18, ...), custom_call_target="tpu_custom_call" | custom-call | flops 3221225472 | bytes 4194304 | tf_op jit(solution)/shard_map/forward/pallas_call | solution.py:184
  32.9 18.9 %all-to-all-start = ((f32[32,1,128]{2,1,0:T(1,128)}), f32[32,1,128]{2,1,0:T(1,128)S(1)}, u32[]{:S(2)}, u32[]{:S(2)}) async-start(f32[32,1,128]{2,1,0:T(1,128)} %get-tuple-element.68), calls=%async_computation | async-start | bytes 32768 | tf_op jit(solution)/shard_map/all_to_all | solution.py:257
  51.9 10.6 %backward.1 = (bf16[128,2048]{1,0:T(8,128)(2,1)}, f32[128,512]{1,0:T(8,128)S(1)}, bf16[3,128,512]{2,1,0:T(8,128)(2,1)S(1)}) custom-call(s32[8,16]{1,0:T(8,128)S(1)} %copy-done.1, s32[16]{0:T(128)S(1)} %copy-done.3, bf16[128,2048]{1,0:T(8,128)(2,1)S(1)} %get-tuple-element.61.q_ref, bf16[128,2048]{1,0:T(8,128)(2,1)S(1)} %bitcast.19, ...), custom_call_target="tpu_custom_call" | custom-call | flops 6442450944 | bytes 4194304 | tf_op jit(solution)/shard_map/backward/pallas_call | solution.py:202
  62.5 2.3 %collective-permute-start.14 = (bf16[128,512]{1,0:T(8,128)(2,1)S(1)}, bf16[128,512]{1,0:T(8,128)(2,1)S(1)}, u32[]{:S(2)}, u32[]{:S(2)}) collective-permute-start(bf16[128,512]{1,0:T(8,128)(2,1)S(1)} %get-tuple-element.69), channel_id=1, source_target_pairs={{1,0},{2,1},{3,2},{5,4},{6,5},{7,6},{9,8},{10,9},{11,10},{13,12},{... | collective-permute-start | bytes 393224 | tf_op jit(solution)/shard_map/ppermute | solution.py:290
  64.8 0.7 collective-permute-start.16
  65.5 1.3 %collective-permute-start.15 = (bf16[128,512]{1,0:T(8,128)(2,1)S(1)}, bf16[128,512]{1,0:T(8,128)(2,1)S(1)}, u32[]{:S(2)}, u32[]{:S(2)}) collective-permute-start(bf16[128,512]{1,0:T(8,128)(2,1)S(1)} %get-tuple-element.71), channel_id=1, source_target_pairs={{2,0},{3,1},{6,4},{7,5},{10,8},{11,9},{14,12},{15,13},{18,16},{19,... | collective-permute-start | bytes 393224 | tf_op jit(solution)/shard_map/ppermute | solution.py:290
  66.8 0.0 all-to-all-done.rows_ref
  66.8 0.0 copy-start.7
  66.8 0.6 copy-done.7
  67.4 1.4 %relay.1 = f32[16,1,128]{2,1,0:T(1,128)} custom-call(f32[32,1,128]{2,1,0:T(1,128)} %copy-done.7), custom_call_target="tpu_custom_call" | custom-call | flops 10000000000 | bytes 32768 | tf_op jit(solution)/shard_map/relay/pallas_call | solution.py:224
  68.8 9.8 %all_to_all.10 = f32[16,1,128]{2,1,0:T(1,128)S(1)} all-to-all(f32[16,1,128]{2,1,0:T(1,128)} %relay.1), channel_id=1, replica_groups={{0,32,64,96,128,160,192,224,256,288,320,352,384,416,448,480},{1,33,65,9..., dimensions={0} | all-to-all | bytes 16384 | tf_op jit(solution)/shard_map/all_to_all | solution.py:259
  78.5 0.5 reduce_sum.9
  79.1 0.0 collective-permute-done.14
  79.1 0.0 collective-permute-done.16
  79.1 0.0 collective-permute-done.15
  79.1 0.1 add_convert_fusion
  79.2 0.7 slice_bitcast_fusion.3
  (10 shorter events, 0.1 us)
Async XLA Ops:
  0.6 2.9 %copy-start.4 = (bf16[1,128,2048]{2,1,0:T(8,128)(2,1)S(1)}, bf16[1,128,2048]{2,1,0:T(8,128)(2,1)}, u32[]{:S(2)}) copy-start(bf16[1,128,2048]{2,1,0:T(8,128)(2,1)} %param.15) | copy-start | bytes 1572868
  0.6 0.9 %copy-start.6 = (bf16[1,128,256]{2,1,0:T(8,128)(2,1)S(1)}, bf16[1,128,256]{2,1,0:T(8,128)(2,1)}, u32[]{:S(2)}) copy-start(bf16[1,128,256]{2,1,0:T(8,128)(2,1)} %param.16) | copy-start | bytes 196612
  0.7 0.9 %copy-start.5 = (bf16[1,128,256]{2,1,0:T(8,128)(2,1)S(1)}, bf16[1,128,256]{2,1,0:T(8,128)(2,1)}, u32[]{:S(2)}) copy-start(bf16[1,128,256]{2,1,0:T(8,128)(2,1)} %param.17) | copy-start | bytes 196612
  1.6 0.7 copy-start.3
  3.5 23.5 %copy-start = (bf16[1,128,2048]{2,1,0:T(8,128)(2,1)S(1)}, bf16[1,128,2048]{2,1,0:T(8,128)(2,1)}, u32[]{:S(2)}) copy-start(bf16[1,128,2048]{2,1,0:T(8,128)(2,1)} %param.18) | copy-start | bytes 1572868
  3.6 8.0 %collective-permute-start.5 = (bf16[128,512]{1,0:T(8,128)(2,1)S(1)}, bf16[128,512]{1,0:T(8,128)(2,1)S(1)}, u32[]{:S(2)}, u32[]{:S(2)}) collective-permute-start(bf16[128,512]{1,0:T(8,128)(2,1)S(1)} %get-tuple-element.39), channel_id=1, source_target_pairs={{0,192},{64,128},{128,64},{192,0},{256,448},{320,384},{384,320},{4... | collective-permute-start | bytes 393224 | tf_op jit(solution)/shard_map/cond/branch_3_fun/ppermute | solution.py:279
  9.2 17.7 %collective-permute-start.4 = (bf16[128,2048]{1,0:T(8,128)(2,1)S(1)}, bf16[128,2048]{1,0:T(8,128)(2,1)S(1)}, u32[]{:S(2)}, u32[]{:S(2)}) collective-permute-start(bf16[128,2048]{1,0:T(8,128)(2,1)S(1)} %get-tuple-element.38), channel_id=1, source_target_pairs={{0,192},{64,128},{128,64},{192,0},{256,448},{320,384},{384,320},{4... | collective-permute-start | bytes 1572872 | tf_op jit(solution)/shard_map/cond/branch_3_fun/ppermute | solution.py:278
  26.9 0.7 copy-start.1
  27.0 0.7 copy-start.2
  32.9 33.9 %all-to-all-start = ((f32[32,1,128]{2,1,0:T(1,128)}), f32[32,1,128]{2,1,0:T(1,128)S(1)}, u32[]{:S(2)}, u32[]{:S(2)}) async-start(f32[32,1,128]{2,1,0:T(1,128)} %get-tuple-element.68), calls=%async_computation | async-start | bytes 32768 | tf_op jit(solution)/shard_map/all_to_all | solution.py:257
  62.5 16.6 %collective-permute-start.14 = (bf16[128,512]{1,0:T(8,128)(2,1)S(1)}, bf16[128,512]{1,0:T(8,128)(2,1)S(1)}, u32[]{:S(2)}, u32[]{:S(2)}) collective-permute-start(bf16[128,512]{1,0:T(8,128)(2,1)S(1)} %get-tuple-element.69), channel_id=1, source_target_pairs={{1,0},{2,1},{3,2},{5,4},{6,5},{7,6},{9,8},{10,9},{11,10},{13,12},{... | collective-permute-start | bytes 393224 | tf_op jit(solution)/shard_map/ppermute | solution.py:290
  64.8 14.3 %collective-permute-start.16 = (bf16[128,512]{1,0:T(8,128)(2,1)S(1)}, bf16[128,512]{1,0:T(8,128)(2,1)S(1)}, u32[]{:S(2)}, u32[]{:S(2)}) collective-permute-start(bf16[128,512]{1,0:T(8,128)(2,1)S(1)} %get-tuple-element.70), channel_id=1, source_target_pairs={{3,0},{7,4},{11,8},{15,12},{19,16},{23,20},{27,24},{31,28},{35,32}... | collective-permute-start | bytes 393224 | tf_op jit(solution)/shard_map/ppermute | solution.py:290
  65.5 13.6 %collective-permute-start.15 = (bf16[128,512]{1,0:T(8,128)(2,1)S(1)}, bf16[128,512]{1,0:T(8,128)(2,1)S(1)}, u32[]{:S(2)}, u32[]{:S(2)}) collective-permute-start(bf16[128,512]{1,0:T(8,128)(2,1)S(1)} %get-tuple-element.71), channel_id=1, source_target_pairs={{2,0},{3,1},{6,4},{7,5},{10,8},{11,9},{14,12},{15,13},{18,16},{19,... | collective-permute-start | bytes 393224 | tf_op jit(solution)/shard_map/ppermute | solution.py:290
  66.8 0.6 copy-start.7

commit v3 on v2

v3 whole, which is shorter than its diff:
```python
import jax
import jax.numpy as jnp
from jax import lax
from jax.experimental import pallas as pl
from jax.experimental.pallas import tpu as pltpu
from jax.sharding import PartitionSpec as P

D_HEAD = 64
KV_HEADS = 4
HEAD_GROUP = 8
Q_HEADS = KV_HEADS * HEAD_GROUP
SPAN = 4
LANES = 128
KV_COLS = KV_HEADS * D_HEAD
SCALE = D_HEAD**-0.5
TO_LOG2 = SCALE * 1.4426950408889634
MASKED = -1e30
Z_CORE = 32
X_Y = 16
W_PREPARE = 10**10
W_NEAR = 10**10
W_FAR = 10**10

F32, BF16 = jnp.float32, jnp.bfloat16
SMEM = pl.BlockSpec(memory_space=pltpu.SMEM)
VMEM = pl.BlockSpec(memory_space=pltpu.VMEM)
ANY = pl.BlockSpec(memory_space=pl.ANY)


def dot(a, b):
    return jnp.dot(a, b, preferred_element_type=F32)


def dot_nt(a, b):
    return lax.dot_general(a, b, (((1,), (1,)), ((), ())), preferred_element_type=F32)


def struct(shape, dtype):
    return jax.ShapeDtypeStruct(shape, dtype)


def params(mib=16):
    return pltpu.CompilerParams(vmem_limit_bytes=mib * 2**20)


def within_slot():
    return lax.axis_index("ctx") % SPAN


def prepare_kernel(lengths_ref, plan_ref, sink_ref, kv_ref, live_ref, sink8_ref):
    rows = live_ref.shape[0]
    slot = lax.axis_index("ctx") // SPAN
    source = jnp.bitwise_xor(lax.axis_index("dp"), plan_ref[slot])
    length = lengths_ref[source, slot]
    row_pos = lax.broadcasted_iota(jnp.int32, (rows, LANES), 0) + within_slot() * rows
    live_ref[...] = jnp.where(row_pos < length, 1.0, 0.0).astype(F32)
    for head in range(Q_HEADS):
        sink8_ref[head : head + 1, :] = jnp.full((1, LANES), sink_ref[head] / SCALE, F32)


def prepare(lengths, route_plan, sink_logits, kv):
    rows = kv.shape[0] // SPAN
    return pl.pallas_call(
        prepare_kernel,
        grid=(1,),
        out_shape=(struct((rows, LANES), F32), struct((Q_HEADS, LANES), F32)),
        in_specs=[SMEM] * 3 + [pl.BlockSpec((16, LANES), lambda i: (0, 0))],
        out_specs=(
            pl.BlockSpec((rows, LANES), lambda i: (0, 0)),
            pl.BlockSpec((Q_HEADS, LANES), lambda i: (0, 0)),
        ),
        compiler_params=params(1),
        cost_estimate=pl.CostEstimate(flops=W_PREPARE, bytes_accessed=0, transcendentals=0),
        name="prepare",
    )(lengths, route_plan, sink_logits, kv)


def lane_halves(two, half):
    low = lax.broadcasted_iota(jnp.int32, two.shape, 1) < D_HEAD
    zero = jnp.zeros_like(two)
    swapped = jnp.concatenate([two[:, D_HEAD:], two[:, :D_HEAD]], axis=1)
    left, right = (two, swapped) if half == 0 else (swapped, two)
    return jnp.where(low, left, zero), jnp.where(low, zero, right)


def forward_kernel(
    q_ref, do_ref, kv_ref, live_ref, sink8_ref, out_ref, kept_ref, stat_ref, part_ref, terms
):
    rows = q_ref.shape[0]
    window = kv_ref.shape[0]
    query_pos = lax.broadcasted_iota(jnp.int32, (rows, window), 0) + within_slot() * rows
    key_pos = lax.broadcasted_iota(jnp.int32, (rows, window), 1)
    bias = jnp.where(key_pos <= query_pos, 0.0, MASKED).astype(F32)
    wide_low = lax.broadcasted_iota(jnp.int32, (window, LANES), 1) < D_HEAD
    zero = jnp.zeros((window, LANES), BF16)
    one = jnp.ones((window, LANES), BF16)
    ones = (jnp.where(wide_low, one, zero), jnp.where(wide_low, zero, one))
    lane = lax.broadcasted_iota(jnp.int32, (rows, LANES), 1)
    low = lane < D_HEAD
    live = live_ref[...] > 0.5
    terms[...] = jnp.zeros_like(terms)
    stat = jnp.zeros((rows, LANES), F32)
    for group in range(KV_HEADS):
        duo, half = group // 2, group % 2
        keys = lane_halves(kv_ref[:, duo * LANES : (duo + 1) * LANES], half)
        values = lane_halves(kv_ref[:, KV_COLS + duo * LANES : KV_COLS + (duo + 1) * LANES], half)
        values = [jnp.concatenate([values[i], ones[i]], axis=1) for i in range(2)]
        for pair in range(group * 4, group * 4 + 4):
            cols = slice(pair * LANES, (pair + 1) * LANES)
            q2 = q_ref[:, cols]
            sink8 = [sink8_ref[2 * pair + which : 2 * pair + which + 1, :] for which in range(2)]
            sums, maxima = None, []
            for which in range(2):
                scores = dot_nt(q2, keys[which]) + bias
                row_max = sink8[which]
                for block in range(SPAN):
                    row_max = jnp.maximum(row_max, scores[:, block * LANES : (block + 1) * LANES])
                row_max = jnp.max(row_max, axis=1, keepdims=True)
                weights = jnp.exp2((scores - row_max) * TO_LOG2).astype(BF16)
                product = dot(weights, values[which])
                sums = product if sums is None else sums + product
                maxima.append(row_max)
            row_max = jnp.where(low, maxima[0], maxima[1])
            sink_weight = jnp.exp2((jnp.where(low[:1], sink8[0], sink8[1]) - row_max) * TO_LOG2)
            totals = sums[:, LANES:] + sink_weight
            inverse = jnp.where(live, 1.0 / totals, 0.0)
            out = (sums[:, :LANES] * inverse).astype(BF16)
            out_ref[:, cols] = out
            kept_ref[:, cols] = out
            product = do_ref[:, cols].astype(F32) * out.astype(F32)
            term = jnp.sum(-(sink_weight * inverse) * product, axis=0, keepdims=True)
            terms[2 * pair : 2 * pair + 1, :] = jnp.where(low[:1], term, 0.0)
            terms[2 * pair + 1 : 2 * pair + 2, :] = jnp.where(low[:1], 0.0, term)
            log_total = jnp.where(live, row_max * TO_LOG2 + jnp.log2(totals), -MASKED)
            stat = jnp.where((lane == pair) | (lane == D_HEAD + pair), log_total, stat)
    stat_ref[...] = stat.T
    part = jnp.sum(terms[...].T, axis=0, keepdims=True)
    part_ref[...] = jnp.broadcast_to(part, part_ref.shape)


def backward_kernel(
    q_ref, do_ref, out_ref, kv_ref, stat_ref, dq_ref, own_ref, send_ref, acc_k, acc_v, held
):
    rows = q_ref.shape[0]
    window = kv_ref.shape[0]
    within = within_slot()
    key_pos = lax.broadcasted_iota(jnp.int32, (window, rows), 0)
    query_pos = lax.broadcasted_iota(jnp.int32, (window, rows), 1) + within * rows
    bias = jnp.where(key_pos <= query_pos, 0.0, MASKED).astype(F32)
    bias = jnp.concatenate([bias, bias], axis=1)
    low = lax.broadcasted_iota(jnp.int32, (2 * rows, LANES), 1) < D_HEAD
    wide_low = lax.broadcasted_iota(jnp.int32, (window, LANES), 1) < D_HEAD
    zero = jnp.zeros((2 * rows, LANES), BF16)
    side = lax.broadcasted_iota(jnp.int32, (8, LANES), 1) // D_HEAD
    head_lanes = jnp.where(lax.broadcasted_iota(jnp.int32, (8, LANES), 0) == side, 1.0, 0.0).astype(BF16)

    for duo in range(KV_HEADS // 2):
        key_two = kv_ref[:, duo * LANES : (duo + 1) * LANES]
        value_two = kv_ref[:, KV_COLS + duo * LANES : KV_COLS + (duo + 1) * LANES]
        keys_t = key_two.T
        for half in range(2):
            group = 2 * duo + half
            keys = lane_halves(key_two, half)
            values = lane_halves(value_two, half)
            dk = dv = None
            for quad in range(2):
                pair = group * 4 + 2 * quad
                two = [slice(at * LANES, (at + 1) * LANES) for at in (pair, pair + 1)]
                q4 = jnp.concatenate([q_ref[:, cols] for cols in two], axis=0)
                do4 = jnp.concatenate([do_ref[:, cols] for cols in two], axis=0)
                out4 = jnp.concatenate([out_ref[:, cols] for cols in two], axis=0)
                product = do4.astype(F32) * out4.astype(F32)
                rounded = product.astype(BF16)
                rest = (product - rounded.astype(F32)).astype(BF16)
                out_dot = dot_nt(head_lanes, rounded) + dot_nt(head_lanes, rest)
                for which in range(2):
                    at = which * D_HEAD + pair
                    log_total = jnp.concatenate([stat_ref[at : at + 1, :], stat_ref[at + 1 : at + 2, :]], axis=1)
                    scores = dot_nt(keys[which], q4) + bias
                    probs = jnp.exp2(scores * TO_LOG2 - log_total)
                    dprobs = dot_nt(values[which], do4)
                    dscores = (probs * (dprobs - out_dot[which : which + 1])).astype(BF16)
                    own_q = jnp.where(low, q4, zero) if which == 0 else jnp.where(low, zero, q4)
                    own_do = jnp.where(low, do4, zero) if which == 0 else jnp.where(low, zero, do4)
                    dk_part = dot(dscores, own_q)
                    dv_part = dot(probs.astype(BF16), own_do)
                    dk = dk_part if dk is None else dk + dk_part
                    dv = dv_part if dv is None else dv + dv_part
                    at = (2 * quad + which) * 2 * rows
                    held[:, at : at + 2 * rows] = dscores
            dq_t = dot(keys_t[half * D_HEAD : (half + 1) * D_HEAD], held[...]) * SCALE
            for quad in range(2):
                at = 4 * quad * rows
                both = jnp.concatenate(
                    [dq_t[:, at : at + 2 * rows], dq_t[:, at + 2 * rows : at + 4 * rows]], axis=0
                ).astype(BF16)
                pair = group * 4 + 2 * quad
                dq_ref[:, pair * LANES : (pair + 1) * LANES] = both[:, :rows].T
                dq_ref[:, (pair + 1) * LANES : (pair + 2) * LANES] = both[:, rows:].T
            acc_k[half] = dk
            acc_v[half] = dv
        for which, acc, factor in ((0, acc_k, SCALE), (1, acc_v, None)):
            even = acc[0] + pltpu.roll(acc[0], D_HEAD, 1)
            odd = acc[1] + pltpu.roll(acc[1], D_HEAD, 1)
            total = jnp.where(wide_low, even, odd)
            acc[0] = total if factor is None else total * factor
            at = slice(which * KV_COLS + duo * LANES, which * KV_COLS + (duo + 1) * LANES)
            own_ref[:, at] = acc[0, pl.ds(pl.multiple_of(within * rows, rows), rows), :]
            for distance in range(1, SPAN):
                block = jnp.maximum(within - distance, 0)
                send_ref[distance - 1, :, at] = acc[
                    0, pl.ds(pl.multiple_of(block * rows, rows), rows), :
                ].astype(BF16)


def estimate(products, rows):
    return pl.CostEstimate(
        flops=products * 2 * Q_HEADS * rows * SPAN * rows * D_HEAD * 4,
        bytes_accessed=4 * 2**20,
        transcendentals=Q_HEADS * rows * SPAN * rows,
    )


def forward(queries, out_grad, kv, live, sink8):
    rows, width = queries.shape
    return pl.pallas_call(
        forward_kernel,
        out_shape=(
            struct((rows, width), BF16),
            struct((rows, width), BF16),
            struct((LANES, rows), F32),
            struct((Z_CORE, LANES), F32),
        ),
        in_specs=[VMEM] * 5,
        out_specs=(VMEM,) * 4,
        scratch_shapes=[pltpu.VMEM((LANES, LANES), F32)],
        compiler_params=params(),
        cost_estimate=estimate(3, rows),
        name="forward",
    )(queries, out_grad, kv, live, sink8)


def backward(queries, out_grad, out, kv, stat):
    rows, width = queries.shape
    window = kv.shape[0]
    return pl.pallas_call(
        backward_kernel,
        out_shape=(
            struct((rows, width), BF16),
            struct((rows, 2 * KV_COLS), F32),
            struct((SPAN - 1, rows, 2 * KV_COLS), BF16),
        ),
        in_specs=[VMEM] * 5,
        out_specs=(VMEM,) * 3,
        scratch_shapes=[pltpu.VMEM((2, window, LANES), F32)] * 2
        + [pltpu.VMEM((window, HEAD_GROUP * rows), BF16)],
        compiler_params=params(),
        cost_estimate=estimate(6, rows),
        name="backward",
    )(queries, out_grad, out, kv, stat)


def relay_kernel(rows_ref, out_ref):
    out_ref[...] = jnp.broadcast_to(jnp.sum(rows_ref[...], axis=0, keepdims=True), out_ref.shape)


def relay(rows, copies):
    return pl.pallas_call(
        relay_kernel,
        out_shape=struct((copies, LANES), F32),
        in_specs=[VMEM],
        out_specs=VMEM,
        cost_estimate=pl.CostEstimate(flops=W_NEAR, bytes_accessed=32768, transcendentals=0),
        compiler_params=params(1),
        name="relay",
    )(rows)


def finish_kernel(rows_ref, out_ref):
    out_ref[...] = jnp.sum(rows_ref[...], axis=0)[:Q_HEADS]


def finish(rows):
    return pl.pallas_call(
        finish_kernel,
        out_shape=struct((Q_HEADS,), F32),
        in_specs=[VMEM],
        out_specs=VMEM,
        cost_estimate=pl.CostEstimate(flops=W_FAR, bytes_accessed=32768, transcendentals=0),
        compiler_params=params(1),
        name="finish",
    )(rows)


def sink_total(part):
    z_core = [[x * 32 + i for i in range(Z_CORE)] for x in range(2)]
    x_y = [[dp * 64 + x * 32 + i for dp in range(8) for x in range(2)] for i in range(Z_CORE)]

    def exchange(rows, axis, groups):
        rows = rows[:, None, :]
        return lax.all_to_all(rows, axis, 0, 0, axis_index_groups=groups, tiled=True)[:, 0, :]

    near = exchange(part, "ctx", z_core)
    far = exchange(relay(near, X_Y), ("dp", "ctx"), x_y)
    return finish(far)


def grads_kernel(own_ref, first_ref, second_ref, third_ref, key_ref, value_ref):
    total = own_ref[...]
    for ref in (first_ref, second_ref, third_ref):
        total = total + ref[...].astype(F32)
    total = total.astype(BF16)
    key_ref[...] = total[:, :KV_COLS]
    value_ref[...] = total[:, KV_COLS:]


def grads(own, received):
    shape = struct((own.shape[0], KV_COLS), BF16)
    return pl.pallas_call(
        grads_kernel,
        out_shape=(shape, shape),
        in_specs=[VMEM] * SPAN,
        out_specs=(VMEM, VMEM),
        compiler_params=params(2),
        name="grads",
    )(own, *received)


def per_device(queries, key_vectors, value_vectors, out_grad, sink_logits, lengths, route_plan):
    slot = lax.axis_index("ctx") // SPAN
    key = lax.dynamic_index_in_dim(route_plan, slot, 0, keepdims=False)
    kv = jnp.concatenate([key_vectors[0], value_vectors[0]], axis=1)
    slots = [[SPAN * s + i for i in range(SPAN)] for s in range(16)]

    def branch(bits):
        pairs = [(i, i ^ bits) for i in range(8)]

        def move(queries, kv):
            moved_queries = queries
            if bits:
                moved_queries = lax.ppermute(queries, "dp", pairs)
                kv = lax.ppermute(kv, "dp", pairs)
            window = lax.all_gather(kv, "ctx", axis_index_groups=slots, tiled=True)
            return moved_queries, window, *prepare(lengths, route_plan, sink_logits, window)

        return move

    my_queries, window, live, sink8 = lax.switch(key, [branch(bits) for bits in range(8)], queries[0], kv)
    out, kept, stat, part = forward(my_queries, out_grad[0], window, live, sink8)
    dq, own, send = backward(my_queries, out_grad[0], kept, window, stat)
    received = []
    for distance in range(1, SPAN):
        pairs = [(SPAN * s + i, SPAN * s + i - distance) for s in range(16) for i in range(distance, SPAN)]
        received.append(lax.ppermute(send[distance - 1], "ctx", pairs))
    key_grad, value_grad = grads(own, received)
    return out[None], dq[None], key_grad[None], value_grad[None], sink_total(part)


def solution(mesh):
    split = P("dp", "ctx", None)
    return jax.shard_map(
        per_device,
        mesh=mesh,
        in_specs=(split, split, split, split, P(), P(), P()),
        out_specs=(split, split, split, split, P()),
        check_vma=False,
    )
```

time: 80.8 us -> 80.2 us (level)
  waiting for transfers between devices: 0.43 us -> 10.5 us
  blocking collectives: 25.1 us -> 15.2 us
  starting transfers between devices: 30.8 us -> 35.6 us
  Pallas kernels: 17.2 us -> 14.5 us
  local copies, waits for them, and re-layouts: 4.14 us -> 2.34 us
    all_to_all x1 -> x0, blocking collectives: 9.75 us -> none  [sink_total(): lax.all_to_all(rows, ('dp', 'ctx'), 0, 0, axis_index_groups=x_y, tiled=True)]
    all_to_all x1 -> x2, waiting for transfers between devices: 0.01 us -> 6.15 us  [exchange(): lax.all_to_all(rows, axis, 0, 0, axis_index_groups=groups, tiled=True)]
    ppermute x4, waiting for transfers between devices: 0.42 us -> 4.37 us  [the longest x3 3.95 us: per_device(): received.append(lax.ppermute(send[distance - 1], 'ctx', pairs))]
    all_to_all x1 -> x2, starting transfers between devices: 18.9 us -> 22.7 us  [exchange(): lax.all_to_all(rows, axis, 0, 0, axis_index_groups=groups, tiled=True)]
    pallas_call x4 -> x6, Pallas kernels: 17.2 us -> 14.5 us  [the longest x1 6.37 us: backward(): pl.pallas_call(backward_kernel, out_shape=(struct((rows, width), BF16), s...]
    unnamed x16, local copies, waits for them, and re-layouts: 2.83 us -> 1.56 us
    ppermute x4, starting transfers between devices: 9.89 us -> 11 us  [the longest x1 5.61 us: move(): kv = lax.ppermute(kv, 'dp', pairs)]
  transfers between devices with their start and end apart: 6 -> 7, of which waited for: 1 -> 5; matrix products, arithmetic and copies ran while one was open for 1% -> 0% of each run, Pallas kernels for 15% -> 9%
where the time goes in v3:
time: 80.2 us; the launch traced here: 79.8 us
  starting transfers between devices  35.6 us (44%)
  blocking collectives  15.2 us (19%)
  Pallas kernels  14.5 us (18%)
  waiting for transfers between devices  10.5 us (13%)
  local copies, waits for them, and re-layouts  2.34 us (3%)
  between operations  1.49 us (2%)
    all_to_all x2, starting transfers between devices, exchange(): lax.all_to_all(rows, axis, 0, 0, axis_index_groups=groups, tiled=True)  22.7 us
    all_gather x1, blocking collectives, move(): window = lax.all_gather(kv, 'ctx', axis_index_groups=slots, tiled=True)  15.2 us
    pallas_call x1, Pallas kernels, backward(): pl.pallas_call(backward_kernel, out_shape=(struct((rows, width), BF16), s...  6.37 us
    all_to_all x2, waiting for transfers between devices, exchange(): lax.all_to_all(rows, axis, 0, 0, axis_index_groups=groups, tiled=True)  6.15 us
    pallas_call x1, Pallas kernels, forward(): pl.pallas_call(forward_kernel, out_shape=(struct((rows, width), BF16), st...  5.71 us
    ppermute x1, starting transfers between devices, move(): kv = lax.ppermute(kv, 'dp', pairs)  5.61 us
    ppermute x3, starting transfers between devices, per_device(): received.append(lax.ppermute(send[distance - 1], 'ctx', pairs))  5.4 us
    ppermute x3, waiting for transfers between devices, per_device(): received.append(lax.ppermute(send[distance - 1], 'ctx', pairs))  3.95 us
  transfers between devices with their start and end apart: 7, of which 5 were waited for; matrix products, arithmetic and copies ran while one was open for 0% of the time, Pallas kernels for 9%

profile of v3, /device:TPU:1, one launch (start us, length us, event | category | flops | bytes accessed | tf_op | source)
XLA Modules:
  0.0 79.8 jit_solution(2234575275368283069)
XLA Ops:
  0.7 0.9 %copy-done.12 = bf16[1,128,256]{2,1,0:T(8,128)(2,1)S(1)} copy-done((bf16[1,128,256]{2,1,0:T(8,128)(2,1)S(1)}, bf16[1,128,256]{2,1,0:T(8,128)(2,1)}, u32[]{:S(2)}) %copy-start.12) | copy-done | bytes 65560
  1.5 0.0 copy-done.11
  1.6 0.0 copy-start.14
  1.6 0.0 copy-start.13
  1.6 0.6 copy-done.14
  2.2 0.6 dynamic_slice.4
  3.5 0.0 copy-done.10
  3.5 0.0 copy-start
  3.5 24.1 %conditional.1 = (bf16[128,2048]{1,0:T(8,128)(2,1)S(1)}, bf16[512,512]{1,0:T(8,128)(2,1)}, f32[128,128]{1,0:T(8,128)S(1)}, f32[32,128]{1,0:T(8,128)S(1)}) conditional(s32[]{:T(128)} %bitcast, (bf16[128,512]{1,0:T(8,128)(2,1)S(1)}, s32[8,16]{1,0:T(8,128)S(1)}, s32[16]{0:T(128)S(1)}, f32[32]{0:T(128)S(1)}, ...), branch_computations={%region_0.1_spmd, %region_1.2_spmd, %region_2.3_spmd, %region_3.4_... | conditional | flops 10000000000 | bytes 6422668 | solution.py:348
  3.6 5.6 %collective-permute-start.7 = (bf16[128,512]{1,0:T(8,128)(2,1)S(1)}, bf16[128,512]{1,0:T(8,128)(2,1)S(1)}, u32[]{:S(2)}, u32[]{:S(2)}) collective-permute-start(bf16[128,512]{1,0:T(8,128)(2,1)S(1)} %get-tuple-element.109), channel_id=1, source_target_pairs={{0,256},{64,320},{128,384},{192,448},{256,0},{320,64},{384,128},{4... | collective-permute-start | bytes 393224 | tf_op jit(solution)/shard_map/cond/branch_4_fun/ppermute | solution.py:342
  9.2 1.9 %collective-permute-start.6 = (bf16[128,2048]{1,0:T(8,128)(2,1)S(1)}, bf16[128,2048]{1,0:T(8,128)(2,1)S(1)}, u32[]{:S(2)}, u32[]{:S(2)}) collective-permute-start(bf16[128,2048]{1,0:T(8,128)(2,1)S(1)} %get-tuple-element.108), channel_id=1, source_target_pairs={{0,256},{64,320},{128,384},{192,448},{256,0},{320,64},{384,128},{4... | collective-permute-start | bytes 1572872 | tf_op jit(solution)/shard_map/cond/branch_4_fun/ppermute | solution.py:341
  11.1 0.4 collective-permute-done.7
  11.5 15.2 %all_gather.20.kv_ref = bf16[512,512]{1,0:T(8,128)(2,1)S(1)} all-gather(bf16[128,512]{1,0:T(8,128)(2,1)S(1)} %collective-permute-done.7), channel_id=1, replica_groups={{0,1,2,3},{4,5,6,7},{8,9,10,11},{12,13,14,15},{16,17,18,19},{20,21,22,2..., dimensions={0}, use_global_device_ids=true | all-gather | bytes 655360 | tf_op jit(solution)/shard_map/cond/branch_4_fun/all_gather | solution.py:343
  26.8 0.6 prepare.12
  27.4 0.1 copy-done.5
  27.5 0.0 collective-permute-done.6
  27.6 0.0 copy-start.9
  27.6 5.7 %forward.1 = (bf16[128,2048]{1,0:T(8,128)(2,1)}, bf16[128,2048]{1,0:T(8,128)(2,1)S(1)}, f32[128,128]{1,0:T(8,128)S(1)}, f32[32,128]{1,0:T(8,128)}) custom-call(bf16[128,2048]{1,0:T(8,128)(2,1)S(1)} %get-tuple-element.154.q_ref, bf16[128,2048]{1,0:T(8,128)(2,1)S(1)} %bitcast.25, bf16[512,512]{1,0:T(8,128)(2,1)} %get-tuple-element.155.kv_ref, ...), custom_call_target="tpu_custom_call" | custom-call | flops 3221225472 | bytes 4194304 | tf_op jit(solution)/shard_map/forward/pallas_call | solution.py:226
  33.3 19.2 %all-to-all-start = ((f32[32,1,128]{2,1,0:T(1,128)}), f32[32,1,128]{2,1,0:T(1,128)S(1)}, u32[]{:S(2)}, u32[]{:S(2)}) async-start(f32[32,1,128]{2,1,0:T(1,128)} %bitcast.13), calls=%async_computation | async-start | bytes 32768 | tf_op jit(solution)/shard_map/all_to_all | solution.py:301
  52.5 6.4 %backward.1 = (bf16[128,2048]{1,0:T(8,128)(2,1)}, f32[128,512]{1,0:T(8,128)S(1)}, bf16[3,128,512]{2,1,0:T(8,128)(2,1)S(1)}) custom-call(bf16[128,2048]{1,0:T(8,128)(2,1)S(1)} %get-tuple-element.154.q_ref, bf16[128,2048]{1,0:T(8,128)(2,1)S(1)} %bitcast.26, bf16[128,2048]{1,0:T(8,128)(2,1)S(1)} %get-tuple-element.159.out_ref, bf16[512,512]{1,0:T(8,128)(2,1)S(1)} %copy-done.9, ...), custom_call_target="tpu_custom_call" | custom-call | flops 6442450944 | bytes 4194304 | tf_op jit(solution)/shard_map/backward/pallas_call | solution.py:246
  58.9 5.3 %all-to-all-done = f32[32,1,128]{2,1,0:T(1,128)S(1)} async-done(((f32[32,1,128]{2,1,0:T(1,128)}), f32[32,1,128]{2,1,0:T(1,128)S(1)}, u32[]{:S(2)}, u32[]{:S(2)}) %all-to-all-start) | async-done | bytes 16416 | tf_op jit(solution)/shard_map/all_to_all | solution.py:301
  64.2 0.6 relay.1
  64.9 3.5 %all-to-all-start.1 = ((f32[16,1,128]{2,1,0:T(1,128)}), f32[16,1,128]{2,1,0:T(1,128)S(1)}, u32[]{:S(2)}, u32[]{:S(2)}) async-start(f32[16,1,128]{2,1,0:T(1,128)} %bitcast.16), calls=%async_computation.1 | async-start | bytes 16384 | tf_op jit(solution)/shard_map/all_to_all | solution.py:301
  68.4 0.7 collective-permute-start.16
  69.0 1.3 %collective-permute-start.15 = (bf16[128,512]{1,0:T(8,128)(2,1)S(1)}, bf16[128,512]{1,0:T(8,128)(2,1)S(1)}, u32[]{:S(2)}, u32[]{:S(2)}) collective-permute-start(bf16[128,512]{1,0:T(8,128)(2,1)S(1)} %get-tuple-element.168), channel_id=1, source_target_pairs={{2,0},{3,1},{6,4},{7,5},{10,8},{11,9},{14,12},{15,13},{18,16},{19,... | collective-permute-start | bytes 393224 | tf_op jit(solution)/shard_map/ppermute | solution.py:354
  70.3 3.4 %collective-permute-start.14 = (bf16[128,512]{1,0:T(8,128)(2,1)S(1)}, bf16[128,512]{1,0:T(8,128)(2,1)S(1)}, u32[]{:S(2)}, u32[]{:S(2)}) collective-permute-start(bf16[128,512]{1,0:T(8,128)(2,1)S(1)} %get-tuple-element.169), channel_id=1, source_target_pairs={{1,0},{2,1},{3,2},{5,4},{6,5},{7,6},{9,8},{10,9},{11,10},{13,12},{... | collective-permute-start | bytes 393224 | tf_op jit(solution)/shard_map/ppermute | solution.py:354
  73.8 0.8 %all-to-all-done.1 = f32[16,1,128]{2,1,0:T(1,128)S(1)} async-done(((f32[16,1,128]{2,1,0:T(1,128)}), f32[16,1,128]{2,1,0:T(1,128)S(1)}, u32[]{:S(2)}, u32[]{:S(2)}) %all-to-all-start.1) | async-done | bytes 8224 | tf_op jit(solution)/shard_map/all_to_all | solution.py:301
  74.6 0.5 finish.1
  75.1 0.0 collective-permute-done.16.third_ref
  75.1 2.3 %collective-permute-done.15.second_ref = bf16[128,512]{1,0:T(8,128)(2,1)S(1)} collective-permute-done((bf16[128,512]{1,0:T(8,128)(2,1)S(1)}, bf16[128,512]{1,0:T(8,128)(2,1)S(1)}, u32[]{:S(2)}, u32[]{:S(2)}) %collective-permute-start.15) | collective-permute-done | bytes 131104 | tf_op jit(solution)/shard_map/ppermute | solution.py:354
  77.4 1.6 %collective-permute-done.14.first_ref = bf16[128,512]{1,0:T(8,128)(2,1)S(1)} collective-permute-done((bf16[128,512]{1,0:T(8,128)(2,1)S(1)}, bf16[128,512]{1,0:T(8,128)(2,1)S(1)}, u32[]{:S(2)}, u32[]{:S(2)}) %collective-permute-start.14) | collective-permute-done | bytes 131104 | tf_op jit(solution)/shard_map/ppermute | solution.py:354
  79.1 0.7 grads.1
  (12 shorter events, 0.1 us)
Async XLA Ops:
  0.6 2.9 %copy-start.10 = (bf16[1,128,2048]{2,1,0:T(8,128)(2,1)S(1)}, bf16[1,128,2048]{2,1,0:T(8,128)(2,1)}, u32[]{:S(2)}) copy-start(bf16[1,128,2048]{2,1,0:T(8,128)(2,1)} %param.15) | copy-start | bytes 1572868
  0.6 0.9 %copy-start.12 = (bf16[1,128,256]{2,1,0:T(8,128)(2,1)S(1)}, bf16[1,128,256]{2,1,0:T(8,128)(2,1)}, u32[]{:S(2)}) copy-start(bf16[1,128,256]{2,1,0:T(8,128)(2,1)} %param.16) | copy-start | bytes 196612
  0.7 0.9 %copy-start.11 = (bf16[1,128,256]{2,1,0:T(8,128)(2,1)S(1)}, bf16[1,128,256]{2,1,0:T(8,128)(2,1)}, u32[]{:S(2)}) copy-start(bf16[1,128,256]{2,1,0:T(8,128)(2,1)} %param.17) | copy-start | bytes 196612
  1.6 0.7 copy-start.14
  1.6 1.9 %copy-start.13 = (s32[8,16]{1,0:T(8,128)S(1)}, s32[8,16]{1,0:T(8,128)}, u32[]{:S(2)}) copy-start(s32[8,16]{1,0:T(8,128)} %param.20) | copy-start | bytes 1540
  2.8 0.7 copy-start.15
  3.5 24.1 %copy-start = (bf16[1,128,2048]{2,1,0:T(8,128)(2,1)S(1)}, bf16[1,128,2048]{2,1,0:T(8,128)(2,1)}, u32[]{:S(2)}) copy-start(bf16[1,128,2048]{2,1,0:T(8,128)(2,1)} %param.18) | copy-start | bytes 1572868
  3.6 8.0 %collective-permute-start.7 = (bf16[128,512]{1,0:T(8,128)(2,1)S(1)}, bf16[128,512]{1,0:T(8,128)(2,1)S(1)}, u32[]{:S(2)}, u32[]{:S(2)}) collective-permute-start(bf16[128,512]{1,0:T(8,128)(2,1)S(1)} %get-tuple-element.109), channel_id=1, source_target_pairs={{0,256},{64,320},{128,384},{192,448},{256,0},{320,64},{384,128},{4... | collective-permute-start | bytes 393224 | tf_op jit(solution)/shard_map/cond/branch_4_fun/ppermute | solution.py:342
  9.2 18.4 %collective-permute-start.6 = (bf16[128,2048]{1,0:T(8,128)(2,1)S(1)}, bf16[128,2048]{1,0:T(8,128)(2,1)S(1)}, u32[]{:S(2)}, u32[]{:S(2)}) collective-permute-start(bf16[128,2048]{1,0:T(8,128)(2,1)S(1)} %get-tuple-element.108), channel_id=1, source_target_pairs={{0,256},{64,320},{128,384},{192,448},{256,0},{320,64},{384,128},{4... | collective-permute-start | bytes 1572872 | tf_op jit(solution)/shard_map/cond/branch_4_fun/ppermute | solution.py:341
  26.7 0.8 copy-start.5
  27.6 24.9 %copy-start.9 = (bf16[512,512]{1,0:T(8,128)(2,1)S(1)}, bf16[512,512]{1,0:T(8,128)(2,1)}, u32[]{:S(2)}) copy-start(bf16[512,512]{1,0:T(8,128)(2,1)} %get-tuple-element.155.kv_ref) | copy-start | bytes 1572868
  33.3 30.9 %all-to-all-start = ((f32[32,1,128]{2,1,0:T(1,128)}), f32[32,1,128]{2,1,0:T(1,128)S(1)}, u32[]{:S(2)}, u32[]{:S(2)}) async-start(f32[32,1,128]{2,1,0:T(1,128)} %bitcast.13), calls=%async_computation | async-start | bytes 32768 | tf_op jit(solution)/shard_map/all_to_all | solution.py:301
  64.9 9.8 %all-to-all-start.1 = ((f32[16,1,128]{2,1,0:T(1,128)}), f32[16,1,128]{2,1,0:T(1,128)S(1)}, u32[]{:S(2)}, u32[]{:S(2)}) async-start(f32[16,1,128]{2,1,0:T(1,128)} %bitcast.16), calls=%async_computation.1 | async-start | bytes 16384 | tf_op jit(solution)/shard_map/all_to_all | solution.py:301
  68.4 6.8 %collective-permute-start.16 = (bf16[128,512]{1,0:T(8,128)(2,1)S(1)}, bf16[128,512]{1,0:T(8,128)(2,1)S(1)}, u32[]{:S(2)}, u32[]{:S(2)}) collective-permute-start(bf16[128,512]{1,0:T(8,128)(2,1)S(1)} %get-tuple-element.167), channel_id=1, source_target_pairs={{3,0},{7,4},{11,8},{15,12},{19,16},{23,20},{27,24},{31,28},{35,32}... | collective-permute-start | bytes 393224 | tf_op jit(solution)/shard_map/ppermute | solution.py:354
  69.0 8.4 %collective-permute-start.15 = (bf16[128,512]{1,0:T(8,128)(2,1)S(1)}, bf16[128,512]{1,0:T(8,128)(2,1)S(1)}, u32[]{:S(2)}, u32[]{:S(2)}) collective-permute-start(bf16[128,512]{1,0:T(8,128)(2,1)S(1)} %get-tuple-element.168), channel_id=1, source_target_pairs={{2,0},{3,1},{6,4},{7,5},{10,8},{11,9},{14,12},{15,13},{18,16},{19,... | collective-permute-start | bytes 393224 | tf_op jit(solution)/shard_map/ppermute | solution.py:354
  70.3 8.7 %collective-permute-start.14 = (bf16[128,512]{1,0:T(8,128)(2,1)S(1)}, bf16[128,512]{1,0:T(8,128)(2,1)S(1)}, u32[]{:S(2)}, u32[]{:S(2)}) collective-permute-start(bf16[128,512]{1,0:T(8,128)(2,1)S(1)} %get-tuple-element.169), channel_id=1, source_target_pairs={{1,0},{2,1},{3,2},{5,4},{6,5},{7,6},{9,8},{10,9},{11,10},{13,12},{... | collective-permute-start | bytes 393224 | tf_op jit(solution)/shard_map/ppermute | solution.py:354

commit v4 on v3

--- a/solution.py
+++ b/solution.py
@@ -19,7 +19,6 @@
 X_Y = 16
 W_PREPARE = 10**10
 W_NEAR = 10**10
-W_FAR = 10**10
 
 F32, BF16 = jnp.float32, jnp.bfloat16
 SMEM = pl.BlockSpec(memory_space=pltpu.SMEM)
@@ -47,29 +46,44 @@
     return lax.axis_index("ctx") % SPAN
 
 
-def prepare_kernel(lengths_ref, plan_ref, sink_ref, kv_ref, live_ref, sink8_ref):
+def head_kernel(plan_ref, k_ref, v_ref, key_ref, kv_ref):
+    key_ref[0] = plan_ref[lax.axis_index("ctx") // SPAN]
+    kv_ref[:, :KV_COLS] = k_ref[...]
+    kv_ref[:, KV_COLS:] = v_ref[...]
+
+
+def head(route_plan, keys, values):
+    rows = keys.shape[0]
+    return pl.pallas_call(
+        head_kernel,
+        out_shape=(struct((1,), jnp.int32), struct((rows, 2 * KV_COLS), BF16)),
+        in_specs=[SMEM, VMEM, VMEM],
+        out_specs=(SMEM, VMEM),
+        compiler_params=params(2),
+        name="head",
+    )(route_plan, keys, values)
+
+
+def prepare_kernel(lengths_ref, plan_ref, sink_ref, kv_ref, copy_ref, live_ref, sink8_ref):
     rows = live_ref.shape[0]
     slot = lax.axis_index("ctx") // SPAN
     source = jnp.bitwise_xor(lax.axis_index("dp"), plan_ref[slot])
     length = lengths_ref[source, slot]
     row_pos = lax.broadcasted_iota(jnp.int32, (rows, LANES), 0) + within_slot() * rows
     live_ref[...] = jnp.where(row_pos < length, 1.0, 0.0).astype(F32)
-    for head in range(Q_HEADS):
-        sink8_ref[head : head + 1, :] = jnp.full((1, LANES), sink_ref[head] / SCALE, F32)
+    for head_at in range(Q_HEADS):
+        sink8_ref[head_at : head_at + 1, :] = jnp.full((1, LANES), sink_ref[head_at] / SCALE, F32)
+    copy_ref[...] = kv_ref[...]
 
 
 def prepare(lengths, route_plan, sink_logits, kv):
     rows = kv.shape[0] // SPAN
     return pl.pallas_call(
         prepare_kernel,
-        grid=(1,),
-        out_shape=(struct((rows, LANES), F32), struct((Q_HEADS, LANES), F32)),
-        in_specs=[SMEM] * 3 + [pl.BlockSpec((16, LANES), lambda i: (0, 0))],
-        out_specs=(
-            pl.BlockSpec((rows, LANES), lambda i: (0, 0)),
-            pl.BlockSpec((Q_HEADS, LANES), lambda i: (0, 0)),
-        ),
-        compiler_params=params(1),
+        out_shape=(struct(kv.shape, BF16), struct((rows, LANES), F32), struct((Q_HEADS, LANES), F32)),
+        in_specs=[SMEM] * 3 + [VMEM],
+        out_specs=(VMEM,) * 3,
+        compiler_params=params(4),
         cost_estimate=pl.CostEstimate(flops=W_PREPARE, bytes_accessed=0, transcendentals=0),
         name="prepare",
     )(lengths, route_plan, sink_logits, kv)
@@ -84,7 +98,7 @@
 
 
 def forward_kernel(
-    q_ref, do_ref, kv_ref, live_ref, sink8_ref, out_ref, kept_ref, stat_ref, part_ref, terms
+    q_ref, do_ref, kv_ref, live_ref, sink8_ref, kept_ref, stat_ref, part_ref, terms
 ):
     rows = q_ref.shape[0]
     window = kv_ref.shape[0]
@@ -125,7 +139,6 @@
             totals = sums[:, LANES:] + sink_weight
             inverse = jnp.where(live, 1.0 / totals, 0.0)
             out = (sums[:, :LANES] * inverse).astype(BF16)
-            out_ref[:, cols] = out
             kept_ref[:, cols] = out
             product = do_ref[:, cols].astype(F32) * out.astype(F32)
             term = jnp.sum(-(sink_weight * inverse) * product, axis=0, keepdims=True)
@@ -139,7 +152,7 @@
 
 
 def backward_kernel(
-    q_ref, do_ref, out_ref, kv_ref, stat_ref, dq_ref, own_ref, send_ref, acc_k, acc_v, held
+    q_ref, do_ref, kept_ref, kv_ref, stat_ref, out_ref, dq_ref, own_ref, send_ref, acc_k, acc_v, held
 ):
     rows = q_ref.shape[0]
     window = kv_ref.shape[0]
@@ -168,7 +181,9 @@
                 two = [slice(at * LANES, (at + 1) * LANES) for at in (pair, pair + 1)]
                 q4 = jnp.concatenate([q_ref[:, cols] for cols in two], axis=0)
                 do4 = jnp.concatenate([do_ref[:, cols] for cols in two], axis=0)
-                out4 = jnp.concatenate([out_ref[:, cols] for cols in two], axis=0)
+                out4 = jnp.concatenate([kept_ref[:, cols] for cols in two], axis=0)
+                for at, cols in enumerate(two):
+                    out_ref[:, cols] = out4[at * rows : (at + 1) * rows]
                 product = do4.astype(F32) * out4.astype(F32)
                 rounded = product.astype(BF16)
                 rest = (product - rounded.astype(F32)).astype(BF16)
@@ -227,12 +242,11 @@
         forward_kernel,
         out_shape=(
             struct((rows, width), BF16),
-            struct((rows, width), BF16),
             struct((LANES, rows), F32),
             struct((Z_CORE, LANES), F32),
         ),
         in_specs=[VMEM] * 5,
-        out_specs=(VMEM,) * 4,
+        out_specs=(VMEM,) * 3,
         scratch_shapes=[pltpu.VMEM((LANES, LANES), F32)],
         compiler_params=params(),
         cost_estimate=estimate(3, rows),
@@ -247,11 +261,12 @@
         backward_kernel,
         out_shape=(
             struct((rows, width), BF16),
+            struct((rows, width), BF16),
             struct((rows, 2 * KV_COLS), F32),
             struct((SPAN - 1, rows, 2 * KV_COLS), BF16),
         ),
         in_specs=[VMEM] * 5,
-        out_specs=(VMEM,) * 3,
+        out_specs=(VMEM,) * 4,
         scratch_shapes=[pltpu.VMEM((2, window, LANES), F32)] * 2
         + [pltpu.VMEM((window, HEAD_GROUP * rows), BF16)],
         compiler_params=params(),
@@ -286,7 +301,7 @@
         out_shape=struct((Q_HEADS,), F32),
         in_specs=[VMEM],
         out_specs=VMEM,
-        cost_estimate=pl.CostEstimate(flops=W_FAR, bytes_accessed=32768, transcendentals=0),
+        cost_estimate=pl.CostEstimate(flops=1024, bytes_accessed=32768, transcendentals=0),
         compiler_params=params(1),
         name="finish",
     )(rows)
@@ -327,9 +342,7 @@
 
 
 def per_device(queries, key_vectors, value_vectors, out_grad, sink_logits, lengths, route_plan):
-    slot = lax.axis_index("ctx") // SPAN
-    key = lax.dynamic_index_in_dim(route_plan, slot, 0, keepdims=False)
-    kv = jnp.concatenate([key_vectors[0], value_vectors[0]], axis=1)
+    key, kv = head(route_plan, key_vectors[0], value_vectors[0])
     slots = [[SPAN * s + i for i in range(SPAN)] for s in range(16)]
 
     def branch(bits):
@@ -345,9 +358,11 @@
 
         return move
 
-    my_queries, window, live, sink8 = lax.switch(key, [branch(bits) for bits in range(8)], queries[0], kv)
-    out, kept, stat, part = forward(my_queries, out_grad[0], window, live, sink8)
-    dq, own, send = backward(my_queries, out_grad[0], kept, window, stat)
+    my_queries, window, copied, live, sink8 = lax.switch(
+        key[0], [branch(bits) for bits in range(8)], queries[0], kv
+    )
+    kept, stat, part = forward(my_queries, out_grad[0], copied, live, sink8)
+    out, dq, own, send = backward(my_queries, out_grad[0], kept, window, stat)
     received = []
     for distance in range(1, SPAN):
         pairs = [(SPAN * s + i, SPAN * s + i - distance) for s in range(16) for i in range(distance, SPAN)]

time: 80.2 us -> 72.5 us (0.904)
  blocking collectives: 15.2 us -> 25.3 us
  waiting for transfers between devices: 10.5 us -> 0.69 us
  starting transfers between devices: 35.6 us -> 29.1 us
  local copies, waits for them, and re-layouts: 2.34 us -> 1.13 us
    all_to_all x0 -> x1, blocking collectives: none -> 10.1 us  [exchange(): lax.all_to_all(rows, axis, 0, 0, axis_index_groups=groups, tiled=True)]
    all_to_all x2 -> x1, waiting for transfers between devices: 6.15 us -> 0.27 us  [exchange(): lax.all_to_all(rows, axis, 0, 0, axis_index_groups=groups, tiled=True)]
    all_to_all x2 -> x1, starting transfers between devices: 22.7 us -> 18.1 us  [exchange(): lax.all_to_all(rows, axis, 0, 0, axis_index_groups=groups, tiled=True)]
    ppermute x3, waiting for transfers between devices: 3.95 us -> 0.01 us  [per_device(): received.append(lax.ppermute(send[distance - 1], 'ctx', pairs))]
    ppermute x1, starting transfers between devices: 5.61 us -> 4.17 us  [move(): kv = lax.ppermute(kv, 'dp', pairs)]
    pallas_call x1, Pallas kernels: 5.71 us -> 4.56 us  [forward(): pl.pallas_call(forward_kernel, out_shape=(struct((rows, width), BF16), st...]
    pallas_call x1 -> x2, Pallas kernels: 0.64 us -> 1.73 us  [the longest x1 1.07 us: head(): pl.pallas_call(head_kernel, out_shape=(struct((1,), jnp.int32), struct((r...]
  transfers between devices with their start and end apart: 7 -> 6, of which waited for: 5 -> 2; matrix products, arithmetic and copies ran while one was open for 0% -> 0% of each run, Pallas kernels for 9% -> 11%
where the time goes in v4:
time: 72.5 us; the launch traced here: 71.7 us
  starting transfers between devices  29.1 us (40%)
  blocking collectives  25.3 us (35%)
  Pallas kernels  14 us (19%)
  between operations  1.46 us (2%)
  local copies, waits for them, and re-layouts  1.13 us (2%)
    all_to_all x1, starting transfers between devices, exchange(): lax.all_to_all(rows, axis, 0, 0, axis_index_groups=groups, tiled=True)  18.1 us
    all_gather x1, blocking collectives, move(): window = lax.all_gather(kv, 'ctx', axis_index_groups=slots, tiled=True)  15.2 us
    all_to_all x1, blocking collectives, exchange(): lax.all_to_all(rows, axis, 0, 0, axis_index_groups=groups, tiled=True)  10.1 us
    pallas_call x1, Pallas kernels, backward(): pl.pallas_call(backward_kernel, out_shape=(struct((rows, width), BF16), s...  6.48 us
    ppermute x3, starting transfers between devices, per_device(): received.append(lax.ppermute(send[distance - 1], 'ctx', pairs))  4.9 us
    pallas_call x1, Pallas kernels, forward(): pl.pallas_call(forward_kernel, out_shape=(struct((rows, width), BF16), st...  4.56 us
    ppermute x1, starting transfers between devices, move(): kv = lax.ppermute(kv, 'dp', pairs)  4.17 us
    ppermute x1, starting transfers between devices, move(): moved_queries = lax.ppermute(queries, 'dp', pairs)  1.92 us
  transfers between devices with their start and end apart: 6, of which 2 were waited for; matrix products, arithmetic and copies ran while one was open for 0% of the time, Pallas kernels for 11%

profile of v4, /device:TPU:1, one launch (start us, length us, event | category | flops | bytes accessed | tf_op | source)
XLA Modules:
  0.0 71.7 jit_solution(784533246905868126)
XLA Ops:
  0.6 0.0 copy-start.12
  0.6 0.0 copy-start
  0.7 0.0 copy-start.1
  0.7 0.0 copy-start.13
  0.7 0.9 %copy-done = bf16[1,128,256]{2,1,0:T(8,128)(2,1)S(1)} copy-done((bf16[1,128,256]{2,1,0:T(8,128)(2,1)S(1)}, bf16[1,128,256]{2,1,0:T(8,128)(2,1)}, u32[]{:S(2)}) %copy-start) | copy-done | bytes 65560
  1.5 0.0 copy-done.1
  1.6 1.1 %head.1 = (s32[1]{0:T(128)}, bf16[128,512]{1,0:T(8,128)(2,1)S(1)}) custom-call(s32[16]{0:T(128)S(1)} %copy-done.13, bf16[128,256]{1,0:T(8,128)(2,1)S(1)} %bitcast.23, bf16[128,256]{1,0:T(8,128)(2,1)S(1)} %bitcast.24), custom_call_target="tpu_custom_call" | custom-call | tf_op jit(solution)/shard_map/head/pallas_call | solution.py:57
  2.7 0.0 copy-start.14
  2.7 0.0 copy-start.15
  3.4 0.0 copy-start.2
  3.4 22.6 %conditional.1 = (bf16[128,2048]{1,0:T(8,128)(2,1)S(1)}, bf16[512,512]{1,0:T(8,128)(2,1)}, bf16[512,512]{1,0:T(8,128)(2,1)S(1)}, f32[128,128]{1,0:T(8,128)S(1)}, f32[32,128]{1,0:T(8,128)S(1)}) conditional(s32[]{:T(128)} %bitcast.2, (bf16[128,512]{1,0:T(8,128)(2,1)S(1)}, s32[8,16]{1,0:T(8,128)S(1)}, s32[16]{0:T(128)S(1)}, ...), branch_computations={%region_0.0_spmd, %region_1.0_spmd, %region_2.0_spmd, %region_3.0_... | conditional | flops 10000000000 | bytes 6422676 | solution.py:361
  3.4 4.2 %collective-permute-start.1 = (bf16[128,512]{1,0:T(8,128)(2,1)S(1)}, bf16[128,512]{1,0:T(8,128)(2,1)S(1)}, u32[]{:S(2)}, u32[]{:S(2)}) collective-permute-start(bf16[128,512]{1,0:T(8,128)(2,1)S(1)} %get-tuple-element.89), channel_id=1, source_target_pairs={{0,64},{64,0},{128,192},{192,128},{256,320},{320,256},{384,448},{4... | collective-permute-start | bytes 393224 | tf_op jit(solution)/shard_map/cond/branch_1_fun/ppermute | solution.py:355
  7.6 1.9 %collective-permute-start = (bf16[128,2048]{1,0:T(8,128)(2,1)S(1)}, bf16[128,2048]{1,0:T(8,128)(2,1)S(1)}, u32[]{:S(2)}, u32[]{:S(2)}) collective-permute-start(bf16[128,2048]{1,0:T(8,128)(2,1)S(1)} %get-tuple-element.88), channel_id=1, source_target_pairs={{0,64},{64,0},{128,192},{192,128},{256,320},{320,256},{384,448},{4... | collective-permute-start | bytes 1572872 | tf_op jit(solution)/shard_map/cond/branch_1_fun/ppermute | solution.py:354
  9.5 0.4 collective-permute-done.1
  9.9 15.2 %all_gather.17.kv_ref = bf16[512,512]{1,0:T(8,128)(2,1)S(1)} all-gather(bf16[128,512]{1,0:T(8,128)(2,1)S(1)} %collective-permute-done.1), channel_id=1, replica_groups={{0,1,2,3},{4,5,6,7},{8,9,10,11},{12,13,14,15},{16,17,18,19},{20,21,22,2..., dimensions={0}, use_global_device_ids=true | all-gather | bytes 655360 | tf_op jit(solution)/shard_map/cond/branch_1_fun/all_gather | solution.py:356
  25.1 0.7 prepare.9
  25.8 0.1 copy-done.4
  25.9 0.0 collective-permute-done
  26.0 0.0 copy-start.11
  26.0 4.6 %forward.1 = (bf16[128,2048]{1,0:T(8,128)(2,1)S(1)}, f32[128,128]{1,0:T(8,128)S(1)}, f32[32,128]{1,0:T(8,128)}) custom-call(bf16[128,2048]{1,0:T(8,128)(2,1)S(1)} %get-tuple-element.167.q_ref, bf16[128,2048]{1,0:T(8,128)(2,1)S(1)} %bitcast.28, bf16[512,512]{1,0:T(8,128)(2,1)S(1)} %get-tuple-element.168.kv_ref, f32[128,128]{1,0:T(8,128)S(1)} %get-tuple-element.169.live_ref, ...), custom_call_target="tpu_custom_call" | custom-call | flops 3221225472 | bytes 4194304 | tf_op jit(solution)/shard_map/forward/pallas_call | solution.py:241
  30.5 18.1 %all-to-all-start = ((f32[32,1,128]{2,1,0:T(1,128)}), f32[32,1,128]{2,1,0:T(1,128)S(1)}, u32[]{:S(2)}, u32[]{:S(2)}) async-start(f32[32,1,128]{2,1,0:T(1,128)} %bitcast.13), calls=%async_computation | async-start | bytes 32768 | tf_op jit(solution)/shard_map/all_to_all | solution.py:316
  48.7 6.5 %backward.1 = (bf16[128,2048]{1,0:T(8,128)(2,1)}, bf16[128,2048]{1,0:T(8,128)(2,1)}, f32[128,512]{1,0:T(8,128)S(1)}, bf16[3,128,512]{2,1,0:T(8,128)(2,1)S(1)}) custom-call(bf16[128,2048]{1,0:T(8,128)(2,1)S(1)} %get-tuple-element.167.q_ref, bf16[128,2048]{1,0:T(8,128)(2,1)S(1)} %bitcast.29, bf16[128,2048]{1,0:T(8,128)(2,1)S(1)} %get-tuple-element.171.kept_ref, ...), custom_call_target="tpu_custom_call" | custom-call | flops 6442450944 | bytes 4194304 | tf_op jit(solution)/shard_map/backward/pallas_call | solution.py:260
  55.2 0.7 collective-permute-start.16
  55.9 1.3 %collective-permute-start.15 = (bf16[128,512]{1,0:T(8,128)(2,1)S(1)}, bf16[128,512]{1,0:T(8,128)(2,1)S(1)}, u32[]{:S(2)}, u32[]{:S(2)}) collective-permute-start(bf16[128,512]{1,0:T(8,128)(2,1)S(1)} %get-tuple-element.182), channel_id=1, source_target_pairs={{2,0},{3,1},{6,4},{7,5},{10,8},{11,9},{14,12},{15,13},{18,16},{19,... | collective-permute-start | bytes 393224 | tf_op jit(solution)/shard_map/ppermute | solution.py:369
  57.2 2.9 %collective-permute-start.14 = (bf16[128,512]{1,0:T(8,128)(2,1)S(1)}, bf16[128,512]{1,0:T(8,128)(2,1)S(1)}, u32[]{:S(2)}, u32[]{:S(2)}) collective-permute-start(bf16[128,512]{1,0:T(8,128)(2,1)S(1)} %get-tuple-element.183), channel_id=1, source_target_pairs={{1,0},{2,1},{3,2},{5,4},{6,5},{7,6},{9,8},{10,9},{11,10},{13,12},{... | collective-permute-start | bytes 393224 | tf_op jit(solution)/shard_map/ppermute | solution.py:369
  60.1 0.3 all-to-all-done
  60.4 10.1 %all_to_all.10 = f32[16,1,128]{2,1,0:T(1,128)S(1)} all-to-all(f32[16,1,128]{2,1,0:T(1,128)S(1)} %bitcast.27), channel_id=1, replica_groups={{0,32,64,96,128,160,192,224,256,288,320,352,384,416,448,480},{1,33,65,9..., dimensions={0} | all-to-all | bytes 16384 | tf_op jit(solution)/shard_map/all_to_all | solution.py:316
  70.5 0.5 finish.1
  71.0 0.0 collective-permute-done.16.third_ref
  71.0 0.0 collective-permute-done.15.second_ref
  71.0 0.0 collective-permute-done.14.first_ref
  71.0 0.7 grads.1
  (10 shorter events, 0.1 us)
Async XLA Ops:
  0.6 2.7 %copy-start.12 = (bf16[1,128,2048]{2,1,0:T(8,128)(2,1)S(1)}, bf16[1,128,2048]{2,1,0:T(8,128)(2,1)}, u32[]{:S(2)}) copy-start(bf16[1,128,2048]{2,1,0:T(8,128)(2,1)} %param.15) | copy-start | bytes 1572868
  0.6 0.9 %copy-start = (bf16[1,128,256]{2,1,0:T(8,128)(2,1)S(1)}, bf16[1,128,256]{2,1,0:T(8,128)(2,1)}, u32[]{:S(2)}) copy-start(bf16[1,128,256]{2,1,0:T(8,128)(2,1)} %param.16) | copy-start | bytes 196612
  0.7 0.9 %copy-start.1 = (bf16[1,128,256]{2,1,0:T(8,128)(2,1)S(1)}, bf16[1,128,256]{2,1,0:T(8,128)(2,1)}, u32[]{:S(2)}) copy-start(bf16[1,128,256]{2,1,0:T(8,128)(2,1)} %param.17) | copy-start | bytes 196612
  0.7 0.9 %copy-start.13 = (s32[16]{0:T(128)S(1)}, s32[16]{0:T(128)}, u32[]{:S(2)}) copy-start(s32[16]{0:T(128)} %plan_ref.1) | copy-start | bytes 196
  2.7 0.7 copy-start.14
  2.7 0.7 copy-start.15
  3.4 22.6 %copy-start.2 = (bf16[1,128,2048]{2,1,0:T(8,128)(2,1)S(1)}, bf16[1,128,2048]{2,1,0:T(8,128)(2,1)}, u32[]{:S(2)}) copy-start(bf16[1,128,2048]{2,1,0:T(8,128)(2,1)} %param.18) | copy-start | bytes 1572868
  3.4 6.5 %collective-permute-start.1 = (bf16[128,512]{1,0:T(8,128)(2,1)S(1)}, bf16[128,512]{1,0:T(8,128)(2,1)S(1)}, u32[]{:S(2)}, u32[]{:S(2)}) collective-permute-start(bf16[128,512]{1,0:T(8,128)(2,1)S(1)} %get-tuple-element.89), channel_id=1, source_target_pairs={{0,64},{64,0},{128,192},{192,128},{256,320},{320,256},{384,448},{4... | collective-permute-start | bytes 393224 | tf_op jit(solution)/shard_map/cond/branch_1_fun/ppermute | solution.py:355
  7.6 18.3 %collective-permute-start = (bf16[128,2048]{1,0:T(8,128)(2,1)S(1)}, bf16[128,2048]{1,0:T(8,128)(2,1)S(1)}, u32[]{:S(2)}, u32[]{:S(2)}) collective-permute-start(bf16[128,2048]{1,0:T(8,128)(2,1)S(1)} %get-tuple-element.88), channel_id=1, source_target_pairs={{0,64},{64,0},{128,192},{192,128},{256,320},{320,256},{384,448},{4... | collective-permute-start | bytes 1572872 | tf_op jit(solution)/shard_map/cond/branch_1_fun/ppermute | solution.py:354
  25.1 0.8 %copy-start.4 = (bf16[512,512]{1,0:T(8,128)(2,1)}, bf16[512,512]{1,0:T(8,128)(2,1)S(1)}, u32[]{:S(2)}) copy-start(bf16[512,512]{1,0:T(8,128)(2,1)S(1)} %all_gather.17.kv_ref) | copy-start | bytes 1572868 | tf_op jit(solution)/shard_map/cond
  26.0 22.7 %copy-start.11 = (bf16[512,512]{1,0:T(8,128)(2,1)S(1)}, bf16[512,512]{1,0:T(8,128)(2,1)}, u32[]{:S(2)}) copy-start(bf16[512,512]{1,0:T(8,128)(2,1)} %get-tuple-element.172.kv_ref) | copy-start | bytes 1572868
  30.5 29.9 %all-to-all-start = ((f32[32,1,128]{2,1,0:T(1,128)}), f32[32,1,128]{2,1,0:T(1,128)S(1)}, u32[]{:S(2)}, u32[]{:S(2)}) async-start(f32[32,1,128]{2,1,0:T(1,128)} %bitcast.13), calls=%async_computation | async-start | bytes 32768 | tf_op jit(solution)/shard_map/all_to_all | solution.py:316
  55.2 15.8 %collective-permute-start.16 = (bf16[128,512]{1,0:T(8,128)(2,1)S(1)}, bf16[128,512]{1,0:T(8,128)(2,1)S(1)}, u32[]{:S(2)}, u32[]{:S(2)}) collective-permute-start(bf16[128,512]{1,0:T(8,128)(2,1)S(1)} %get-tuple-element.181), channel_id=1, source_target_pairs={{3,0},{7,4},{11,8},{15,12},{19,16},{23,20},{27,24},{31,28},{35,32}... | collective-permute-start | bytes 393224 | tf_op jit(solution)/shard_map/ppermute | solution.py:369
  55.9 15.2 %collective-permute-start.15 = (bf16[128,512]{1,0:T(8,128)(2,1)S(1)}, bf16[128,512]{1,0:T(8,128)(2,1)S(1)}, u32[]{:S(2)}, u32[]{:S(2)}) collective-permute-start(bf16[128,512]{1,0:T(8,128)(2,1)S(1)} %get-tuple-element.182), channel_id=1, source_target_pairs={{2,0},{3,1},{6,4},{7,5},{10,8},{11,9},{14,12},{15,13},{18,16},{19,... | collective-permute-start | bytes 393224 | tf_op jit(solution)/shard_map/ppermute | solution.py:369
  57.2 13.9 %collective-permute-start.14 = (bf16[128,512]{1,0:T(8,128)(2,1)S(1)}, bf16[128,512]{1,0:T(8,128)(2,1)S(1)}, u32[]{:S(2)}, u32[]{:S(2)}) collective-permute-start(bf16[128,512]{1,0:T(8,128)(2,1)S(1)} %get-tuple-element.183), channel_id=1, source_target_pairs={{1,0},{2,1},{3,2},{5,4},{6,5},{7,6},{9,8},{10,9},{11,10},{13,12},{... | collective-permute-start | bytes 393224 | tf_op jit(solution)/shard_map/ppermute | solution.py:369

commit v5 on v4

--- a/solution.py
+++ b/solution.py
@@ -17,6 +17,9 @@
 MASKED = -1e30
 Z_CORE = 32
 X_Y = 16
+FIRST_PAIRS = 3
+FIRST_COLS = FIRST_PAIRS * LANES
+SENDS = (((1, 0), (3, 2)), ((2, 0), (3, 1)), ((3, 0), (2, 1)))
 W_PREPARE = 10**10
 W_NEAR = 10**10
 
@@ -46,22 +49,44 @@
     return lax.axis_index("ctx") % SPAN
 
 
-def head_kernel(plan_ref, k_ref, v_ref, key_ref, kv_ref):
-    key_ref[0] = plan_ref[lax.axis_index("ctx") // SPAN]
-    kv_ref[:, :KV_COLS] = k_ref[...]
-    kv_ref[:, KV_COLS:] = v_ref[...]
-
-
-def head(route_plan, keys, values):
-    rows = keys.shape[0]
+def head_kernel(plan_ref, k_ref, v_ref, q_ref, key_ref, first_ref, second_ref, plan, sems):
+    copies = [
+        pltpu.make_async_copy(plan_ref, plan, sems.at[0]),
+        pltpu.make_async_copy(k_ref, first_ref.at[:, :KV_COLS], sems.at[1]),
+        pltpu.make_async_copy(v_ref, first_ref.at[:, KV_COLS : 2 * KV_COLS], sems.at[2]),
+        pltpu.make_async_copy(q_ref.at[:, :FIRST_COLS], first_ref.at[:, 2 * KV_COLS :], sems.at[3]),
+        pltpu.make_async_copy(q_ref.at[:, FIRST_COLS:], second_ref, sems.at[4]),
+    ]
+    for copy in copies:
+        copy.start()
+    copies[0].wait()
+    key_ref[0] = plan[lax.axis_index("ctx") // SPAN]
+    for copy in copies[1:]:
+        copy.wait()
+
+
+def head(route_plan, keys, values, queries):
+    rows, width = queries.shape
+    hbm = pl.BlockSpec(memory_space=pltpu.HBM)
     return pl.pallas_call(
         head_kernel,
-        out_shape=(struct((1,), jnp.int32), struct((rows, 2 * KV_COLS), BF16)),
-        in_specs=[SMEM, VMEM, VMEM],
-        out_specs=(SMEM, VMEM),
-        compiler_params=params(2),
+        out_shape=(
+            struct((1,), jnp.int32),
+            struct((rows, 2 * KV_COLS + FIRST_COLS), BF16),
+            struct((rows, width - FIRST_COLS), BF16),
+        ),
+        in_specs=[hbm] * 4,
+        out_specs=(SMEM, VMEM, VMEM),
+        scratch_shapes=[pltpu.SMEM(route_plan.shape, jnp.int32), pltpu.SemaphoreType.DMA((5,))],
+        compiler_params=params(60),
         name="head",
-    )(route_plan, keys, values)
+    )(route_plan, keys, values, queries)
+
+
+def pair_queries(first_ref, second_ref, pair):
+    if pair < FIRST_PAIRS:
+        return first_ref[:, 2 * KV_COLS + pair * LANES : 2 * KV_COLS + (pair + 1) * LANES]
+    return second_ref[:, (pair - FIRST_PAIRS) * LANES : (pair - FIRST_PAIRS + 1) * LANES]
 
 
 def prepare_kernel(lengths_ref, plan_ref, sink_ref, kv_ref, copy_ref, live_ref, sink8_ref):
@@ -98,9 +123,9 @@
 
 
 def forward_kernel(
-    q_ref, do_ref, kv_ref, live_ref, sink8_ref, kept_ref, stat_ref, part_ref, terms
+    first_ref, second_ref, do_ref, kv_ref, live_ref, sink8_ref, kept_ref, stat_ref, part_ref, terms
 ):
-    rows = q_ref.shape[0]
+    rows = do_ref.shape[0]
     window = kv_ref.shape[0]
     query_pos = lax.broadcasted_iota(jnp.int32, (rows, window), 0) + within_slot() * rows
     key_pos = lax.broadcasted_iota(jnp.int32, (rows, window), 1)
@@ -121,7 +146,7 @@
         values = [jnp.concatenate([values[i], ones[i]], axis=1) for i in range(2)]
         for pair in range(group * 4, group * 4 + 4):
             cols = slice(pair * LANES, (pair + 1) * LANES)
-            q2 = q_ref[:, cols]
+            q2 = pair_queries(first_ref, second_ref, pair)
             sink8 = [sink8_ref[2 * pair + which : 2 * pair + which + 1, :] for which in range(2)]
             sums, maxima = None, []
             for which in range(2):
@@ -152,11 +177,12 @@
 
 
 def backward_kernel(
-    q_ref, do_ref, kept_ref, kv_ref, stat_ref, out_ref, dq_ref, own_ref, send_ref, acc_k, acc_v, held
+    first_ref, second_ref, do_ref, kept_ref, kv_ref, stat_ref, out_ref, dq_ref, own_ref, send_ref, acc_k, acc_v, held
 ):
-    rows = q_ref.shape[0]
+    rows = do_ref.shape[0]
     window = kv_ref.shape[0]
     within = within_slot()
+    targets = (jnp.maximum(within - 1, 0), jnp.maximum(within - 2, 0), SPAN - 1 - within)
     key_pos = lax.broadcasted_iota(jnp.int32, (window, rows), 0)
     query_pos = lax.broadcasted_iota(jnp.int32, (window, rows), 1) + within * rows
     bias = jnp.where(key_pos <= query_pos, 0.0, MASKED).astype(F32)
@@ -179,7 +205,7 @@
             for quad in range(2):
                 pair = group * 4 + 2 * quad
                 two = [slice(at * LANES, (at + 1) * LANES) for at in (pair, pair + 1)]
-                q4 = jnp.concatenate([q_ref[:, cols] for cols in two], axis=0)
+                q4 = jnp.concatenate([pair_queries(first_ref, second_ref, at) for at in (pair, pair + 1)], axis=0)
                 do4 = jnp.concatenate([do_ref[:, cols] for cols in two], axis=0)
                 out4 = jnp.concatenate([kept_ref[:, cols] for cols in two], axis=0)
                 for at, cols in enumerate(two):
@@ -221,9 +247,8 @@
             acc[0] = total if factor is None else total * factor
             at = slice(which * KV_COLS + duo * LANES, which * KV_COLS + (duo + 1) * LANES)
             own_ref[:, at] = acc[0, pl.ds(pl.multiple_of(within * rows, rows), rows), :]
-            for distance in range(1, SPAN):
-                block = jnp.maximum(within - distance, 0)
-                send_ref[distance - 1, :, at] = acc[
+            for turn, block in enumerate(targets):
+                send_ref[turn, :, at] = acc[
                     0, pl.ds(pl.multiple_of(block * rows, rows), rows), :
                 ].astype(BF16)
 
@@ -236,8 +261,8 @@
     )
 
 
-def forward(queries, out_grad, kv, live, sink8):
-    rows, width = queries.shape
+def forward(first, second, out_grad, kv, live, sink8):
+    rows, width = out_grad.shape
     return pl.pallas_call(
         forward_kernel,
         out_shape=(
@@ -245,17 +270,17 @@
             struct((LANES, rows), F32),
             struct((Z_CORE, LANES), F32),
         ),
-        in_specs=[VMEM] * 5,
+        in_specs=[VMEM] * 6,
         out_specs=(VMEM,) * 3,
         scratch_shapes=[pltpu.VMEM((LANES, LANES), F32)],
         compiler_params=params(),
         cost_estimate=estimate(3, rows),
         name="forward",
-    )(queries, out_grad, kv, live, sink8)
-
-
-def backward(queries, out_grad, out, kv, stat):
-    rows, width = queries.shape
+    )(first, second, out_grad, kv, live, sink8)
+
+
+def backward(first, second, out_grad, out, kv, stat):
+    rows, width = out_grad.shape
     window = kv.shape[0]
     return pl.pallas_call(
         backward_kernel,
@@ -265,14 +290,14 @@
             struct((rows, 2 * KV_COLS), F32),
             struct((SPAN - 1, rows, 2 * KV_COLS), BF16),
         ),
-        in_specs=[VMEM] * 5,
+        in_specs=[VMEM] * 6,
         out_specs=(VMEM,) * 4,
         scratch_shapes=[pltpu.VMEM((2, window, LANES), F32)] * 2
         + [pltpu.VMEM((window, HEAD_GROUP * rows), BF16)],
         compiler_params=params(),
         cost_estimate=estimate(6, rows),
         name="backward",
-    )(queries, out_grad, out, kv, stat)
+    )(first, second, out_grad, out, kv, stat)
 
 
 def relay_kernel(rows_ref, out_ref):
@@ -291,23 +316,7 @@
     )(rows)
 
 
-def finish_kernel(rows_ref, out_ref):
-    out_ref[...] = jnp.sum(rows_ref[...], axis=0)[:Q_HEADS]
-
-
-def finish(rows):
-    return pl.pallas_call(
-        finish_kernel,
-        out_shape=struct((Q_HEADS,), F32),
-        in_specs=[VMEM],
-        out_specs=VMEM,
-        cost_estimate=pl.CostEstimate(flops=1024, bytes_accessed=32768, transcendentals=0),
-        compiler_params=params(1),
-        name="finish",
-    )(rows)
-
-
-def sink_total(part):
+def sink_rows(part):
     z_core = [[x * 32 + i for i in range(Z_CORE)] for x in range(2)]
     x_y = [[dp * 64 + x * 32 + i for dp in range(8) for x in range(2)] for i in range(Z_CORE)]
 
@@ -316,11 +325,11 @@
         return lax.all_to_all(rows, axis, 0, 0, axis_index_groups=groups, tiled=True)[:, 0, :]
 
     near = exchange(part, "ctx", z_core)
-    far = exchange(relay(near, X_Y), ("dp", "ctx"), x_y)
-    return finish(far)
-
-
-def grads_kernel(own_ref, first_ref, second_ref, third_ref, key_ref, value_ref):
+    return exchange(relay(near, X_Y), ("dp", "ctx"), x_y)
+
+
+def finish_kernel(rows_ref, own_ref, first_ref, second_ref, third_ref, sink_ref, key_ref, value_ref):
+    sink_ref[...] = jnp.sum(rows_ref[...], axis=0)[:Q_HEADS]
     total = own_ref[...]
     for ref in (first_ref, second_ref, third_ref):
         total = total + ref[...].astype(F32)
@@ -329,46 +338,45 @@
     value_ref[...] = total[:, KV_COLS:]
 
 
-def grads(own, received):
+def finish(rows, own, received):
     shape = struct((own.shape[0], KV_COLS), BF16)
     return pl.pallas_call(
-        grads_kernel,
-        out_shape=(shape, shape),
-        in_specs=[VMEM] * SPAN,
-        out_specs=(VMEM, VMEM),
+        finish_kernel,
+        out_shape=(struct((Q_HEADS,), F32), shape, shape),
+        in_specs=[VMEM] * (SPAN + 1),
+        out_specs=(VMEM,) * 3,
         compiler_params=params(2),
-        name="grads",
-    )(own, *received)
+        name="finish",
+    )(rows, own, *received)
 
 
 def per_device(queries, key_vectors, value_vectors, out_grad, sink_logits, lengths, route_plan):
-    key, kv = head(route_plan, key_vectors[0], value_vectors[0])
+    key, first, second = head(route_plan, key_vectors[0], value_vectors[0], queries[0])
     slots = [[SPAN * s + i for i in range(SPAN)] for s in range(16)]
 
     def branch(bits):
         pairs = [(i, i ^ bits) for i in range(8)]
 
-        def move(queries, kv):
-            moved_queries = queries
+        def move(first, second):
             if bits:
-                moved_queries = lax.ppermute(queries, "dp", pairs)
-                kv = lax.ppermute(kv, "dp", pairs)
-            window = lax.all_gather(kv, "ctx", axis_index_groups=slots, tiled=True)
-            return moved_queries, window, *prepare(lengths, route_plan, sink_logits, window)
+                second = lax.ppermute(second, "dp", pairs)
+                first = lax.ppermute(first, "dp", pairs)
+            window = lax.all_gather(first[:, : 2 * KV_COLS], "ctx", axis_index_groups=slots, tiled=True)
+            return first, second, *prepare(lengths, route_plan, sink_logits, window)
 
         return move
 
-    my_queries, window, copied, live, sink8 = lax.switch(
-        key[0], [branch(bits) for bits in range(8)], queries[0], kv
+    first, second, window, live, sink8 = lax.switch(
+        key[0], [branch(bits) for bits in range(8)], first, second
     )
-    kept, stat, part = forward(my_queries, out_grad[0], copied, live, sink8)
-    out, dq, own, send = backward(my_queries, out_grad[0], kept, window, stat)
+    kept, stat, part = forward(first, second, out_grad[0], window, live, sink8)
+    out, dq, own, send = backward(first, second, out_grad[0], kept, window, stat)
     received = []
-    for distance in range(1, SPAN):
-        pairs = [(SPAN * s + i, SPAN * s + i - distance) for s in range(16) for i in range(distance, SPAN)]
-        received.append(lax.ppermute(send[distance - 1], "ctx", pairs))
-    key_grad, value_grad = grads(own, received)
-    return out[None], dq[None], key_grad[None], value_grad[None], sink_total(part)
+    for turn in (2, 1, 0):
+        pairs = [(SPAN * s + a, SPAN * s + b) for s in range(16) for a, b in SENDS[turn]]
+        received.append(lax.ppermute(send[turn], "ctx", pairs))
+    sink_grad, key_grad, value_grad = finish(sink_rows(part), own, received)
+    return out[None], dq[None], key_grad[None], value_grad[None], sink_grad
 
 
 def solution(mesh):

time: 72.5 us -> 72.5 us (level)
  starting transfers between devices: 29.1 us -> 25.9 us
  waiting for transfers between devices: 0.69 us -> 2.71 us
  blocking collectives: 25.3 us -> 26.9 us
    all_to_all x1, starting transfers between devices: 18.1 us -> 11 us  [exchange(): lax.all_to_all(rows, axis, 0, 0, axis_index_groups=groups, tiled=True)]
    ppermute x5, starting transfers between devices: 11 us -> 14.9 us  [the longest x1 8.06 us: move(): first = lax.ppermute(first, 'dp', pairs)]
    all_to_all x1, blocking collectives: 10.1 us -> 12.4 us  [exchange(): lax.all_to_all(rows, axis, 0, 0, axis_index_groups=groups, tiled=True)]
    ppermute x5, waiting for transfers between devices: 0.42 us -> 2.33 us  [the longest x1 2.32 us: move(): first = lax.ppermute(first, 'dp', pairs)]
  transfers between devices with their start and end apart: 6 -> 6, of which waited for: 2 -> 2; matrix products, arithmetic and copies ran while one was open for 0% -> 0% of each run, Pallas kernels for 11% -> 10%
where the time goes in v5:
time: 72.5 us; the launch traced here: 71.7 us
  blocking collectives  26.9 us (37%)
  starting transfers between devices  25.9 us (36%)
  Pallas kernels  13.9 us (19%)
  waiting for transfers between devices  2.71 us (4%)
  between operations  1.41 us (2%)
  local copies, waits for them, and re-layouts  0.76 us (1%)
    all_gather x1, blocking collectives, move(): lax.all_gather(first[:, :2 * KV_COLS], 'ctx', axis_index_groups=slots, ti...  14.5 us
    all_to_all x1, blocking collectives, exchange(): lax.all_to_all(rows, axis, 0, 0, axis_index_groups=groups, tiled=True)  12.4 us
    all_to_all x1, starting transfers between devices, exchange(): lax.all_to_all(rows, axis, 0, 0, axis_index_groups=groups, tiled=True)  11 us
    ppermute x1, starting transfers between devices, move(): first = lax.ppermute(first, 'dp', pairs)  8.06 us
    pallas_call x1, Pallas kernels, backward(): pl.pallas_call(backward_kernel, out_shape=(struct((rows, width), BF16), s...  6.37 us
    ppermute x3, starting transfers between devices, per_device(): received.append(lax.ppermute(send[turn], 'ctx', pairs))  4.91 us
    pallas_call x1, Pallas kernels, forward(): pl.pallas_call(forward_kernel, out_shape=(struct((rows, width), BF16), st...  4.53 us
    ppermute x1, waiting for transfers between devices, move(): first = lax.ppermute(first, 'dp', pairs)  2.32 us
  transfers between devices with their start and end apart: 6, of which 2 were waited for; matrix products, arithmetic and copies ran while one was open for 0% of the time, Pallas kernels for 10%

profile of v5, /device:TPU:1, one launch (start us, length us, event | category | flops | bytes accessed | tf_op | source)
XLA Modules:
  0.0 71.7 jit_solution(11927479038217085939)
XLA Ops:
  0.6 0.0 copy-start.1
  0.6 0.6 copy-done.1
  1.3 1.7 %head.1 = (s32[1]{0:T(128)}, bf16[128,896]{1,0:T(8,128)(2,1)S(1)}, bf16[128,1664]{1,0:T(8,128)(2,1)S(1)}) custom-call(s32[16]{0:T(128)S(1)} %copy-done.1, bf16[128,256]{1,0:T(8,128)(2,1)} %bitcast.29, bf16[128,256]{1,0:T(8,128)(2,1)} %bitcast.30, bf16[128,2048]{1,0:T(8,128)(2,1)} %bitcast.28), custom_call_target="tpu_custom_call" | custom-call | tf_op jit(solution)/shard_map/head/pallas_call | solution.py:71
  3.0 0.0 copy-start.2
  3.0 0.0 copy-start.3
  3.7 0.0 copy-done.2
  3.7 0.0 copy-done.3
  3.7 0.0 copy-start
  3.7 27.6 %conditional.1 = (bf16[128,896]{1,0:T(8,128)(2,1)S(1)}, bf16[128,1664]{1,0:T(8,128)(2,1)S(1)}, bf16[512,512]{1,0:T(8,128)(2,1)S(1)}, f32[128,128]{1,0:T(8,128)S(1)}, f32[32,128]{1,0:T(8,128)S(1)}) conditional(s32[]{:T(128)} %bitcast.3, (bf16[128,896]{1,0:T(8,128)(2,1)S(1)}, s32[8,16]{1,0:T(8,128)S(1)}, ...), branch_computations={%region_0.0_spmd, %region_1.0_spmd, %region_2.0_spmd, %region_3.0_... | conditional | flops 10000000000 | bytes 4849784 | solution.py:369
  3.8 8.1 %collective-permute-start.12 = (bf16[128,896]{1,0:T(8,128)(2,1)S(1)}, bf16[128,896]{1,0:T(8,128)(2,1)S(1)}, u32[]{:S(2)}, u32[]{:S(2)}) collective-permute-start(bf16[128,896]{1,0:T(8,128)(2,1)S(1)} %get-tuple-element.136), channel_id=1, source_target_pairs={{0,448},{64,384},{128,320},{192,256},{256,192},{320,128},{384,64},... | collective-permute-start | bytes 688136 | tf_op jit(solution)/shard_map/cond/branch_7_fun/ppermute | solution.py:363
  11.8 1.9 %collective-permute-start.13 = (bf16[128,1664]{1,0:T(8,128)(2,1)S(1)}, bf16[128,1664]{1,0:T(8,128)(2,1)S(1)}, u32[]{:S(2)}, u32[]{:S(2)}) collective-permute-start(bf16[128,1664]{1,0:T(8,128)(2,1)S(1)} %get-tuple-element.137), channel_id=1, source_target_pairs={{0,448},{64,384},{128,320},{192,256},{256,192},{320,128},{384,64},... | collective-permute-start | bytes 1277960 | tf_op jit(solution)/shard_map/cond/branch_7_fun/ppermute | solution.py:362
  13.8 2.3 %collective-permute-done.12 = bf16[128,896]{1,0:T(8,128)(2,1)S(1)} collective-permute-done((bf16[128,896]{1,0:T(8,128)(2,1)S(1)}, bf16[128,896]{1,0:T(8,128)(2,1)S(1)}, u32[]{:S(2)}, u32[]{:S(2)}) %collective-permute-start.12) | collective-permute-done | bytes 229408 | tf_op jit(solution)/shard_map/cond/branch_7_fun/ppermute | solution.py:363
  16.1 14.5 %all_gather.23.kv_ref = bf16[512,512]{1,0:T(8,128)(2,1)S(1)} all-gather(bf16[128,512]{1,0:T(8,128)(2,1)S(1)} %slice.42), channel_id=1, replica_groups={{0,1,2,3},{4,5,6,7},{8,9,10,11},{12,13,14,15},{16,17,18,19},{20,21,22,2..., dimensions={0}, use_global_device_ids=true | all-gather | bytes 655360 | tf_op jit(solution)/shard_map/cond/branch_7_fun/all_gather | solution.py:364
  30.6 0.7 prepare.15
  31.3 0.0 collective-permute-done.13
  31.3 0.0 copy-done
  31.3 4.5 %forward.1 = (bf16[128,2048]{1,0:T(8,128)(2,1)S(1)}, f32[128,128]{1,0:T(8,128)S(1)}, f32[32,128]{1,0:T(8,128)}) custom-call(bf16[128,896]{1,0:T(8,128)(2,1)S(1)} %get-tuple-element.170.first_ref, bf16[128,1664]{1,0:T(8,128)(2,1)S(1)} %get-tuple-element.171.second_ref, bf16[128,2048]{1,0:T(8,128)(2,1)S(1)} %bitcast.26, ...), custom_call_target="tpu_custom_call" | custom-call | flops 3221225472 | bytes 4194304 | tf_op jit(solution)/shard_map/forward/pallas_call | solution.py:266
  35.9 11.0 %all-to-all-start = ((f32[32,1,128]{2,1,0:T(1,128)}), f32[32,1,128]{2,1,0:T(1,128)S(1)}, u32[]{:S(2)}, u32[]{:S(2)}) async-start(f32[32,1,128]{2,1,0:T(1,128)} %bitcast.8), calls=%async_computation | async-start | bytes 32768 | tf_op jit(solution)/shard_map/all_to_all | solution.py:325
  46.9 6.4 %backward.1 = (bf16[128,2048]{1,0:T(8,128)(2,1)}, bf16[128,2048]{1,0:T(8,128)(2,1)}, f32[128,512]{1,0:T(8,128)S(1)}, bf16[3,128,512]{2,1,0:T(8,128)(2,1)S(1)}) custom-call(bf16[128,896]{1,0:T(8,128)(2,1)S(1)} %get-tuple-element.170.first_ref, bf16[128,1664]{1,0:T(8,128)(2,1)S(1)} %get-tuple-element.171.second_ref, bf16[128,2048]{1,0:T(8,128)(2,1)S(1)} %bitcast.27, ...), custom_call_target="tpu_custom_call" | custom-call | flops 6442450944 | bytes 4194304 | tf_op jit(solution)/shard_map/backward/pallas_call | solution.py:285
  53.3 2.3 %collective-permute-start.16 = (bf16[128,512]{1,0:T(8,128)(2,1)S(1)}, bf16[128,512]{1,0:T(8,128)(2,1)S(1)}, u32[]{:S(2)}, u32[]{:S(2)}) collective-permute-start(bf16[128,512]{1,0:T(8,128)(2,1)S(1)} %get-tuple-element.185), channel_id=1, source_target_pairs={{1,0},{3,2},{5,4},{7,6},{9,8},{11,10},{13,12},{15,14},{17,16},{19,... | collective-permute-start | bytes 393224 | tf_op jit(solution)/shard_map/ppermute | solution.py:377
  55.6 1.3 %collective-permute-start.15 = (bf16[128,512]{1,0:T(8,128)(2,1)S(1)}, bf16[128,512]{1,0:T(8,128)(2,1)S(1)}, u32[]{:S(2)}, u32[]{:S(2)}) collective-permute-start(bf16[128,512]{1,0:T(8,128)(2,1)S(1)} %get-tuple-element.186), channel_id=1, source_target_pairs={{2,0},{3,1},{6,4},{7,5},{10,8},{11,9},{14,12},{15,13},{18,16},{19,... | collective-permute-start | bytes 393224 | tf_op jit(solution)/shard_map/ppermute | solution.py:377
  56.9 1.3 %collective-permute-start.14 = (bf16[128,512]{1,0:T(8,128)(2,1)S(1)}, bf16[128,512]{1,0:T(8,128)(2,1)S(1)}, u32[]{:S(2)}, u32[]{:S(2)}) collective-permute-start(bf16[128,512]{1,0:T(8,128)(2,1)S(1)} %get-tuple-element.187), channel_id=1, source_target_pairs={{3,0},{2,1},{7,4},{6,5},{11,8},{10,9},{15,12},{14,13},{19,16},{18,... | collective-permute-start | bytes 393224 | tf_op jit(solution)/shard_map/ppermute | solution.py:377
  58.2 0.4 all-to-all-done
  58.6 12.4 %all_to_all.10 = f32[16,1,128]{2,1,0:T(1,128)S(1)} all-to-all(f32[16,1,128]{2,1,0:T(1,128)S(1)} %bitcast.25), channel_id=1, replica_groups={{0,32,64,96,128,160,192,224,256,288,320,352,384,416,448,480},{1,33,65,9..., dimensions={0} | all-to-all | bytes 16384 | tf_op jit(solution)/shard_map/all_to_all | solution.py:325
  71.0 0.0 collective-permute-done.16.third_ref
  71.0 0.0 collective-permute-done.15.second_ref
  71.0 0.0 collective-permute-done.14.first_ref
  71.0 0.7 finish.1
  (5 shorter events, 0.1 us)
Async XLA Ops:
  0.6 0.7 copy-start.1
  3.0 0.7 copy-start.2
  3.0 0.7 copy-start.3
  3.7 27.6 %copy-start = (bf16[1,128,2048]{2,1,0:T(8,128)(2,1)S(1)}, bf16[1,128,2048]{2,1,0:T(8,128)(2,1)}, u32[]{:S(2)}) copy-start(bf16[1,128,2048]{2,1,0:T(8,128)(2,1)} %param.18) | copy-start | bytes 1572868
  3.8 12.3 %collective-permute-start.12 = (bf16[128,896]{1,0:T(8,128)(2,1)S(1)}, bf16[128,896]{1,0:T(8,128)(2,1)S(1)}, u32[]{:S(2)}, u32[]{:S(2)}) collective-permute-start(bf16[128,896]{1,0:T(8,128)(2,1)S(1)} %get-tuple-element.136), channel_id=1, source_target_pairs={{0,448},{64,384},{128,320},{192,256},{256,192},{320,128},{384,64},... | collective-permute-start | bytes 688136 | tf_op jit(solution)/shard_map/cond/branch_7_fun/ppermute | solution.py:363
  11.8 19.4 %collective-permute-start.13 = (bf16[128,1664]{1,0:T(8,128)(2,1)S(1)}, bf16[128,1664]{1,0:T(8,128)(2,1)S(1)}, u32[]{:S(2)}, u32[]{:S(2)}) collective-permute-start(bf16[128,1664]{1,0:T(8,128)(2,1)S(1)} %get-tuple-element.137), channel_id=1, source_target_pairs={{0,448},{64,384},{128,320},{192,256},{256,192},{320,128},{384,64},... | collective-permute-start | bytes 1277960 | tf_op jit(solution)/shard_map/cond/branch_7_fun/ppermute | solution.py:362
  35.9 22.7 %all-to-all-start = ((f32[32,1,128]{2,1,0:T(1,128)}), f32[32,1,128]{2,1,0:T(1,128)S(1)}, u32[]{:S(2)}, u32[]{:S(2)}) async-start(f32[32,1,128]{2,1,0:T(1,128)} %bitcast.8), calls=%async_computation | async-start | bytes 32768 | tf_op jit(solution)/shard_map/all_to_all | solution.py:325
  53.3 17.7 %collective-permute-start.16 = (bf16[128,512]{1,0:T(8,128)(2,1)S(1)}, bf16[128,512]{1,0:T(8,128)(2,1)S(1)}, u32[]{:S(2)}, u32[]{:S(2)}) collective-permute-start(bf16[128,512]{1,0:T(8,128)(2,1)S(1)} %get-tuple-element.185), channel_id=1, source_target_pairs={{1,0},{3,2},{5,4},{7,6},{9,8},{11,10},{13,12},{15,14},{17,16},{19,... | collective-permute-start | bytes 393224 | tf_op jit(solution)/shard_map/ppermute | solution.py:377
  55.6 15.4 %collective-permute-start.15 = (bf16[128,512]{1,0:T(8,128)(2,1)S(1)}, bf16[128,512]{1,0:T(8,128)(2,1)S(1)}, u32[]{:S(2)}, u32[]{:S(2)}) collective-permute-start(bf16[128,512]{1,0:T(8,128)(2,1)S(1)} %get-tuple-element.186), channel_id=1, source_target_pairs={{2,0},{3,1},{6,4},{7,5},{10,8},{11,9},{14,12},{15,13},{18,16},{19,... | collective-permute-start | bytes 393224 | tf_op jit(solution)/shard_map/ppermute | solution.py:377
  56.9 14.1 %collective-permute-start.14 = (bf16[128,512]{1,0:T(8,128)(2,1)S(1)}, bf16[128,512]{1,0:T(8,128)(2,1)S(1)}, u32[]{:S(2)}, u32[]{:S(2)}) collective-permute-start(bf16[128,512]{1,0:T(8,128)(2,1)S(1)} %get-tuple-element.187), channel_id=1, source_target_pairs={{3,0},{2,1},{7,4},{6,5},{11,8},{10,9},{15,12},{14,13},{19,16},{18,... | collective-permute-start | bytes 393224 | tf_op jit(solution)/shard_map/ppermute | solution.py:377

commit v6 on v5

--- a/solution.py
+++ b/solution.py
@@ -318,7 +318,7 @@
 
 def sink_rows(part):
     z_core = [[x * 32 + i for i in range(Z_CORE)] for x in range(2)]
-    x_y = [[dp * 64 + x * 32 + i for dp in range(8) for x in range(2)] for i in range(Z_CORE)]
+    x_y = [[dp * 64 + x * 32 + i for dp in (6, 7, 2, 3, 5, 4, 1, 0) for x in range(2)] for i in range(Z_CORE)]
 
     def exchange(rows, axis, groups):
         rows = rows[:, None, :]

time: 72.5 us -> 70.9 us (0.978)
  blocking collectives: 26.9 us -> 22.4 us
  starting transfers between devices: 25.9 us -> 28.4 us
    all_to_all x1, blocking collectives: 12.4 us -> 7.89 us  [exchange(): lax.all_to_all(rows, axis, 0, 0, axis_index_groups=groups, tiled=True)]
    all_to_all x1, starting transfers between devices: 11 us -> 13.5 us  [exchange(): lax.all_to_all(rows, axis, 0, 0, axis_index_groups=groups, tiled=True)]
where the time goes in v6:
time: 70.9 us; the launch traced here: 69.7 us
  starting transfers between devices  28.4 us (40%)
  blocking collectives  22.4 us (32%)
  Pallas kernels  13.9 us (20%)
  waiting for transfers between devices  2.72 us (4%)
  between operations  1.41 us (2%)
  local copies, waits for them, and re-layouts  0.76 us (1%)
    all_gather x1, blocking collectives, move(): lax.all_gather(first[:, :2 * KV_COLS], 'ctx', axis_index_groups=slots, ti...  14.5 us
    all_to_all x1, starting transfers between devices, exchange(): lax.all_to_all(rows, axis, 0, 0, axis_index_groups=groups, tiled=True)  13.5 us
    ppermute x1, starting transfers between devices, move(): first = lax.ppermute(first, 'dp', pairs)  8.06 us
    all_to_all x1, blocking collectives, exchange(): lax.all_to_all(rows, axis, 0, 0, axis_index_groups=groups, tiled=True)  7.89 us
    pallas_call x1, Pallas kernels, backward(): pl.pallas_call(backward_kernel, out_shape=(struct((rows, width), BF16), s...  6.37 us
    ppermute x3, starting transfers between devices, per_device(): received.append(lax.ppermute(send[turn], 'ctx', pairs))  4.9 us
    pallas_call x1, Pallas kernels, forward(): pl.pallas_call(forward_kernel, out_shape=(struct((rows, width), BF16), st...  4.53 us
    ppermute x1, waiting for transfers between devices, move(): first = lax.ppermute(first, 'dp', pairs)  2.32 us
  transfers between devices with their start and end apart: 6, of which 2 were waited for; matrix products, arithmetic and copies ran while one was open for 0% of the time, Pallas kernels for 10%

profile of v6, /device:TPU:1, one launch (start us, length us, event | category | flops | bytes accessed | tf_op | source)
XLA Modules:
  0.0 69.7 jit_solution(2742320621384596963)
XLA Ops:
  0.6 0.0 copy-start.1
  0.6 0.6 copy-done.1
  1.3 1.7 %head.1 = (s32[1]{0:T(128)}, bf16[128,896]{1,0:T(8,128)(2,1)S(1)}, bf16[128,1664]{1,0:T(8,128)(2,1)S(1)}) custom-call(s32[16]{0:T(128)S(1)} %copy-done.1, bf16[128,256]{1,0:T(8,128)(2,1)} %bitcast.29, bf16[128,256]{1,0:T(8,128)(2,1)} %bitcast.30, bf16[128,2048]{1,0:T(8,128)(2,1)} %bitcast.28), custom_call_target="tpu_custom_call" | custom-call | tf_op jit(solution)/shard_map/head/pallas_call | solution.py:71
  3.0 0.0 copy-start.2
  3.0 0.0 copy-start.3
  3.7 0.0 copy-done.2
  3.7 0.0 copy-done.3
  3.7 0.0 copy-start
  3.7 27.6 %conditional.1 = (bf16[128,896]{1,0:T(8,128)(2,1)S(1)}, bf16[128,1664]{1,0:T(8,128)(2,1)S(1)}, bf16[512,512]{1,0:T(8,128)(2,1)S(1)}, f32[128,128]{1,0:T(8,128)S(1)}, f32[32,128]{1,0:T(8,128)S(1)}) conditional(s32[]{:T(128)} %bitcast.3, (bf16[128,896]{1,0:T(8,128)(2,1)S(1)}, s32[8,16]{1,0:T(8,128)S(1)}, ...), branch_computations={%region_0.0_spmd, %region_1.0_spmd, %region_2.0_spmd, %region_3.0_... | conditional | flops 10000000000 | bytes 4849784 | solution.py:369
  3.8 8.1 %collective-permute-start.12 = (bf16[128,896]{1,0:T(8,128)(2,1)S(1)}, bf16[128,896]{1,0:T(8,128)(2,1)S(1)}, u32[]{:S(2)}, u32[]{:S(2)}) collective-permute-start(bf16[128,896]{1,0:T(8,128)(2,1)S(1)} %get-tuple-element.136), channel_id=1, source_target_pairs={{0,448},{64,384},{128,320},{192,256},{256,192},{320,128},{384,64},... | collective-permute-start | bytes 688136 | tf_op jit(solution)/shard_map/cond/branch_7_fun/ppermute | solution.py:363
  11.8 1.9 %collective-permute-start.13 = (bf16[128,1664]{1,0:T(8,128)(2,1)S(1)}, bf16[128,1664]{1,0:T(8,128)(2,1)S(1)}, u32[]{:S(2)}, u32[]{:S(2)}) collective-permute-start(bf16[128,1664]{1,0:T(8,128)(2,1)S(1)} %get-tuple-element.137), channel_id=1, source_target_pairs={{0,448},{64,384},{128,320},{192,256},{256,192},{320,128},{384,64},... | collective-permute-start | bytes 1277960 | tf_op jit(solution)/shard_map/cond/branch_7_fun/ppermute | solution.py:362
  13.8 2.3 %collective-permute-done.12 = bf16[128,896]{1,0:T(8,128)(2,1)S(1)} collective-permute-done((bf16[128,896]{1,0:T(8,128)(2,1)S(1)}, bf16[128,896]{1,0:T(8,128)(2,1)S(1)}, u32[]{:S(2)}, u32[]{:S(2)}) %collective-permute-start.12) | collective-permute-done | bytes 229408 | tf_op jit(solution)/shard_map/cond/branch_7_fun/ppermute | solution.py:363
  16.1 14.5 %all_gather.23.kv_ref = bf16[512,512]{1,0:T(8,128)(2,1)S(1)} all-gather(bf16[128,512]{1,0:T(8,128)(2,1)S(1)} %slice.42), channel_id=1, replica_groups={{0,1,2,3},{4,5,6,7},{8,9,10,11},{12,13,14,15},{16,17,18,19},{20,21,22,2..., dimensions={0}, use_global_device_ids=true | all-gather | bytes 655360 | tf_op jit(solution)/shard_map/cond/branch_7_fun/all_gather | solution.py:364
  30.6 0.7 prepare.15
  31.3 0.0 collective-permute-done.13
  31.3 0.0 copy-done
  31.3 4.5 %forward.1 = (bf16[128,2048]{1,0:T(8,128)(2,1)S(1)}, f32[128,128]{1,0:T(8,128)S(1)}, f32[32,128]{1,0:T(8,128)}) custom-call(bf16[128,896]{1,0:T(8,128)(2,1)S(1)} %get-tuple-element.170.first_ref, bf16[128,1664]{1,0:T(8,128)(2,1)S(1)} %get-tuple-element.171.second_ref, bf16[128,2048]{1,0:T(8,128)(2,1)S(1)} %bitcast.26, ...), custom_call_target="tpu_custom_call" | custom-call | flops 3221225472 | bytes 4194304 | tf_op jit(solution)/shard_map/forward/pallas_call | solution.py:266
  35.9 13.5 %all-to-all-start = ((f32[32,1,128]{2,1,0:T(1,128)}), f32[32,1,128]{2,1,0:T(1,128)S(1)}, u32[]{:S(2)}, u32[]{:S(2)}) async-start(f32[32,1,128]{2,1,0:T(1,128)} %bitcast.8), calls=%async_computation | async-start | bytes 32768 | tf_op jit(solution)/shard_map/all_to_all | solution.py:325
  49.4 6.4 %backward.1 = (bf16[128,2048]{1,0:T(8,128)(2,1)}, bf16[128,2048]{1,0:T(8,128)(2,1)}, f32[128,512]{1,0:T(8,128)S(1)}, bf16[3,128,512]{2,1,0:T(8,128)(2,1)S(1)}) custom-call(bf16[128,896]{1,0:T(8,128)(2,1)S(1)} %get-tuple-element.170.first_ref, bf16[128,1664]{1,0:T(8,128)(2,1)S(1)} %get-tuple-element.171.second_ref, bf16[128,2048]{1,0:T(8,128)(2,1)S(1)} %bitcast.27, ...), custom_call_target="tpu_custom_call" | custom-call | flops 6442450944 | bytes 4194304 | tf_op jit(solution)/shard_map/backward/pallas_call | solution.py:285
  55.8 2.3 %collective-permute-start.16 = (bf16[128,512]{1,0:T(8,128)(2,1)S(1)}, bf16[128,512]{1,0:T(8,128)(2,1)S(1)}, u32[]{:S(2)}, u32[]{:S(2)}) collective-permute-start(bf16[128,512]{1,0:T(8,128)(2,1)S(1)} %get-tuple-element.185), channel_id=1, source_target_pairs={{1,0},{3,2},{5,4},{7,6},{9,8},{11,10},{13,12},{15,14},{17,16},{19,... | collective-permute-start | bytes 393224 | tf_op jit(solution)/shard_map/ppermute | solution.py:377
  58.1 1.3 %collective-permute-start.15 = (bf16[128,512]{1,0:T(8,128)(2,1)S(1)}, bf16[128,512]{1,0:T(8,128)(2,1)S(1)}, u32[]{:S(2)}, u32[]{:S(2)}) collective-permute-start(bf16[128,512]{1,0:T(8,128)(2,1)S(1)} %get-tuple-element.186), channel_id=1, source_target_pairs={{2,0},{3,1},{6,4},{7,5},{10,8},{11,9},{14,12},{15,13},{18,16},{19,... | collective-permute-start | bytes 393224 | tf_op jit(solution)/shard_map/ppermute | solution.py:377
  59.4 1.3 %collective-permute-start.14 = (bf16[128,512]{1,0:T(8,128)(2,1)S(1)}, bf16[128,512]{1,0:T(8,128)(2,1)S(1)}, u32[]{:S(2)}, u32[]{:S(2)}) collective-permute-start(bf16[128,512]{1,0:T(8,128)(2,1)S(1)} %get-tuple-element.187), channel_id=1, source_target_pairs={{3,0},{2,1},{7,4},{6,5},{11,8},{10,9},{15,12},{14,13},{19,16},{18,... | collective-permute-start | bytes 393224 | tf_op jit(solution)/shard_map/ppermute | solution.py:377
  60.7 0.4 all-to-all-done
  61.1 7.9 %all_to_all.10 = f32[16,1,128]{2,1,0:T(1,128)S(1)} all-to-all(f32[16,1,128]{2,1,0:T(1,128)S(1)} %bitcast.25), channel_id=1, replica_groups={{384,416,448,480,128,160,192,224,320,352,256,288,64,96,0,32},{385,417,4..., dimensions={0} | all-to-all | bytes 16384 | tf_op jit(solution)/shard_map/all_to_all | solution.py:325
  69.0 0.0 collective-permute-done.16.third_ref
  69.0 0.0 collective-permute-done.15.second_ref
  69.0 0.0 collective-permute-done.14.first_ref
  69.0 0.7 finish.1
  (5 shorter events, 0.1 us)
Async XLA Ops:
  0.6 0.7 copy-start.1
  3.0 0.7 copy-start.2
  3.0 0.7 copy-start.3
  3.7 27.6 %copy-start = (bf16[1,128,2048]{2,1,0:T(8,128)(2,1)S(1)}, bf16[1,128,2048]{2,1,0:T(8,128)(2,1)}, u32[]{:S(2)}) copy-start(bf16[1,128,2048]{2,1,0:T(8,128)(2,1)} %param.18) | copy-start | bytes 1572868
  3.8 12.3 %collective-permute-start.12 = (bf16[128,896]{1,0:T(8,128)(2,1)S(1)}, bf16[128,896]{1,0:T(8,128)(2,1)S(1)}, u32[]{:S(2)}, u32[]{:S(2)}) collective-permute-start(bf16[128,896]{1,0:T(8,128)(2,1)S(1)} %get-tuple-element.136), channel_id=1, source_target_pairs={{0,448},{64,384},{128,320},{192,256},{256,192},{320,128},{384,64},... | collective-permute-start | bytes 688136 | tf_op jit(solution)/shard_map/cond/branch_7_fun/ppermute | solution.py:363
  11.8 19.4 %collective-permute-start.13 = (bf16[128,1664]{1,0:T(8,128)(2,1)S(1)}, bf16[128,1664]{1,0:T(8,128)(2,1)S(1)}, u32[]{:S(2)}, u32[]{:S(2)}) collective-permute-start(bf16[128,1664]{1,0:T(8,128)(2,1)S(1)} %get-tuple-element.137), channel_id=1, source_target_pairs={{0,448},{64,384},{128,320},{192,256},{256,192},{320,128},{384,64},... | collective-permute-start | bytes 1277960 | tf_op jit(solution)/shard_map/cond/branch_7_fun/ppermute | solution.py:362
  35.9 25.3 %all-to-all-start = ((f32[32,1,128]{2,1,0:T(1,128)}), f32[32,1,128]{2,1,0:T(1,128)S(1)}, u32[]{:S(2)}, u32[]{:S(2)}) async-start(f32[32,1,128]{2,1,0:T(1,128)} %bitcast.8), calls=%async_computation | async-start | bytes 32768 | tf_op jit(solution)/shard_map/all_to_all | solution.py:325
  55.8 13.2 %collective-permute-start.16 = (bf16[128,512]{1,0:T(8,128)(2,1)S(1)}, bf16[128,512]{1,0:T(8,128)(2,1)S(1)}, u32[]{:S(2)}, u32[]{:S(2)}) collective-permute-start(bf16[128,512]{1,0:T(8,128)(2,1)S(1)} %get-tuple-element.185), channel_id=1, source_target_pairs={{1,0},{3,2},{5,4},{7,6},{9,8},{11,10},{13,12},{15,14},{17,16},{19,... | collective-permute-start | bytes 393224 | tf_op jit(solution)/shard_map/ppermute | solution.py:377
  58.1 10.9 %collective-permute-start.15 = (bf16[128,512]{1,0:T(8,128)(2,1)S(1)}, bf16[128,512]{1,0:T(8,128)(2,1)S(1)}, u32[]{:S(2)}, u32[]{:S(2)}) collective-permute-start(bf16[128,512]{1,0:T(8,128)(2,1)S(1)} %get-tuple-element.186), channel_id=1, source_target_pairs={{2,0},{3,1},{6,4},{7,5},{10,8},{11,9},{14,12},{15,13},{18,16},{19,... | collective-permute-start | bytes 393224 | tf_op jit(solution)/shard_map/ppermute | solution.py:377
  59.4 9.6 %collective-permute-start.14 = (bf16[128,512]{1,0:T(8,128)(2,1)S(1)}, bf16[128,512]{1,0:T(8,128)(2,1)S(1)}, u32[]{:S(2)}, u32[]{:S(2)}) collective-permute-start(bf16[128,512]{1,0:T(8,128)(2,1)S(1)} %get-tuple-element.187), channel_id=1, source_target_pairs={{3,0},{2,1},{7,4},{6,5},{11,8},{10,9},{15,12},{14,13},{19,16},{18,... | collective-permute-start | bytes 393224 | tf_op jit(solution)/shard_map/ppermute | solution.py:377

commit v7 on v6

--- a/solution.py
+++ b/solution.py
@@ -49,23 +49,38 @@
     return lax.axis_index("ctx") % SPAN
 
 
-def head_kernel(plan_ref, k_ref, v_ref, q_ref, key_ref, first_ref, second_ref, plan, sems):
-    copies = [
-        pltpu.make_async_copy(plan_ref, plan, sems.at[0]),
-        pltpu.make_async_copy(k_ref, first_ref.at[:, :KV_COLS], sems.at[1]),
-        pltpu.make_async_copy(v_ref, first_ref.at[:, KV_COLS : 2 * KV_COLS], sems.at[2]),
-        pltpu.make_async_copy(q_ref.at[:, :FIRST_COLS], first_ref.at[:, 2 * KV_COLS :], sems.at[3]),
-        pltpu.make_async_copy(q_ref.at[:, FIRST_COLS:], second_ref, sems.at[4]),
+def head_kernel(
+    lengths_ref, plan_ref, sink_ref, k_ref, v_ref, q_ref,
+    key_ref, first_ref, second_ref, live_ref, sink8_ref,
+    lengths, plan, sinks, sems,
+):
+    pieces = [
+        (plan_ref, plan),
+        (lengths_ref, lengths),
+        (sink_ref, sinks),
+        (k_ref, first_ref.at[:, :KV_COLS]),
+        (v_ref, first_ref.at[:, KV_COLS : 2 * KV_COLS]),
+        (q_ref.at[:, :FIRST_COLS], first_ref.at[:, 2 * KV_COLS :]),
+        (q_ref.at[:, FIRST_COLS:], second_ref),
     ]
+    copies = [pltpu.make_async_copy(*piece, sems.at[at]) for at, piece in enumerate(pieces)]
     for copy in copies:
         copy.start()
-    copies[0].wait()
-    key_ref[0] = plan[lax.axis_index("ctx") // SPAN]
-    for copy in copies[1:]:
+    for copy in copies[:3]:
         copy.wait()
-
-
-def head(route_plan, keys, values, queries):
+    slot = lax.axis_index("ctx") // SPAN
+    key = plan[slot]
+    key_ref[0] = key
+    length = lengths[jnp.bitwise_xor(lax.axis_index("dp"), key), slot]
+    row_pos = lax.broadcasted_iota(jnp.int32, live_ref.shape, 0) + within_slot() * live_ref.shape[0]
+    live_ref[...] = jnp.where(row_pos < length, 1.0, 0.0).astype(F32)
+    for head_at in range(Q_HEADS):
+        sink8_ref[head_at : head_at + 1, :] = jnp.full((1, LANES), sinks[head_at] / SCALE, F32)
+    for copy in copies[3:]:
+        copy.wait()
+
+
+def head(lengths, route_plan, sink_logits, keys, values, queries):
     rows, width = queries.shape
     hbm = pl.BlockSpec(memory_space=pltpu.HBM)
     return pl.pallas_call(
@@ -74,13 +89,20 @@
             struct((1,), jnp.int32),
             struct((rows, 2 * KV_COLS + FIRST_COLS), BF16),
             struct((rows, width - FIRST_COLS), BF16),
+            struct((rows, LANES), F32),
+            struct((Q_HEADS, LANES), F32),
         ),
-        in_specs=[hbm] * 4,
-        out_specs=(SMEM, VMEM, VMEM),
-        scratch_shapes=[pltpu.SMEM(route_plan.shape, jnp.int32), pltpu.SemaphoreType.DMA((5,))],
+        in_specs=[hbm] * 6,
+        out_specs=(SMEM, VMEM, VMEM, VMEM, VMEM),
+        scratch_shapes=[
+            pltpu.SMEM(lengths.shape, jnp.int32),
+            pltpu.SMEM(route_plan.shape, jnp.int32),
+            pltpu.SMEM(sink_logits.shape, F32),
+            pltpu.SemaphoreType.DMA((7,)),
+        ],
         compiler_params=params(60),
         name="head",
-    )(route_plan, keys, values, queries)
+    )(lengths, route_plan, sink_logits, keys, values, queries)
 
 
 def pair_queries(first_ref, second_ref, pair):
@@ -89,29 +111,20 @@
     return second_ref[:, (pair - FIRST_PAIRS) * LANES : (pair - FIRST_PAIRS + 1) * LANES]
 
 
-def prepare_kernel(lengths_ref, plan_ref, sink_ref, kv_ref, copy_ref, live_ref, sink8_ref):
-    rows = live_ref.shape[0]
-    slot = lax.axis_index("ctx") // SPAN
-    source = jnp.bitwise_xor(lax.axis_index("dp"), plan_ref[slot])
-    length = lengths_ref[source, slot]
-    row_pos = lax.broadcasted_iota(jnp.int32, (rows, LANES), 0) + within_slot() * rows
-    live_ref[...] = jnp.where(row_pos < length, 1.0, 0.0).astype(F32)
-    for head_at in range(Q_HEADS):
-        sink8_ref[head_at : head_at + 1, :] = jnp.full((1, LANES), sink_ref[head_at] / SCALE, F32)
+def prepare_kernel(kv_ref, copy_ref):
     copy_ref[...] = kv_ref[...]
 
 
-def prepare(lengths, route_plan, sink_logits, kv):
-    rows = kv.shape[0] // SPAN
+def prepare(kv):
     return pl.pallas_call(
         prepare_kernel,
-        out_shape=(struct(kv.shape, BF16), struct((rows, LANES), F32), struct((Q_HEADS, LANES), F32)),
-        in_specs=[SMEM] * 3 + [VMEM],
-        out_specs=(VMEM,) * 3,
+        out_shape=struct(kv.shape, BF16),
+        in_specs=[VMEM],
+        out_specs=VMEM,
         compiler_params=params(4),
         cost_estimate=pl.CostEstimate(flops=W_PREPARE, bytes_accessed=0, transcendentals=0),
         name="prepare",
-    )(lengths, route_plan, sink_logits, kv)
+    )(kv)
 
 
 def lane_halves(two, half):
@@ -351,7 +364,9 @@
 
 
 def per_device(queries, key_vectors, value_vectors, out_grad, sink_logits, lengths, route_plan):
-    key, first, second = head(route_plan, key_vectors[0], value_vectors[0], queries[0])
+    key, first, second, live, sink8 = head(
+        lengths, route_plan, sink_logits, key_vectors[0], value_vectors[0], queries[0]
+    )
     slots = [[SPAN * s + i for i in range(SPAN)] for s in range(16)]
 
     def branch(bits):
@@ -362,11 +377,11 @@
                 second = lax.ppermute(second, "dp", pairs)
                 first = lax.ppermute(first, "dp", pairs)
             window = lax.all_gather(first[:, : 2 * KV_COLS], "ctx", axis_index_groups=slots, tiled=True)
-            return first, second, *prepare(lengths, route_plan, sink_logits, window)
+            return first, second, prepare(window)
 
         return move
 
-    first, second, window, live, sink8 = lax.switch(
+    first, second, window = lax.switch(
         key[0], [branch(bits) for bits in range(8)], first, second
     )
     kept, stat, part = forward(first, second, out_grad[0], window, live, sink8)

time: 70.9 us -> 66.5 us (0.938)
  starting transfers between devices: 28.4 us -> 22.9 us
  blocking collectives: 22.4 us -> 25.5 us
  waiting for transfers between devices: 2.72 us -> 1.86 us
    all_to_all x1, starting transfers between devices: 13.5 us -> 10.5 us  [exchange(): lax.all_to_all(rows, axis, 0, 0, axis_index_groups=groups, tiled=True)]
    ppermute x1, starting transfers between devices: 8.06 us -> 5.61 us  [move(): first = lax.ppermute(first, 'dp', pairs)]
    all_gather x1, blocking collectives: 14.5 us -> 16.3 us  [move(): lax.all_gather(first[:, :2 * KV_COLS], 'ctx', axis_index_groups=slots, ti...]
    all_to_all x1, blocking collectives: 7.89 us -> 9.24 us  [exchange(): lax.all_to_all(rows, axis, 0, 0, axis_index_groups=groups, tiled=True)]
    ppermute x1, waiting for transfers between devices: 2.32 us -> 1.47 us  [move(): first = lax.ppermute(first, 'dp', pairs)]
where the time goes in v7:
time: 66.5 us; the launch traced here: 65.3 us
  blocking collectives  25.5 us (38%)
  starting transfers between devices  22.9 us (34%)
  Pallas kernels  13.5 us (20%)
  waiting for transfers between devices  1.86 us (3%)
  between operations  1.39 us (2%)
    all_gather x1, blocking collectives, move(): lax.all_gather(first[:, :2 * KV_COLS], 'ctx', axis_index_groups=slots, ti...  16.3 us
    all_to_all x1, starting transfers between devices, exchange(): lax.all_to_all(rows, axis, 0, 0, axis_index_groups=groups, tiled=True)  10.5 us
    all_to_all x1, blocking collectives, exchange(): lax.all_to_all(rows, axis, 0, 0, axis_index_groups=groups, tiled=True)  9.24 us
    pallas_call x1, Pallas kernels, backward(): pl.pallas_call(backward_kernel, out_shape=(struct((rows, width), BF16), s...  6.37 us
    ppermute x1, starting transfers between devices, move(): first = lax.ppermute(first, 'dp', pairs)  5.61 us
    ppermute x3, starting transfers between devices, per_device(): received.append(lax.ppermute(send[turn], 'ctx', pairs))  4.9 us
    pallas_call x1, Pallas kernels, forward(): pl.pallas_call(forward_kernel, out_shape=(struct((rows, width), BF16), st...  4.52 us
    ppermute x1, starting transfers between devices, move(): second = lax.ppermute(second, 'dp', pairs)  1.92 us
  transfers between devices with their start and end apart: 6, of which 2 were waited for; matrix products, arithmetic and copies ran while one was open for 0% of the time, Pallas kernels for 10%

profile of v7, /device:TPU:1, one launch (start us, length us, event | category | flops | bytes accessed | tf_op | source)
XLA Modules:
  0.0 65.3 jit_solution(5456440350150365730)
XLA Ops:
  0.6 1.8 %head.1 = (s32[1]{0:T(128)}, bf16[128,896]{1,0:T(8,128)(2,1)S(1)}, bf16[128,1664]{1,0:T(8,128)(2,1)S(1)}, f32[128,128]{1,0:T(8,128)}, f32[32,128]{1,0:T(8,128)}) custom-call(s32[8,16]{1,0:T(8,128)} %lengths_ref.1, s32[16]{0:T(128)} %plan_ref.1, f32[32]{0:T(128)} %sink_ref.1, bf16[128,256]{1,0:T(8,128)(2,1)} %bitcast.29, bf16[128,256]{1,0:T(8,128)(2,1)} %bitcast.30, ...), custom_call_target="tpu_custom_call" | custom-call | tf_op jit(solution)/shard_map/head/pallas_call | solution.py:86
  3.1 0.0 copy-start
  3.1 0.0 copy-start.1
  3.2 0.0 copy-start.2
  3.2 25.5 %conditional.1 = (bf16[128,896]{1,0:T(8,128)(2,1)S(1)}, bf16[128,1664]{1,0:T(8,128)(2,1)S(1)}, bf16[512,512]{1,0:T(8,128)(2,1)S(1)}) conditional(s32[]{:T(128)} %bitcast.3, (bf16[128,896]{1,0:T(8,128)(2,1)S(1)}, bf16[128,1664]{1,0:T(8,128)(2,1)S(1)}) %tuple.40, (bf16[128,896]{1,0:T(8,128)(2,1)S(1)}, ...), branch_computations={%region_0.0_spmd, %region_1.0_spmd, %region_2.0_spmd, %region_3.0_... | conditional | flops 10000000000 | bytes 4849768 | solution.py:384
  3.2 5.6 %collective-permute-start.6 = (bf16[128,896]{1,0:T(8,128)(2,1)S(1)}, bf16[128,896]{1,0:T(8,128)(2,1)S(1)}, u32[]{:S(2)}, u32[]{:S(2)}) collective-permute-start(bf16[128,896]{1,0:T(8,128)(2,1)S(1)} %get-tuple-element.40), channel_id=1, source_target_pairs={{0,256},{64,320},{128,384},{192,448},{256,0},{320,64},{384,128},{4... | collective-permute-start | bytes 688136 | tf_op jit(solution)/shard_map/cond/branch_4_fun/ppermute | solution.py:378
  8.8 1.9 %collective-permute-start.7 = (bf16[128,1664]{1,0:T(8,128)(2,1)S(1)}, bf16[128,1664]{1,0:T(8,128)(2,1)S(1)}, u32[]{:S(2)}, u32[]{:S(2)}) collective-permute-start(bf16[128,1664]{1,0:T(8,128)(2,1)S(1)} %get-tuple-element.41), channel_id=1, source_target_pairs={{0,256},{64,320},{128,384},{192,448},{256,0},{320,64},{384,128},{4... | collective-permute-start | bytes 1277960 | tf_op jit(solution)/shard_map/cond/branch_4_fun/ppermute | solution.py:377
  10.7 1.5 %collective-permute-done.6 = bf16[128,896]{1,0:T(8,128)(2,1)S(1)} collective-permute-done((bf16[128,896]{1,0:T(8,128)(2,1)S(1)}, bf16[128,896]{1,0:T(8,128)(2,1)S(1)}, u32[]{:S(2)}, u32[]{:S(2)}) %collective-permute-start.6) | collective-permute-done | bytes 229408 | tf_op jit(solution)/shard_map/cond/branch_4_fun/ppermute | solution.py:378
  12.2 16.3 %all_gather.20.kv_ref = bf16[512,512]{1,0:T(8,128)(2,1)S(1)} all-gather(bf16[128,512]{1,0:T(8,128)(2,1)S(1)} %slice.39), channel_id=1, replica_groups={{0,1,2,3},{4,5,6,7},{8,9,10,11},{12,13,14,15},{16,17,18,19},{20,21,22,2..., dimensions={0}, use_global_device_ids=true | all-gather | bytes 655360 | tf_op jit(solution)/shard_map/cond/branch_4_fun/all_gather | solution.py:379
  28.6 0.0 collective-permute-done.7
  28.6 0.0 copy-done
  28.7 0.0 copy-done.1
  28.7 0.0 copy-done.2
  28.7 4.5 %forward.1 = (bf16[128,2048]{1,0:T(8,128)(2,1)S(1)}, f32[128,128]{1,0:T(8,128)S(1)}, f32[32,128]{1,0:T(8,128)}) custom-call(bf16[128,896]{1,0:T(8,128)(2,1)S(1)} %get-tuple-element.74.first_ref, bf16[128,1664]{1,0:T(8,128)(2,1)S(1)} %get-tuple-element.75.second_ref, bf16[128,2048]{1,0:T(8,128)(2,1)S(1)} %bitcast.26, ...), custom_call_target="tpu_custom_call" | custom-call | flops 3221225472 | bytes 4194304 | tf_op jit(solution)/shard_map/forward/pallas_call | solution.py:279
  33.2 10.5 %all-to-all-start = ((f32[32,1,128]{2,1,0:T(1,128)}), f32[32,1,128]{2,1,0:T(1,128)S(1)}, u32[]{:S(2)}, u32[]{:S(2)}) async-start(f32[32,1,128]{2,1,0:T(1,128)} %bitcast.8), calls=%async_computation | async-start | bytes 32768 | tf_op jit(solution)/shard_map/all_to_all | solution.py:338
  43.7 6.4 %backward.1 = (bf16[128,2048]{1,0:T(8,128)(2,1)}, bf16[128,2048]{1,0:T(8,128)(2,1)}, f32[128,512]{1,0:T(8,128)S(1)}, bf16[3,128,512]{2,1,0:T(8,128)(2,1)S(1)}) custom-call(bf16[128,896]{1,0:T(8,128)(2,1)S(1)} %get-tuple-element.74.first_ref, bf16[128,1664]{1,0:T(8,128)(2,1)S(1)} %get-tuple-element.75.second_ref, bf16[128,2048]{1,0:T(8,128)(2,1)S(1)} %bitcast.27, ...), custom_call_target="tpu_custom_call" | custom-call | flops 6442450944 | bytes 4194304 | tf_op jit(solution)/shard_map/backward/pallas_call | solution.py:298
  50.1 2.3 %collective-permute-start.16 = (bf16[128,512]{1,0:T(8,128)(2,1)S(1)}, bf16[128,512]{1,0:T(8,128)(2,1)S(1)}, u32[]{:S(2)}, u32[]{:S(2)}) collective-permute-start(bf16[128,512]{1,0:T(8,128)(2,1)S(1)} %get-tuple-element.89), channel_id=1, source_target_pairs={{1,0},{3,2},{5,4},{7,6},{9,8},{11,10},{13,12},{15,14},{17,16},{19,... | collective-permute-start | bytes 393224 | tf_op jit(solution)/shard_map/ppermute | solution.py:392
  52.4 1.3 %collective-permute-start.15 = (bf16[128,512]{1,0:T(8,128)(2,1)S(1)}, bf16[128,512]{1,0:T(8,128)(2,1)S(1)}, u32[]{:S(2)}, u32[]{:S(2)}) collective-permute-start(bf16[128,512]{1,0:T(8,128)(2,1)S(1)} %get-tuple-element.90), channel_id=1, source_target_pairs={{2,0},{3,1},{6,4},{7,5},{10,8},{11,9},{14,12},{15,13},{18,16},{19,... | collective-permute-start | bytes 393224 | tf_op jit(solution)/shard_map/ppermute | solution.py:392
  53.7 1.3 %collective-permute-start.14 = (bf16[128,512]{1,0:T(8,128)(2,1)S(1)}, bf16[128,512]{1,0:T(8,128)(2,1)S(1)}, u32[]{:S(2)}, u32[]{:S(2)}) collective-permute-start(bf16[128,512]{1,0:T(8,128)(2,1)S(1)} %get-tuple-element.91), channel_id=1, source_target_pairs={{3,0},{2,1},{7,4},{6,5},{11,8},{10,9},{15,12},{14,13},{19,16},{18,... | collective-permute-start | bytes 393224 | tf_op jit(solution)/shard_map/ppermute | solution.py:392
  55.0 0.4 all-to-all-done
  55.4 9.2 %all_to_all.10 = f32[16,1,128]{2,1,0:T(1,128)S(1)} all-to-all(f32[16,1,128]{2,1,0:T(1,128)S(1)} %bitcast.25), channel_id=1, replica_groups={{384,416,448,480,128,160,192,224,320,352,256,288,64,96,0,32},{385,417,4..., dimensions={0} | all-to-all | bytes 16384 | tf_op jit(solution)/shard_map/all_to_all | solution.py:338
  64.6 0.0 collective-permute-done.16.third_ref
  64.6 0.0 collective-permute-done.15.second_ref
  64.6 0.0 collective-permute-done.14.first_ref
  64.6 0.7 %finish.1 = (f32[32]{0:T(128)}, bf16[128,256]{1,0:T(8,128)(2,1)}, bf16[128,256]{1,0:T(8,128)(2,1)}) custom-call(f32[16,128]{1,0:T(8,128)S(1)} %bitcast.23, f32[128,512]{1,0:T(8,128)S(1)} %get-tuple-element.84.own_ref, bf16[128,512]{1,0:T(8,128)(2,1)S(1)} %collective-permute-done.14.first_ref, bf16[128,512]{1,0:T(8,128)(2,1)S(1)} %collective-permute-done.15.second_ref, ...), custom_call_target="tpu_custom_call" | custom-call | tf_op jit(solution)/shard_map/finish/pallas_call | solution.py:356
  (6 shorter events, 0.1 us)
Async XLA Ops:
  3.1 25.5 %copy-start = (bf16[1,128,2048]{2,1,0:T(8,128)(2,1)S(1)}, bf16[1,128,2048]{2,1,0:T(8,128)(2,1)}, u32[]{:S(2)}) copy-start(bf16[1,128,2048]{2,1,0:T(8,128)(2,1)} %param.18) | copy-start | bytes 1572868
  3.1 25.5 %copy-start.1 = (f32[128,128]{1,0:T(8,128)S(1)}, f32[128,128]{1,0:T(8,128)}, u32[]{:S(2)}) copy-start(f32[128,128]{1,0:T(8,128)} %get-tuple-element.77.live_ref) | copy-start | bytes 196612
  3.2 25.5 %copy-start.2 = (f32[32,128]{1,0:T(8,128)S(1)}, f32[32,128]{1,0:T(8,128)}, u32[]{:S(2)}) copy-start(f32[32,128]{1,0:T(8,128)} %get-tuple-element.78.sink8_ref) | copy-start | bytes 49156
  3.2 9.0 %collective-permute-start.6 = (bf16[128,896]{1,0:T(8,128)(2,1)S(1)}, bf16[128,896]{1,0:T(8,128)(2,1)S(1)}, u32[]{:S(2)}, u32[]{:S(2)}) collective-permute-start(bf16[128,896]{1,0:T(8,128)(2,1)S(1)} %get-tuple-element.40), channel_id=1, source_target_pairs={{0,256},{64,320},{128,384},{192,448},{256,0},{320,64},{384,128},{4... | collective-permute-start | bytes 688136 | tf_op jit(solution)/shard_map/cond/branch_4_fun/ppermute | solution.py:378
  8.8 19.8 %collective-permute-start.7 = (bf16[128,1664]{1,0:T(8,128)(2,1)S(1)}, bf16[128,1664]{1,0:T(8,128)(2,1)S(1)}, u32[]{:S(2)}, u32[]{:S(2)}) collective-permute-start(bf16[128,1664]{1,0:T(8,128)(2,1)S(1)} %get-tuple-element.41), channel_id=1, source_target_pairs={{0,256},{64,320},{128,384},{192,448},{256,0},{320,64},{384,128},{4... | collective-permute-start | bytes 1277960 | tf_op jit(solution)/shard_map/cond/branch_4_fun/ppermute | solution.py:377
  33.2 22.2 %all-to-all-start = ((f32[32,1,128]{2,1,0:T(1,128)}), f32[32,1,128]{2,1,0:T(1,128)S(1)}, u32[]{:S(2)}, u32[]{:S(2)}) async-start(f32[32,1,128]{2,1,0:T(1,128)} %bitcast.8), calls=%async_computation | async-start | bytes 32768 | tf_op jit(solution)/shard_map/all_to_all | solution.py:338
  50.1 14.6 %collective-permute-start.16 = (bf16[128,512]{1,0:T(8,128)(2,1)S(1)}, bf16[128,512]{1,0:T(8,128)(2,1)S(1)}, u32[]{:S(2)}, u32[]{:S(2)}) collective-permute-start(bf16[128,512]{1,0:T(8,128)(2,1)S(1)} %get-tuple-element.89), channel_id=1, source_target_pairs={{1,0},{3,2},{5,4},{7,6},{9,8},{11,10},{13,12},{15,14},{17,16},{19,... | collective-permute-start | bytes 393224 | tf_op jit(solution)/shard_map/ppermute | solution.py:392
  52.4 12.2 %collective-permute-start.15 = (bf16[128,512]{1,0:T(8,128)(2,1)S(1)}, bf16[128,512]{1,0:T(8,128)(2,1)S(1)}, u32[]{:S(2)}, u32[]{:S(2)}) collective-permute-start(bf16[128,512]{1,0:T(8,128)(2,1)S(1)} %get-tuple-element.90), channel_id=1, source_target_pairs={{2,0},{3,1},{6,4},{7,5},{10,8},{11,9},{14,12},{15,13},{18,16},{19,... | collective-permute-start | bytes 393224 | tf_op jit(solution)/shard_map/ppermute | solution.py:392
  53.7 11.0 %collective-permute-start.14 = (bf16[128,512]{1,0:T(8,128)(2,1)S(1)}, bf16[128,512]{1,0:T(8,128)(2,1)S(1)}, u32[]{:S(2)}, u32[]{:S(2)}) collective-permute-start(bf16[128,512]{1,0:T(8,128)(2,1)S(1)} %get-tuple-element.91), channel_id=1, source_target_pairs={{3,0},{2,1},{7,4},{6,5},{11,8},{10,9},{15,12},{14,13},{19,16},{18,... | collective-permute-start | bytes 393224 | tf_op jit(solution)/shard_map/ppermute | solution.py:392
